TPU v7x, 128 devices: a whole 4x4x4 slice. The times are simulated.
128 devices in a mesh: src: 4 (over x_lo, core), slab: 32 (over x_hi, z, y).
Axes of the slice: x: 4 (x_hi: 2, x_lo: 2; x = x_hi * 2 + x_lo), y: 4, z: 4, core: 2. Of those that a mesh axis runs over, the one named last changes fastest.
Arguments:
- log_cond: float32 [256, 256, 256], P('slab'), may hold values from -1.5 to 1.5
- perturb: float32 [256, 256, 256], P('slab'), may hold values from -6 to 6
- potentials: float32 [4, 256, 256, 256], P('src', 'slab'), may hold values from -6 to 6
- rec_depth: int32 [2, 4096], replicated, may hold values from 0 to 255
- rec_plan: int32 [2, 4096], replicated, may hold values from 0 to 65535
Outputs:
- hess_vec: float32 [256, 256, 256], P('slab')
All inputs are finite; a program needn't handle non-finite values.
Results may differ from a plain program's by a relative error of at most 0.0003.
Values sent between devices are 32-bit elements; how exact they have to be, the bound alone decides.
A program may use at most 256 MiB of HBM per device.

v0:
```python
import jax
import jax.numpy as jnp
from jax import lax
from jax.sharding import PartitionSpec as P

ITERS = 4


def extended(block, sides, width):
    for axis, dim in sides:
        count = lax.axis_size(axis)
        forward = [(i, i + 1) for i in range(count - 1)]
        backward = [(target, source) for source, target in forward]
        low = lax.ppermute(
            lax.slice_in_dim(block, block.shape[dim] - width, None, axis=dim), axis, forward
        )
        high = lax.ppermute(lax.slice_in_dim(block, 0, width, axis=dim), axis, backward)
        block = jnp.concatenate([low, block, high], axis=dim)
    return block


def shifted(field, axis, step):
    size = field.shape[axis]
    zero = jnp.zeros_like(lax.slice_in_dim(field, 0, 1, axis=axis))
    if step > 0:
        return jnp.concatenate([lax.slice_in_dim(field, 1, size, axis=axis), zero], axis=axis)
    return jnp.concatenate([zero, lax.slice_in_dim(field, 0, size - 1, axis=axis)], axis=axis)


def coefficients(padded):
    core = padded[..., 1:-1, :, :]
    faces = 0.5 * (padded[..., 1:, :, :] + padded[..., :-1, :, :])
    return (
        faces[..., :-1, :, :],
        faces[..., 1:, :, :],
        0.5 * (core + shifted(core, -2, -1)),
        0.5 * (core + shifted(core, -2, 1)),
        0.5 * (core + shifted(core, -1, -1)),
        0.5 * (core + shifted(core, -1, 1)),
    )


def apply_faces(coef, padded):
    core = padded[..., 1:-1, :, :]
    total = coef[0] * (core - padded[..., :-2, :, :]) + coef[1] * (core - padded[..., 2:, :, :])
    total = (
        total + coef[2] * (core - shifted(core, -2, -1)) + coef[3] * (core - shifted(core, -2, 1))
    )
    total = (
        total + coef[4] * (core - shifted(core, -1, -1)) + coef[5] * (core - shifted(core, -1, 1))
    )
    return total


def pair_sum(upad, lpad):
    upot = upad[..., 1:-1, :, :]
    ladj = lpad[..., 1:-1, :, :]
    total = (upot - upad[..., :-2, :, :]) * (ladj - lpad[..., :-2, :, :])
    total = total + (upot - upad[..., 2:, :, :]) * (ladj - lpad[..., 2:, :, :])
    for axis in (-2, -1):
        for step in (-1, 1):
            total = total + (upot - shifted(upot, axis, step)) * (ladj - shifted(ladj, axis, step))
    return 0.5 * total


def expand(values):
    return values[:, None, None, None]


def solve(coef, rhs, inside):

    def inner(first, second):
        return jnp.sum(first * second, axis=(1, 2, 3))

    def squares(resid):
        return lax.psum(inner(resid, resid), "slab")

    solution = jnp.zeros_like(rhs)
    resid = rhs
    direction = rhs
    norm_now = squares(resid)
    for step in range(ITERS):
        padded = extended(direction, (("slab", 1),), 1)
        image = apply_faces(coef, padded) * inside
        alpha = norm_now / lax.psum(inner(direction, image), "slab")
        solution = solution + expand(alpha) * direction
        resid = resid - expand(alpha) * image
        norm_next = squares(resid)
        direction = resid + expand(norm_next / norm_now) * direction
        norm_now = norm_next
    return solution


def shards(log_cond, perturb, potentials, rec_depth, rec_plan):
    margin = 0
    depth = log_cond.shape[0]
    sigma = jnp.exp(log_cond)
    weighted = sigma * perturb
    rims = extended(jnp.stack([sigma, weighted]), (("slab", 1),), margin + 1)
    coef = coefficients(rims[0])
    wcoef = coefficients(rims[1])
    upad_wide = extended(potentials, (("slab", 1),), margin + 1)
    extent = depth + 2 * margin
    first_plane = lax.axis_index("slab") * depth - margin
    global_plane = first_plane + jnp.arange(extent, dtype=jnp.int32)
    inside = ((global_plane >= 0) & (global_plane < depth * lax.axis_size("slab"))).astype(
        jnp.float32
    )
    inside = inside[None, :, None, None]
    rhs = -apply_faces(wcoef, upad_wide) * inside
    tangent_wide = solve(coef, rhs, inside)
    sources, unused_depth, rows, cols = tangent_wide.shape
    plane = rows * cols
    local = rec_depth - lax.axis_index("slab") * depth
    owned = ((local >= 0) & (local < depth)).astype(jnp.float32)
    index = (jnp.clip(local, 0, depth - 1) * plane + rec_plan).reshape(-1)
    flat = tangent_wide.reshape(sources, -1)
    picked = flat[:, index].reshape(sources, 2, -1) * owned[None]
    values = lax.psum(picked, "slab")
    data = values[:, 0] - values[:, 1]
    wide_local = rec_depth - first_plane
    wide_owned = ((wide_local >= 0) & (wide_local < extent)).astype(jnp.float32)
    wide_index = (jnp.clip(wide_local, 0, extent - 1) * plane + rec_plan).reshape(-1)
    signed = jnp.stack([data, -data], axis=1) * wide_owned[None]
    back = (
        jnp.zeros((sources, extent * plane), jnp.float32)
        .at[:, wide_index]
        .add(signed.reshape(sources, -1))
    )
    back = back.reshape(sources, extent, rows, cols)
    adjoint = solve(coef, back, inside)
    lpad = extended(adjoint, (("slab", 1),), 1)
    partial_sum = -sigma * jnp.sum(pair_sum(upad_wide, lpad), axis=0)
    return lax.psum(partial_sum, "src")


def solution(mesh):
    in_specs = (
        P("slab", None, None),
        P("slab", None, None),
        P("src", "slab", None, None),
        P(),
        P(),
    )
    out_specs = P("slab", None, None)
    return jax.shard_map(shards, mesh=mesh, in_specs=in_specs, out_specs=out_specs, check_vma=False)
```

profile of v0, /device:TPU:1, one launch (start us, length us, event | category | flops | bytes accessed | tf_op | source)
XLA Modules:
  0.0 1996.0 jit_solution(2515929133254491221)
XLA Ops:
  6.5 4.1 fusion.142
  13.7 5.5 collective-permute-start.2
  34.0 4.9 fusion.140
  39.1 4.7 fusion.141
  52.2 6.5 fusion.103
  61.4 4.0 collective-permute-start.4
  69.8 5.8 collective-permute-done.5
  75.6 8.8 multiply_reduce_fusion.12
  84.4 79.6 %all-reduce.49 = (f32[1]{0:T(128)}, f32[1]{0:T(128)}) all-reduce(f32[1]{0:T(128)} %bitcast.7, f32[1]{0:T(128)} %bitcast.12), channel_id=1, replica_groups=mesh['src'=4,'slab'=32] {'slab'}, use_global_device_ids=true, to_apply=%region_1.0 | all-reduce | flops 2 | bytes 16 | tf_op jit(solution)/shard_map/psum | solution.py:76
  165.3 3.4 multiply_reduce_fusion.11
  168.8 76.0 %psum.128 = f32[1]{0:T(128)} all-reduce(f32[1]{0:T(128)} %bitcast.14), channel_id=1, replica_groups=mesh['src'=4,'slab'=32] {'slab'}, use_global_device_ids=true, to_apply=%region_5.0 | all-reduce | flops 1 | bytes 8 | tf_op jit(solution)/shard_map/psum | solution.py:76
  255.3 4.4 collective-permute-done.7
  259.7 4.8 multiply_reduce_fusion.10
  264.5 75.6 %psum.129 = f32[1]{0:T(128)} all-reduce(f32[1]{0:T(128)} %bitcast.16), channel_id=1, replica_groups=mesh['src'=4,'slab'=32] {'slab'}, use_global_device_ids=true, to_apply=%region_7.0 | all-reduce | flops 1 | bytes 8 | tf_op jit(solution)/shard_map/psum | solution.py:85
  341.4 5.4 multiply_reduce_fusion.9
  346.8 77.0 %psum.130 = f32[1]{0:T(128)} all-reduce(f32[1]{0:T(128)} %bitcast.18), channel_id=1, replica_groups=mesh['src'=4,'slab'=32] {'slab'}, use_global_device_ids=true, to_apply=%region_9.0 | all-reduce | flops 1 | bytes 8 | tf_op jit(solution)/shard_map/psum | solution.py:76
  433.3 4.4 collective-permute-done.9
  437.8 4.8 multiply_reduce_fusion.8
  442.5 77.1 %psum.131 = f32[1]{0:T(128)} all-reduce(f32[1]{0:T(128)} %bitcast.20), channel_id=1, replica_groups=mesh['src'=4,'slab'=32] {'slab'}, use_global_device_ids=true, to_apply=%region_11.0 | all-reduce | flops 1 | bytes 8 | tf_op jit(solution)/shard_map/psum | solution.py:85
  520.9 3.4 multiply_reduce_fusion.7
  524.4 75.9 %psum.132 = f32[1]{0:T(128)} all-reduce(f32[1]{0:T(128)} %bitcast.22), channel_id=1, replica_groups=mesh['src'=4,'slab'=32] {'slab'}, use_global_device_ids=true, to_apply=%region_13.0 | all-reduce | flops 1 | bytes 8 | tf_op jit(solution)/shard_map/psum | solution.py:76
  605.3 3.4 collective-permute-start.10
  612.0 7.7 collective-permute-done.11
  619.8 3.8 fusion.105
  623.6 82.7 %psum.133 = f32[1]{0:T(128)} all-reduce(f32[1]{0:T(128)} %bitcast.24), channel_id=1, replica_groups=mesh['src'=4,'slab'=32] {'slab'}, use_global_device_ids=true, to_apply=%region_15.0 | all-reduce | flops 1 | bytes 8 | tf_op jit(solution)/shard_map/psum | solution.py:85
  707.5 4.9 multiply_add_fusion.4
  713.5 45.5 %gather_fusion = f32[8192]{0:T(1024)S(1)} fusion(f32[524288]{0:T(1024)S(1)} %bitcast.209, s32[8192]{0:T(1024)S(1)} %broadcast_clamp_fusion), kind=kCustom, calls=%fused_computation | custom fusion | bytes 98304 | tf_op jit(solution)/shard_map/gather | solution.py:118
  759.1 149.4 %psum.134 = f32[1,2,4096]{2,1,0:T(2,128)S(1)} all-reduce(f32[1,2,4096]{2,1,0:T(2,128)S(1)} %select_bitcast_fusion), channel_id=1, replica_groups=mesh['src'=4,'slab'=32] {'slab'}, use_global_device_ids=true, to_apply=%region_16.17 | all-reduce | flops 8192 | bytes 65536 | tf_op jit(solution)/shard_map/psum | solution.py:119
  908.6 44.6 %scatter_custom_fusion = f32[524288]{0:T(1024)} fusion(s32[8192]{0:T(1024)S(1)} %bitcast.214, f32[8192]{0:T(1024)S(1)} %bitcast.217, f32[]{:T(128)} %constant.9.clone.1), kind=kCustom, calls=%fused_computation.207 | custom fusion | flops 8192 | bytes 2097156 | tf_op jit(solution)/shard_map/scatter-add | solution.py:128
  966.9 4.7 multiply_reduce_fusion.6
  971.6 86.7 %all-reduce.48 = (f32[1]{0:T(128)}, f32[1]{0:T(128)}) all-reduce(f32[1]{0:T(128)} %bitcast.29, f32[1]{0:T(128)} %bitcast.30), channel_id=1, replica_groups=mesh['src'=4,'slab'=32] {'slab'}, use_global_device_ids=true, to_apply=%region_19.20 | all-reduce | flops 2 | bytes 16 | tf_op jit(solution)/shard_map/psum | solution.py:76
  1063.2 77.6 %psum.137 = f32[1]{0:T(128)} all-reduce(f32[1]{0:T(128)} %bitcast.32), channel_id=1, replica_groups=mesh['src'=4,'slab'=32] {'slab'}, use_global_device_ids=true, to_apply=%region_23.24 | all-reduce | flops 1 | bytes 8 | tf_op jit(solution)/shard_map/psum | solution.py:76
  1151.0 7.8 collective-permute-done.15
  1158.9 4.8 multiply_reduce_fusion.4
  1163.7 83.3 %psum.138 = f32[1]{0:T(128)} all-reduce(f32[1]{0:T(128)} %bitcast.34), channel_id=1, replica_groups=mesh['src'=4,'slab'=32] {'slab'}, use_global_device_ids=true, to_apply=%region_25.26 | all-reduce | flops 1 | bytes 8 | tf_op jit(solution)/shard_map/psum | solution.py:85
  1248.5 5.3 multiply_reduce_fusion.3
  1253.8 76.4 %psum.139 = f32[1]{0:T(128)} all-reduce(f32[1]{0:T(128)} %bitcast.36), channel_id=1, replica_groups=mesh['src'=4,'slab'=32] {'slab'}, use_global_device_ids=true, to_apply=%region_27.28 | all-reduce | flops 1 | bytes 8 | tf_op jit(solution)/shard_map/psum | solution.py:76
  1341.1 8.6 collective-permute-done.17
  1349.7 4.8 multiply_reduce_fusion.2
  1354.5 82.1 %psum.140 = f32[1]{0:T(128)} all-reduce(f32[1]{0:T(128)} %bitcast.38), channel_id=1, replica_groups=mesh['src'=4,'slab'=32] {'slab'}, use_global_device_ids=true, to_apply=%region_29.30 | all-reduce | flops 1 | bytes 8 | tf_op jit(solution)/shard_map/psum | solution.py:85
  1441.3 75.9 %psum.141 = f32[1]{0:T(128)} all-reduce(f32[1]{0:T(128)} %bitcast.40), channel_id=1, replica_groups=mesh['src'=4,'slab'=32] {'slab'}, use_global_device_ids=true, to_apply=%region_31.32 | all-reduce | flops 1 | bytes 8 | tf_op jit(solution)/shard_map/psum | solution.py:76
  1530.2 8.3 collective-permute-done.19
  1538.5 3.8 fusion.106
  1542.3 83.4 %psum.142 = f32[1]{0:T(128)} all-reduce(f32[1]{0:T(128)} %bitcast.42), channel_id=1, replica_groups=mesh['src'=4,'slab'=32] {'slab'}, use_global_device_ids=true, to_apply=%region_33.34 | all-reduce | flops 1 | bytes 8 | tf_op jit(solution)/shard_map/psum | solution.py:85
  1627.0 4.9 multiply_add_fusion
  1638.2 4.0 collective-permute-done.21
  1642.2 6.6 fusion.11
  1648.8 337.1 %all-reduce.52.cloned.1.call-done = f32[8,256,256]{2,1,0:T(8,128)} async-done(((f32[8,256,256]{2,1,0:T(8,128)}), f32[8,256,256]{2,1,0:T(8,128)}) %all-reduce.52.cloned.1.call-update) | async-done | bytes 2097168 | tf_op jit(solution)/shard_map/psum | solution.py:134
  (216 shorter events, 118.1 us)
Async XLA Ops:
  6.5 1979.4 %all-reduce.52.cloned.1.call-start = ((), (), s32[]{:S(2)}) async-start(), calls=%async_computation | async-start | bytes 4194304 | tf_op jit(solution)/shard_map/psum | solution.py:134
  10.6 33.2 %copy-start.37 = (f32[8,256,256]{2,1,0:T(8,128)}, f32[8,256,256]{2,1,0:T(8,128)S(1)}, u32[]{:S(2)}) copy-start(f32[8,256,256]{2,1,0:T(8,128)S(1)} %get-tuple-element.92) | copy-start | bytes 6291460
  12.3 31.5 %collective-permute-start.1 = (f32[2,1,256,256]{3,2,1,0:T(8,128)}, f32[2,1,256,256]{3,2,1,0:T(8,128)S(1)}, u32[]{:S(2)}, u32[]{:S(2)}) collective-permute-start(f32[2,1,256,256]{3,2,1,0:T(8,128)} %get-tuple-element.36), channel_id=1, source_target_pairs={{1,0},{2,1},{3,2},{4,3},{5,4},{6,5},{7,6},{8,7},{9,8},{10,9},{11,1... | collective-permute-start | bytes 1572872 | tf_op jit(solution)/shard_map/ppermute | solution.py:17
  13.7 30.1 %collective-permute-start.2 = (f32[2,1,256,256]{3,2,1,0:T(8,128)}, f32[2,1,256,256]{3,2,1,0:T(8,128)}, u32[]{:S(2)}, u32[]{:S(2)}) collective-permute-start(f32[2,1,256,256]{3,2,1,0:T(8,128)} %get-tuple-element.37), channel_id=1, source_target_pairs={{0,1},{1,2},{2,3},{3,4},{4,5},{5,6},{6,7},{7,8},{8,9},{9,10},{10,1... | collective-permute-start | bytes 1572872 | tf_op jit(solution)/shard_map/ppermute | solution.py:14
  20.0 27.9 %collective-permute-start = (f32[1,1,256,256]{3,2,1,0:T(8,128)}, f32[1,1,256,256]{3,2,1,0:T(8,128)S(1)}, u32[]{:S(2)}, u32[]{:S(2)}) collective-permute-start(f32[1,1,256,256]{3,2,1,0:T(8,128)} %get-tuple-element.104), channel_id=1, source_target_pairs={{0,1},{1,2},{2,3},{3,4},{4,5},{5,6},{6,7},{7,8},{8,9},{9,10},{10,1... | collective-permute-start | bytes 786440 | tf_op jit(solution)/shard_map/ppermute | solution.py:14
  22.6 25.3 %collective-permute-start.3 = (f32[1,1,256,256]{3,2,1,0:T(8,128)}, f32[1,1,256,256]{3,2,1,0:T(8,128)S(1)}, u32[]{:S(2)}, u32[]{:S(2)}) collective-permute-start(f32[1,1,256,256]{3,2,1,0:T(8,128)} %get-tuple-element.103), channel_id=1, source_target_pairs={{1,0},{2,1},{3,2},{4,3},{5,4},{6,5},{7,6},{8,7},{9,8},{10,9},{11,1... | collective-permute-start | bytes 786440 | tf_op jit(solution)/shard_map/ppermute | solution.py:17
  47.9 571.9 %copy-start = (f32[1,9,256,256]{3,2,1,0:T(8,128)}, f32[1,9,256,256]{3,2,1,0:T(8,128)S(1)}, u32[]{:S(2)}) copy-start(f32[1,9,256,256]{3,2,1,0:T(8,128)S(1)} %get-tuple-element.32) | copy-start | bytes 7077892
  47.9 10.8 copy-start.58
  47.9 10.8 copy-start.59
  58.7 16.8 copy-start.2
  61.4 8.3 collective-permute-start.4
  65.5 10.0 collective-permute-start.5
  248.6 11.1 copy-start.8
  249.1 6.2 collective-permute-start.6
  252.0 7.7 collective-permute-start.7
  428.2 5.1 collective-permute-start.8
  430.1 7.7 collective-permute-start.9
  605.3 6.7 collective-permute-start.10
  608.7 11.0 copy-start.11
  608.7 11.0 copy-start.18
  608.7 11.0 copy-start.25
  608.7 11.0 copy-start.32
  608.8 11.0 collective-permute-start.11
  955.1 11.7 copy-start.33
  956.5 8.8 collective-permute-start.12
  959.7 7.2 collective-permute-start.13
  1144.7 14.2 copy-start.7
  1145.2 5.8 collective-permute-start.14
  1147.7 11.2 copy-start.13
  1147.7 11.2 copy-start.20
  1147.7 11.2 copy-start.27
  1147.7 11.2 copy-start.34
  1147.7 11.1 collective-permute-start.15
  1334.1 15.5 copy-start.5
  1334.6 6.5 collective-permute-start.16
  1337.8 11.9 copy-start.14
  1337.8 11.9 copy-start.21
  1337.8 11.9 copy-start.28
  1337.8 11.9 copy-start.35
  1337.8 11.8 collective-permute-start.17
  1522.4 7.8 collective-permute-start.18
  1525.8 12.7 copy-start.15
  1525.8 12.7 copy-start.22
  1525.8 12.7 copy-start.29
  1525.8 12.7 copy-start.36
  1525.8 12.7 collective-permute-start.19
  1632.3 5.9 collective-permute-start.20
  1634.5 7.6 collective-permute-start.21
  (37 other events, 257.1 us)
Sparse Core Ops, SparseCore 0:
  1648.9 336.9 all-reduce.51
where the time goes:
time: 2010 us; the launch traced here: 2000 us
  blocking collectives  1260 us (63%)
  waiting for transfers between devices  396 us (20%)
  other arithmetic  159 us (8%)
  local copies, waits for them, and re-layouts  96.7 us (5%)
  starting transfers between devices  51.4 us (3%)
  between operations  33.6 us (2%)
    psum x8, blocking collectives, squares(): return lax.psum(inner(resid, resid), 'slab')  625 us
    psum x6, blocking collectives, solve(): alpha = norm_now / lax.psum(inner(direction, image), 'slab')  484 us
    psum x1, waiting for transfers between devices, shards(): return lax.psum(partial_sum, 'src')  337 us
    psum x1, blocking collectives, shards(): values = lax.psum(picked, 'slab')  149 us
    reduce_sum x15, other arithmetic, inner(): return jnp.sum(first * second, axis=(1, 2, 3))  65.9 us
    ppermute x11, waiting for transfers between devices, extended(): lax.ppermute(lax.slice_in_dim(block, 0, width, axis=dim), axis, backward)  52.6 us
    gather x1, local copies, waits for them, and re-layouts, shards(): picked = flat[:, index].reshape(sources, 2, -1) * owned[None]  45.5 us
    scatter-add x1, other arithmetic, shards(): back = jnp.zeros((sources, extent * plane), jnp.float32).at[:, wide_index...  44.6 us
  transfers between devices with their start and end apart: 23, of which 16 were waited for; matrix products, arithmetic and copies ran while one was open for 2% of the time, Pallas kernels for 0%

commit v1 on v0

v1 whole, which is shorter than its diff:
```python
import functools

import jax
import jax.numpy as jnp
from jax import lax
from jax.experimental import pallas as pl
from jax.experimental.pallas import tpu as pltpu
from jax.sharding import PartitionSpec as P

MESH = pl.DeviceIdType.MESH
F32 = jnp.float32
VMEM = pltpu.VMEM
SMEM = pltpu.SMEM
DMA = pltpu.SemaphoreType.DMA
PAD = 8
WIDE = 4
ROWS = 64
THETA = (6.0, 2.0, 10.0)


def lane_iota(shape):
    return lax.broadcasted_iota(jnp.int32, shape, len(shape) - 1)


def fold(value):
    rows, cols = value.shape
    return jnp.sum(value.reshape(rows // 8, 8, cols), axis=0)


def next_lane(value):
    return pltpu.roll(value, value.shape[1] - 1, 1)


def prev_lane(value):
    return pltpu.roll(value, 1, 1)


def chunks(nx):
    rows = min(ROWS, nx)
    return [(r, rows) for r in range(0, nx, rows)]


def make_coefs(sig, dg, hx, hy, hz, count, first, last, nx):
    cols = sig.shape[-1]

    def body(q, carry):
        low_in = jnp.logical_and(q - 1 >= first, q <= last).astype(F32)
        for r, rows in chunks(nx):
            here = sig[q + 1, pl.ds(PAD + r, rows), :]
            up = sig[q + 1, pl.ds(PAD + r + 1, rows), :]
            down = sig[q + 1, pl.ds(PAD + r - 1, rows), :]
            low = sig[q, pl.ds(PAD + r, rows), :]
            high = sig[q + 2, pl.ds(PAD + r, rows), :]
            lane = lane_iota(here.shape)
            right = jnp.where(lane == cols - 1, 0.0, next_lane(here))
            left = jnp.where(lane == 0, 0.0, prev_lane(here))
            near = 0.5 * (here + right)
            hx[q, pl.ds(r, rows), :] = jnp.where(lane == cols - 1, 0.0, near)
            hy[q, pl.ds(PAD + r, rows), :] = 0.5 * (here + up)
            hz[q, pl.ds(r, rows), :] = (0.5 * low_in) * (here + low)
            total = ((up + down) + (left + right)) + (low + high)
            dg[q, pl.ds(r, rows), :] = 3.0 * here + 0.5 * total
        return carry

    lax.fori_loop(0, count, body, 0)


def make_top(sig, hz, count, first, last, nx):
    inside = jnp.logical_and(count - 1 >= first, count <= last).astype(F32)
    for r, rows in chunks(nx):
        here = sig[count + 1, pl.ds(PAD + r, rows), :]
        low = sig[count, pl.ds(PAD + r, rows), :]
        hz[count, pl.ds(r, rows), :] = (0.5 * inside) * (here + low)


def operator(v, p, dg, hx, hy, hz, q, r, rows):
    here = v[p, pl.ds(PAD + r, rows), :]
    wx = hx[q, pl.ds(r, rows), :]
    acc = dg[q, pl.ds(r, rows), :] * here
    acc = acc - wx * next_lane(here)
    acc = acc - prev_lane(wx * here)
    acc = acc - hy[q, pl.ds(PAD + r, rows), :] * v[p, pl.ds(PAD + r + 1, rows), :]
    acc = acc - hy[q, pl.ds(PAD + r - 1, rows), :] * v[p, pl.ds(PAD + r - 1, rows), :]
    acc = acc - hz[q, pl.ds(r, rows), :] * v[p - 1, pl.ds(PAD + r, rows), :]
    acc = acc - hz[q + 1, pl.ds(r, rows), :] * v[p + 1, pl.ds(PAD + r, rows), :]
    return here, acc


def zero_pads(ref, nx):
    zero = jnp.zeros((ref.shape[0], PAD, ref.shape[2]), F32)
    ref[:, pl.ds(0, PAD), :] = zero
    ref[:, pl.ds(PAD + nx, PAD), :] = zero


def splat(row, index):
    return jnp.sum(jnp.where(lane_iota(row.shape) == index, row, 0.0), axis=1, keepdims=True)


def solve_small(row, scale, thetas):
    gram = {}
    n = 0
    for i in range(4):
        for j in range(i + 1):
            gram[i, j] = gram[j, i] = splat(row, n)
            n += 1
    last = splat(row, n)
    mat = {}
    for i in range(4):
        for j in range(i + 1):
            if j == 3:
                mat[i, j] = last
            else:
                mat[i, j] = scale * gram[i, j + 1] + thetas[j] * gram[i, j]
    low, inv = {}, {}
    for j in range(4):
        pivot = mat[j, j]
        for k in range(j):
            pivot = pivot - low[j, k] * low[j, k] * mat["d", k]
        mat["d", j] = pivot
        good = pivot > 1e-7 * mat[j, j]
        inv[j] = jnp.where(good, 1.0 / jnp.where(good, pivot, 1.0), 0.0)
        for i in range(j + 1, 4):
            value = mat[i, j]
            for k in range(j):
                value = value - low[i, k] * low[j, k] * mat["d", k]
            low[i, j] = value * inv[j]
    y = []
    for i in range(4):
        value = gram[i, 0]
        for k in range(i):
            value = value - low[i, k] * y[k]
        y.append(value)
    c = [None] * 4
    for i in reversed(range(4)):
        value = y[i] * inv[i]
        for k in range(i + 1, 4):
            value = value - low[k, i] * c[k]
        c[i] = value
    return c


def pack_row(accs):
    lane = lane_iota((1, 128))
    row = jnp.zeros((1, 128), F32)
    for n, acc in enumerate(accs):
        total = jnp.sum(jnp.sum(acc, axis=0, keepdims=True), axis=1, keepdims=True)
        row = row + jnp.where(lane == n, total, 0.0)
    return row


def send_all(buf, send_sem, recv_sem, src, me, slabs):
    for d in range(1, slabs):
        pltpu.make_async_remote_copy(
            src_ref=buf.at[0],
            dst_ref=buf.at[d],
            send_sem=send_sem,
            recv_sem=recv_sem,
            device_id=(src, lax.rem(me + d, slabs)),
            device_id_type=MESH,
        ).start()


def wait_all(buf, sem, slabs):
    rest = buf.at[pl.ds(1, slabs - 1)]
    pltpu.make_async_copy(rest, rest, sem).wait()


def greet(src, me, slabs, others):
    barrier = pltpu.get_barrier_semaphore()
    for d in range(1, slabs):
        pl.semaphore_signal(
            barrier, inc=1, device_id=(src, lax.rem(me + d, slabs)), device_id_type=MESH
        )
    for other in others:
        pl.semaphore_signal(barrier, inc=1, device_id=(other, me), device_id_type=MESH)
    pl.semaphore_wait(barrier, slabs - 1 + len(others))


def flip(src, bit):
    return src + bit - 2 * bit * (lax.rem(src // bit, 2))


def remote(src_ref, dst_ref, send_sem, recv_sem, target):
    return pltpu.make_async_remote_copy(
        src_ref=src_ref,
        dst_ref=dst_ref,
        send_sem=send_sem,
        recv_sem=recv_sem,
        device_id=target,
        device_id_type=MESH,
    )


def first_kernel(
    slabs, lc, pt, u, tan, halo_out, uh_out, mean_out,
    sig, wgt, uw, dg, hx, hy, hz, v0, v1, v2, v3, lch, pth, far, stat, mom,
    s_first, r_first, s_core, r_core, s_far, r_far, s_x, r_x, s_c2, r_c2, s_v, r_v, s_all, r_all,
):
    src = lax.axis_index("src")
    me = lax.axis_index("slab")
    depth, nx, cols = lc.shape
    has_low = me > 0
    has_high = me < slabs - 1
    core = lax.rem(src, 2)
    mate, across = flip(src, 1), flip(src, 2)
    greet(src, me, slabs, (mate, across))

    def both(send):
        @pl.when(has_high)
        def _():
            send(0, me + 1)

        @pl.when(has_low)
        def _():
            send(1, me - 1)

    def arrives(side):
        return has_low if side == 0 else has_high

    def near(side):
        return depth - 1 if side == 0 else 0

    def copy_u(side, to):
        return remote(u.at[near(side)], uh_out.at[side], s_first.at[0, side], r_first.at[0, side], (src, to))

    def copy_c(ref, dst, side, to):
        return remote(ref.at[near(side)], dst.at[side], s_first.at[1, side], r_first.at[1, side], (src, to))

    def begin(side, to):
        copy_u(side, to).start()

        @pl.when(core == 0)
        def _():
            copy_c(lc, lch, side, to).start()

        @pl.when(core == 1)
        def _():
            copy_c(pt, pth, side, to).start()

    both(begin)

    zero_pads(sig, nx)
    zero_pads(wgt, nx)
    zero_pads(uw, nx)
    zero_pads(hy, nx)
    for ref in (v0, v1, v2, v3):
        zero_pads(ref, nx)

    def own(q, acc):
        for r, rows in chunks(nx):
            value = jnp.exp(lc[q, pl.ds(r, rows), :])
            sig[q + 1, pl.ds(PAD + r, rows), :] = value
            wgt[q + 1, pl.ds(PAD + r, rows), :] = value * pt[q, pl.ds(r, rows), :]
            uw[q + 1, pl.ds(PAD + r, rows), :] = u[q, pl.ds(r, rows), :]
            acc = acc + fold(value)
        return acc

    acc = lax.fori_loop(0, depth, own, jnp.zeros((8, cols), F32))
    stat[0] = jnp.broadcast_to(pack_row([acc]), (8, 128))
    send_all(stat, s_all.at[0], r_all.at[0], src, me, slabs)

    far_plane = {0: depth - 2 - src, 1: 1 + src}

    def copy_far(side, to):
        return remote(lc.at[far_plane[side]], far.at[side, 0], s_far.at[side], r_far.at[side], (src, to))

    both(lambda side, to: copy_far(side, to).start())

    for side in (0, 1):
        got = arrives(side)

        @pl.when(got)
        def _():
            copy_u(side, me).wait_recv()

            @pl.when(core == 0)
            def _():
                copy_c(lc, lch, side, me).wait_recv()
                remote(lch.at[side], lch.at[side], s_core.at[side], r_core.at[side], (mate, me)).start()

            @pl.when(core == 1)
            def _():
                copy_c(pt, pth, side, me).wait_recv()
                remote(pth.at[side], pth.at[side], s_core.at[side], r_core.at[side], (mate, me)).start()

    for side in (0, 1):
        plane = 0 if side == 0 else depth + 1

        @pl.when(arrives(side))
        def _():
            @pl.when(core == 0)
            def _():
                remote(lch.at[side], pth.at[side], s_core.at[side], r_core.at[side], (mate, me)).wait_recv()

            @pl.when(core == 1)
            def _():
                remote(pth.at[side], lch.at[side], s_core.at[side], r_core.at[side], (mate, me)).wait_recv()

            for r, rows in chunks(nx):
                value = jnp.exp(lch[side, pl.ds(r, rows), :])
                sig[plane, pl.ds(PAD + r, rows), :] = value
                wgt[plane, pl.ds(PAD + r, rows), :] = value * pth[side, pl.ds(r, rows), :]
                uw[plane, pl.ds(PAD + r, rows), :] = uh_out[side]  [r : r + rows, :]

        @pl.when(jnp.logical_not(arrives(side)))
        def _():
            for ref in (sig, wgt, uw):
                ref[plane, pl.ds(PAD, nx), :] = jnp.zeros((nx, cols), F32)
            uh_out[side] = jnp.zeros((nx, cols), F32)

    def rhs_plane(q, carry):
        for r, rows in chunks(nx):
            c = wgt[q + 1, pl.ds(PAD + r, rows), :]
            f = uw[q + 1, pl.ds(PAD + r, rows), :]
            lane = lane_iota(c.shape)
            cr = jnp.where(lane == cols - 1, 0.0, next_lane(c))
            fr = jnp.where(lane == cols - 1, 0.0, next_lane(f))
            flow = (c + cr) * (f - fr)
            total = flow + jnp.where(lane == 0, c * f, -prev_lane(flow))
            for dq, dr in ((0, 1), (0, -1), (1, 0), (-1, 0)):
                cj = wgt[q + 1 + dq, pl.ds(PAD + r + dr, rows), :]
                fj = uw[q + 1 + dq, pl.ds(PAD + r + dr, rows), :]
                total = total + (c + cj) * (f - fj)
            v0[q + 1, pl.ds(PAD + r, rows), :] = -0.5 * total
        return carry

    fields = (v0, v1, v2, v3)

    def copy_v(k, side, to):
        plane = depth if side == 0 else 1
        halo = 0 if side == 0 else depth + 1
        ref = fields[k]
        return remote(
            ref.at[plane, pl.ds(PAD, nx)], ref.at[halo, pl.ds(PAD, nx)],
            s_v.at[k, side], r_v.at[k, side], (src, to),
        )

    def halo_ready(k):
        for side in (0, 1):
            @pl.when(arrives(side))
            def _():
                copy_v(k, side, me).wait_recv()

    for ref in fields:
        @pl.when(jnp.logical_not(has_low))
        def _():
            ref[0, pl.ds(PAD, nx), :] = jnp.zeros((nx, cols), F32)

        @pl.when(jnp.logical_not(has_high))
        def _():
            ref[depth + 1, pl.ds(PAD, nx), :] = jnp.zeros((nx, cols), F32)

    def edges_first(plane, carry):
        carry = lax.fori_loop(0, 2, lambda i, c: plane(i * (depth - 1), c), carry)
        return carry

    def inner(plane, carry):
        return lax.fori_loop(1, depth - 1, plane, carry)

    edges_first(rhs_plane, 0)
    both(lambda side, to: copy_v(0, side, to).start())
    inner(rhs_plane, 0)
    first, last = -me * depth, (slabs - me) * depth - 1
    make_coefs(sig, dg, hx, hy, hz, depth, first, last, nx)
    make_top(sig, hz, depth, first, last, nx)

    wait_all(stat, r_all.at[0], slabs)
    mean = jnp.sum(stat[...], axis=0)
    mean = jnp.sum(jnp.where(lane_iota((8, 128)) == 0, mean, 0.0), axis=1, keepdims=True)[0:1]
    mean = mean * (1.0 / (slabs * depth * nx * cols))
    mean_out[...] = jnp.broadcast_to(mean, (8, 128))
    scale = 6.0 * mean
    inv = 1.0 / scale

    zero = jnp.zeros((8, cols), F32)
    dots = []
    for k in range(3):
        shift = THETA[k] * mean * inv

        def step(q, accs, k=k, shift=shift):
            accs = list(accs)
            for r, rows in chunks(nx):
                here, image = operator(fields[k], q + 1, dg, hx, hy, hz, q, r, rows)
                new = inv * image - shift * here
                fields[k + 1][q + 1, pl.ds(PAD + r, rows), :] = new
                if k == 0:
                    accs[0] = accs[0] + fold(here * here)
                for i in range(k + 1):
                    other = here if i == k else fields[i][q + 1, pl.ds(PAD + r, rows), :]
                    accs[i + (k == 0)] = accs[i + (k == 0)] + fold(new * other)
                accs[-1] = accs[-1] + fold(new * new)
            return tuple(accs)

        accs = (zero,) * (3 if k == 0 else k + 2)
        accs = inner(step, accs)
        halo_ready(k)
        accs = edges_first(step, accs)
        both(lambda side, to: copy_v(k + 1, side, to).start())
        dots.extend(accs)

    def energy(q, acc):
        for r, rows in chunks(nx):
            here, image = operator(v3, q + 1, dg, hx, hy, hz, q, r, rows)
            acc = acc + fold(here * image)
        return acc

    acc = inner(energy, zero)

    for side in (0, 1):
        @pl.when(arrives(side))
        def _():
            copy_far(side, me).wait_recv()
            remote(far.at[side, 0], far.at[side, 1], s_x.at[side], r_x.at[side], (across, me)).start()

    halo_ready(3)
    dots.append(edges_first(energy, acc))
    mom[0] = jnp.broadcast_to(pack_row(dots), (8, 128))
    send_all(mom, s_all.at[1], r_all.at[1], src, me, slabs)

    for side in (0, 1):
        @pl.when(arrives(side))
        def _():
            remote(far.at[side, 0], far.at[side, 1], s_x.at[side], r_x.at[side], (across, me)).wait_recv()
            remote(
                far.at[side, pl.ds(0, 2)], far.at[side, pl.ds(2, 2)],
                s_c2.at[side], r_c2.at[side], (mate, me),
            ).start()

    wait_all(mom, r_all.at[1], slabs)
    row = jnp.sum(mom[...], axis=0)[0:1]
    c = solve_small(row, scale, [t * mean for t in THETA])

    def combine(q, carry):
        for r, rows in chunks(nx):
            value = c[0] * v0[q + 1, pl.ds(PAD + r, rows), :]
            for i in (1, 2, 3):
                value = value + c[i] * fields[i][q + 1, pl.ds(PAD + r, rows), :]
            tan[q, pl.ds(r, rows), :] = value
        return carry

    lax.fori_loop(0, depth, combine, 0)

    for side in (0, 1):
        @pl.when(arrives(side))
        def _():
            remote(
                far.at[side, pl.ds(0, 2)], far.at[side, pl.ds(2, 2)],
                s_c2.at[side], r_c2.at[side], (mate, me),
            ).wait_recv()
            halo_out[side, 0] = lch[side]
            owners = (src, across, mate, flip(mate, 2))
            for n in range(4):
                halo_out[side, 1 + owners[n]] = far[side, n]

        @pl.when(jnp.logical_not(arrives(side)))
        def _():
            for n in range(5):
                halo_out[side, n] = jnp.zeros((nx, cols), F32)

    def sent(side, to):
        copy_u(side, to).wait_send()
        copy_c(lc, lch, side, to).wait_send()
        copy_far(side, to).wait_send()
        for k in range(4):
            copy_v(k, side, to).wait_send()

    both(sent)
    for side in (0, 1):
        @pl.when(arrives(side))
        def _():
            remote(lch.at[side], lch.at[side], s_core.at[side], r_core.at[side], (mate, me)).wait_send()
            remote(far.at[side, 0], far.at[side, 1], s_x.at[side], r_x.at[side], (across, me)).wait_send()
            remote(
                far.at[side, pl.ds(0, 2)], far.at[side, pl.ds(2, 2)],
                s_c2.at[side], r_c2.at[side], (mate, me),
            ).wait_send()
    wait_all(stat, s_all.at[0], slabs)
    wait_all(mom, s_all.at[1], slabs)


def first_solve(slabs, lc, pt, u):
    depth, nx, cols = lc.shape
    plane = (nx + 2 * PAD, cols)
    full = pl.BlockSpec(memory_space=VMEM)
    return pl.pallas_call(
        functools.partial(first_kernel, slabs),
        name="first_solve",
        out_shape=[
            jax.ShapeDtypeStruct((depth, nx, cols), F32),
            jax.ShapeDtypeStruct((2, 5, nx, cols), F32),
            jax.ShapeDtypeStruct((2, nx, cols), F32),
            jax.ShapeDtypeStruct((8, 128), F32),
        ],
        in_specs=[full] * 3,
        out_specs=[full] * 4,
        scratch_shapes=[VMEM((depth + 2, *plane), F32)] * 3
        + [
            VMEM((depth, nx, cols), F32),
            VMEM((depth, nx, cols), F32),
            VMEM((depth, *plane), F32),
            VMEM((depth + 1, nx, cols), F32),
        ]
        + [VMEM((depth + 2, *plane), F32)] * 4
        + [
            VMEM((2, nx, cols), F32),
            VMEM((2, nx, cols), F32),
            VMEM((2, 4, nx, cols), F32),
            VMEM((slabs, 8, 128), F32),
            VMEM((slabs, 8, 128), F32),
        ]
        + [DMA((2, 2)), DMA((2, 2))]
        + [DMA((2,))] * 8
        + [DMA((4, 2)), DMA((4, 2)), DMA((2,)), DMA((2,))],
        compiler_params=pltpu.CompilerParams(
            collective_id=0, has_side_effects=True, vmem_limit_bytes=56 << 20
        ),
    )(lc, pt, u)


def gather_kernel(group, nx, dipoles, bounds, keys, perm, field, out):
    out[...] = jnp.zeros_like(out)
    cols = field.shape[1]
    lane = lane_iota((1, cols))
    short = lane_iota((1, 128))
    start, stop, base = bounds[0], bounds[1], bounds[2]
    limit = field.shape[0] - 1
    top = keys.shape[0] - 1

    def body(g, carry):
        parts = []
        for e in range(group):
            j = start + g * group + e
            at = jnp.minimum(j, top)
            key, o = keys[at], perm[at]
            line = jnp.clip(key // cols - base, 0, limit)
            sign = jnp.where(j < stop, jnp.where(o < dipoles, 1.0, -1.0), 0.0)
            k = lax.rem(o, dipoles)
            picked = jnp.where(lane == lax.rem(key, cols), field[pl.ds(line, 1), :], 0.0)
            value = jnp.sum(picked, axis=1, keepdims=True) * sign
            parts.append((k // 128, jnp.where(short == lax.rem(k, 128), value, 0.0)))
        for line, value in parts:
            out[pl.ds(line, 1), :] = out[pl.ds(line, 1), :] + value
        return carry

    lax.fori_loop(0, (stop - start + group - 1) // group, body, 0)


def gather(bounds, keys, perm, field, dipoles):
    smem = pl.BlockSpec(memory_space=SMEM)
    full = pl.BlockSpec(memory_space=VMEM)
    return pl.pallas_call(
        functools.partial(gather_kernel, 8, field.shape[1], dipoles),
        name="gather",
        out_shape=jax.ShapeDtypeStruct((dipoles // 128, 128), F32),
        in_specs=[smem, smem, smem, full],
        out_specs=full,
        compiler_params=pltpu.CompilerParams(vmem_limit_bytes=24 << 20),
    )(bounds, keys, perm, field)


def share_kernel(slabs, part, out, buf, send_sem, recv_sem):
    src = lax.axis_index("src")
    me = lax.axis_index("slab")
    greet(src, me, slabs, ())
    buf[0] = part[...]
    send_all(buf, send_sem, recv_sem, src, me, slabs)
    wait_all(buf, recv_sem, slabs)
    out[...] = jnp.sum(buf[...], axis=0)
    wait_all(buf, send_sem, slabs)


def share(slabs, part):
    full = pl.BlockSpec(memory_space=VMEM)
    return pl.pallas_call(
        functools.partial(share_kernel, slabs),
        name="share_data",
        out_shape=jax.ShapeDtypeStruct(part.shape, F32),
        in_specs=[full],
        out_specs=full,
        scratch_shapes=[VMEM((slabs, *part.shape), F32), DMA(()), DMA(())],
        compiler_params=pltpu.CompilerParams(
            collective_id=1, has_side_effects=True, vmem_limit_bytes=16 << 20
        ),
    )(part)


def scatter_kernel(group, nx, dipoles, bounds, keys, perm, data, out):
    planes, _, cols = out.shape
    lane = lane_iota((1, cols))
    start, stop, base = bounds[0], bounds[1], bounds[2]
    top = keys.shape[0] - 1

    def clear(q, carry):
        out[q] = jnp.zeros(out.shape[1:], F32)
        return carry

    lax.fori_loop(0, planes, clear, 0)

    def body(g, carry):
        parts = []
        for e in range(group):
            j = start + g * group + e
            at = jnp.minimum(j, top)
            key, o = keys[at], perm[at]
            line = jnp.clip(key // cols - base, 0, planes * nx - 1)
            sign = jnp.where(j < stop, jnp.where(o < dipoles, 1.0, -1.0), 0.0)
            k = lax.rem(o, dipoles)
            value = data[k // 128, lax.rem(k, 128)] * sign
            parts.append((line // nx, PAD + lax.rem(line, nx), jnp.where(lane == lax.rem(key, cols), value, 0.0)))
        for q, line, value in parts:
            out[q, pl.ds(line, 1), :] = out[q, pl.ds(line, 1), :] + value
        return carry

    lax.fori_loop(0, (stop - start + group - 1) // group, body, 0)


def scatter(bounds, keys, perm, data, planes, nx, cols):
    smem = pl.BlockSpec(memory_space=SMEM)
    full = pl.BlockSpec(memory_space=VMEM)
    dipoles = data.shape[0] * 128
    return pl.pallas_call(
        functools.partial(scatter_kernel, 8, nx, dipoles),
        name="scatter",
        out_shape=jax.ShapeDtypeStruct((planes, nx + 2 * PAD, cols), F32),
        in_specs=[smem, smem, smem, smem],
        out_specs=full,
        compiler_params=pltpu.CompilerParams(vmem_limit_bytes=24 << 20),
    )(bounds, keys, perm, data)


def second_kernel(
    slabs, lc, halo, u, uh, mean_in, v0, out,
    sig, dg, hx, hy, hz, v1, v2, v3, adj, give, take, pair, cross, mom,
    s_all, r_all, s_give, r_give, s_pair, r_pair, s_out, r_out,
):
    src = lax.axis_index("src")
    me = lax.axis_index("slab")
    depth, nx, cols = lc.shape
    half = depth // 2
    core = lax.rem(src, 2)
    mate, across = flip(src, 1), flip(src, 2)
    greet(src, me, slabs, (mate, across))
    wide = depth + 2 * WIDE

    zero_pads(sig, nx)
    zero_pads(hy, nx)
    for ref in (v1, v2, v3, adj):
        zero_pads(ref, nx)

    def own(q, carry):
        for r, rows in chunks(nx):
            sig[q + WIDE + 1, pl.ds(PAD + r, rows), :] = jnp.exp(lc[q, pl.ds(r, rows), :])
        return carry

    lax.fori_loop(0, depth, own, 0)
    low_in, high_in = (me > 0).astype(F32), (me < slabs - 1).astype(F32)

    def sides(n, carry):
        for r, rows in chunks(nx):
            sig[WIDE - n, pl.ds(PAD + r, rows), :] = low_in * jnp.exp(halo[0, n, pl.ds(r, rows), :])
            sig[WIDE + 1 + depth + n, pl.ds(PAD + r, rows), :] = high_in * jnp.exp(halo[1, n, pl.ds(r, rows), :])
        return carry

    lax.fori_loop(0, WIDE + 1, sides, 0)
    first, last = WIDE - me * depth, WIDE + (slabs - me) * depth - 1
    make_coefs(sig, dg, hx, hy, hz, wide, first, last, nx)
    make_top(sig, hz, wide, first, last, nx)

    mean = mean_in[0:1, 0:1]
    scale = 6.0 * mean
    inv = 1.0 / scale
    fields = (v0, v1, v2, v3)
    zero = jnp.zeros((8, cols), F32)
    dots = []
    for k in range(3):
        shift = THETA[k] * mean * inv

        def step(q, accs, k=k, shift=shift, dotted=True):
            accs = list(accs)
            for r, rows in chunks(nx):
                here, image = operator(fields[k], q + 1, dg, hx, hy, hz, q + k + 1, r, rows)
                new = inv * image - shift * here
                fields[k + 1][q, pl.ds(PAD + r, rows), :] = new
                if not dotted:
                    continue
                if k == 0:
                    accs[0] = accs[0] + fold(here * here)
                for i in range(k + 1):
                    other = here if i == k else fields[i][q + k + 1 - i, pl.ds(PAD + r, rows), :]
                    accs[i + (k == 0)] = accs[i + (k == 0)] + fold(new * other)
                accs[-1] = accs[-1] + fold(new * new)
            return tuple(accs)

        planes = wide - 2 * (k + 1)
        rim = WIDE - (k + 1)
        plain = functools.partial(step, dotted=False)
        lax.fori_loop(0, rim, plain, ())
        dots.extend(lax.fori_loop(rim, rim + depth, step, (zero,) * (3 if k == 0 else k + 2)))
        lax.fori_loop(rim + depth, planes, plain, ())

    def energy(q, acc):
        for r, rows in chunks(nx):
            here, image = operator(v3, q + 1, dg, hx, hy, hz, q + WIDE, r, rows)
            acc = acc + fold(here * image)
        return acc

    dots.append(lax.fori_loop(0, depth, energy, zero))
    mom[0] = jnp.broadcast_to(pack_row(dots), (8, 128))
    send_all(mom, s_all, r_all, src, me, slabs)
    wait_all(mom, r_all, slabs)
    row = jnp.sum(mom[...], axis=0)[0:1]
    c = solve_small(row, scale, [t * mean for t in THETA])

    def combine(q, carry):
        for r, rows in chunks(nx):
            value = c[3] * v3[q, pl.ds(PAD + r, rows), :]
            for i in (0, 1, 2):
                value = value + c[i] * fields[i][q + 3 - i, pl.ds(PAD + r, rows), :]
            adj[q, pl.ds(PAD + r, rows), :] = value
        return carry

    lax.fori_loop(0, depth + 2, combine, 0)

    def partial(q, low, high, dst, slot):
        for r, rows in chunks(nx):
            f = u[q, pl.ds(r, rows), :]
            a = adj[q + 1, pl.ds(PAD + r, rows), :]
            lane = lane_iota(f.shape)
            fr = jnp.where(lane == cols - 1, 0.0, next_lane(f))
            ar = jnp.where(lane == cols - 1, 0.0, next_lane(a))
            flow = (f - fr) * (a - ar)
            total = flow + jnp.where(lane == 0, f * a, prev_lane(flow))
            if r + rows < nx:
                fu = u[q, pl.ds(r + 1, rows), :]
            else:
                fu = jnp.concatenate([u[q, pl.ds(r + 1, rows - 1), :], jnp.zeros((1, cols), F32)], axis=0)
            if r > 0:
                fd = u[q, pl.ds(r - 1, rows), :]
            else:
                fd = jnp.concatenate([jnp.zeros((1, cols), F32), u[q, pl.ds(0, rows - 1), :]], axis=0)
            total = total + (f - fu) * (a - adj[q + 1, pl.ds(PAD + r + 1, rows), :])
            total = total + (f - fd) * (a - adj[q + 1, pl.ds(PAD + r - 1, rows), :])
            total = total + (f - low[0][low[1], pl.ds(r, rows), :]) * (a - adj[q, pl.ds(PAD + r, rows), :])
            total = total + (f - high[0][high[1], pl.ds(r, rows), :]) * (a - adj[q + 2, pl.ds(PAD + r, rows), :])
            scaled = -0.5 * sig[q + WIDE + 1, pl.ds(PAD + r, rows), :] * total
            dst[slot, pl.ds(r, rows), :] = scaled

    def part_of(first_plane, dst, after):
        for n in range(half):
            @pl.when(first_plane == 0)
            def _():
                partial(n, (uh, 0) if n == 0 else (u, n - 1), (u, n + 1), dst, n)

            @pl.when(first_plane != 0)
            def _():
                q = half + n
                partial(q, (u, q - 1), (uh, 1) if q == depth - 1 else (u, q + 1), dst, n)

            after(n)

    def copy_give(n):
        return remote(give.at[n], take.at[n], s_give.at[n], r_give.at[n], (mate, me))

    def copy_pair(n):
        return remote(pair.at[n], cross.at[n], s_pair.at[n], r_pair.at[n], (across, me))

    def copy_out(n):
        slot = core * half + n
        return remote(out.at[slot], out.at[slot], s_out.at[n], r_out.at[n], (mate, me))

    part_of((1 - core) * half, give, lambda n: copy_give(n).start())

    def kept(n):
        copy_give(n).wait_recv()
        pair[n] = pair[n] + take[n]
        copy_pair(n).start()

    part_of(core * half, pair, kept)
    for n in range(half):
        copy_pair(n).wait_recv()
        out[core * half + n] = pair[n] + cross[n]
        copy_out(n).start()
    for n in range(half):
        copy_out(n).wait_recv()
    for n in range(half):
        copy_out(n).wait_send()
        copy_give(n).wait_send()
        copy_pair(n).wait_send()
    wait_all(mom, s_all, slabs)


def second_solve(slabs, lc, halo, u, uh, mean, v0):
    depth, nx, cols = lc.shape
    plane = (nx + 2 * PAD, cols)
    wide = depth + 2 * WIDE
    half = depth // 2
    full = pl.BlockSpec(memory_space=VMEM)
    return pl.pallas_call(
        functools.partial(second_kernel, slabs),
        name="second_solve",
        out_shape=jax.ShapeDtypeStruct((depth, nx, cols), F32),
        in_specs=[full] * 6,
        out_specs=full,
        scratch_shapes=[
            VMEM((wide + 2, *plane), F32),
            VMEM((wide, nx, cols), F32),
            VMEM((wide, nx, cols), F32),
            VMEM((wide, *plane), F32),
            VMEM((wide + 1, nx, cols), F32),
            VMEM((wide - 2, *plane), F32),
            VMEM((wide - 4, *plane), F32),
            VMEM((wide - 6, *plane), F32),
            VMEM((depth + 2, *plane), F32),
        ]
        + [VMEM((half, nx, cols), F32)] * 4
        + [VMEM((slabs, 8, 128), F32)]
        + [DMA(()), DMA(())]
        + [DMA((half,))] * 6,
        compiler_params=pltpu.CompilerParams(
            collective_id=2, has_side_effects=True, vmem_limit_bytes=58 << 20
        ),
    )(lc, halo, u, uh, mean, v0)


def shards(slabs, log_cond, perturb, potentials, rec_depth, rec_plan):
    depth, nx, cols = log_cond.shape
    plane = nx * cols
    dipoles = rec_depth.shape[1]
    me = lax.axis_index("slab")
    u = potentials[0]
    flat = (rec_depth * plane + rec_plan).reshape(-1)
    keys, perm = lax.sort_key_val(flat, jnp.arange(2 * dipoles, dtype=jnp.int32))
    planes = rec_depth.reshape(-1)

    def bounds(first, last):
        return jnp.stack([
            jnp.sum((planes < first).astype(jnp.int32)),
            jnp.sum((planes < last).astype(jnp.int32)),
            first * nx,
        ])

    tangent, halo, uh, mean = first_solve(slabs, log_cond, perturb, u)
    part = gather(
        bounds(me * depth, (me + 1) * depth), keys, perm, tangent.reshape(depth * nx, cols), dipoles
    )
    data = share(slabs, part)
    back = scatter(
        bounds(me * depth - WIDE, (me + 1) * depth + WIDE), keys, perm, data, depth + 2 * WIDE, nx, cols
    )
    return second_solve(slabs, log_cond, halo, u, uh, mean, back)


def solution(mesh):
    in_specs = (
        P("slab", None, None),
        P("slab", None, None),
        P("src", "slab", None, None),
        P(),
        P(),
    )
    return jax.shard_map(
        functools.partial(shards, mesh.shape["slab"]),
        mesh=mesh,
        in_specs=in_specs,
        out_specs=P("slab", None, None),
        check_vma=False,
    )
```

time: 2010 us -> 207 us (0.10)
  blocking collectives: 1260 us -> 0 us
  waiting for transfers between devices: 396 us -> 0 us
  Pallas kernels: 0 us -> 190 us
  other arithmetic: 159 us -> 10.4 us
  local copies, waits for them, and re-layouts: 96.7 us -> 6.66 us
  starting transfers between devices: 51.4 us -> 0 us
  between operations: 33.6 us -> 0.06 us
    psum x15 -> x0, blocking collectives: 1260 us -> none  [the longest x8 625 us: squares(): return lax.psum(inner(resid, resid), 'slab')]
    psum x1 -> x0, waiting for transfers between devices: 337 us -> none  [shards(): return lax.psum(partial_sum, 'src')]
    pallas_call x0 -> x5, Pallas kernels: none -> 190 us  [the longest x1 84.9 us: first_solve(): pl.pallas_call(functools.partial(first_kernel, slabs), name='first_solve'...]
    reduce_sum x15 -> x1, other arithmetic: 65.9 us -> 1.59 us  [bounds(): jnp.sum((planes < first).astype(jnp.int32))]
    ppermute x22 -> x0, waiting for transfers between devices: 59.2 us -> none  [the longest x11 52.6 us: extended(): lax.ppermute(lax.slice_in_dim(block, 0, width, axis=dim), axis, backward)]
    ppermute x22 -> x0, starting transfers between devices: 51.4 us -> none  [the longest x11 34.5 us: extended(): lax.ppermute(lax.slice_in_dim(block, block.shape[dim] - width, None, axis...]
    gather x1 -> x0, local copies, waits for them, and re-layouts: 45.5 us -> none  [shards(): picked = flat[:, index].reshape(sources, 2, -1) * owned[None]]
    scatter-add x1 -> x0, other arithmetic: 44.6 us -> none  [shards(): back = jnp.zeros((sources, extent * plane), jnp.float32).at[:, wide_index...]
  transfers between devices with their start and end apart: 23 -> 0, of which waited for: 16 -> 0; matrix products, arithmetic and copies ran while one was open for 2% -> 0% of each run, Pallas kernels for 0% -> 0%
where the time goes in v1:
time: 207 us
  Pallas kernels  190 us (92%)
  other arithmetic  10.4 us (5%)
  local copies, waits for them, and re-layouts  6.66 us (3%)
    pallas_call x1, Pallas kernels, first_solve(): pl.pallas_call(functools.partial(first_kernel, slabs), name='first_solve'...  84.9 us
    pallas_call x1, Pallas kernels, second_solve(): pl.pallas_call(functools.partial(second_kernel, slabs), name='second_solv...  73.7 us
    pallas_call x1, Pallas kernels, share(): pl.pallas_call(functools.partial(share_kernel, slabs), name='share_data',...  13 us
    pallas_call x1, Pallas kernels, scatter(): pl.pallas_call(functools.partial(scatter_kernel, 8, nx, dipoles), name='s...  12 us
    unnamed x6, local copies, waits for them, and re-layouts  6.66 us
    pallas_call x1, Pallas kernels, gather(): pl.pallas_call(functools.partial(gather_kernel, 8, field.shape[1], dipole...  6.3 us
    sort x1, other arithmetic, shards(): lax.sort_key_val(flat, jnp.arange(2 * dipoles, dtype=jnp.int32))  6.16 us

profile of v1, /device:TPU:1, one launch (start us, length us, event | category | flops | bytes accessed | tf_op | source)
XLA Modules:
  0.0 207.0 jit_solution(13630898037613496414)
XLA Ops:
  0.0 1.6 fusion.2
  1.6 1.4 pad_add_fusion.1.bounds
  3.0 1.3 pad_add_fusion.bounds
  4.3 6.2 %sort.15 = (s32[8192]{0:T(1024)S(1)}, s32[8192]{0:T(1024)S(1)}) sort(s32[8192]{0:T(1024)S(1)} %bitcast.14, s32[8192]{0:T(1024)S(1)} %iota.3), dimensions={0}, to_apply=%region_2.0 | sort | flops 106496 | bytes 131072 | tf_op jit(solution)/shard_map/sort | solution.py:832
  10.4 84.9 %first_solve.1 = (f32[8,256,256]{2,1,0:T(8,128)}, f32[2,5,256,256]{3,2,1,0:T(8,128)}, f32[2,256,256]{2,1,0:T(8,128)}, f32[8,128]{1,0:T(8,128)}) custom-call(f32[8,256,256]{2,1,0:T(8,128)} %lc.3, f32[8,256,256]{2,1,0:T(8,128)} %pt.1, f32[8,256,256]{2,1,0:T(8,128)} %bitcast.12), custom_call_target="tpu_custom_call" | custom-call | tf_op jit(solution)/shard_map/first_solve/pallas_call | solution.py:485
  95.3 0.0 copy-start.1
  95.3 1.6 copy-done.1
  96.9 6.3 %gather.1.part = f32[32,128]{1,0:T(8,128)S(1)} custom-call(s32[3]{0:T(128)S(1)} %pad_add_fusion.1.bounds, s32[8192]{0:T(1024)S(1)} %get-tuple-element.14.keys, s32[8192]{0:T(1024)S(1)} %get-tuple-element.15.perm, f32[2048,256]{1,0:T(8,128)S(1)} %bitcast.11), custom_call_target="tpu_custom_call" | custom-call | tf_op jit(solution)/shard_map/gather/pallas_call | solution.py:551
  103.2 13.0 %share_data.1.data = f32[32,128]{1,0:T(8,128)S(1)} custom-call(f32[32,128]{1,0:T(8,128)S(1)} %gather.1.part), custom_call_target="tpu_custom_call" | custom-call | tf_op jit(solution)/shard_map/share_data/pallas_call | solution.py:574
  116.2 12.0 %scatter.1.v0 = f32[16,272,256]{2,1,0:T(8,128)S(1)} custom-call(s32[3]{0:T(128)S(1)} %pad_add_fusion.bounds, s32[8192]{0:T(1024)S(1)} %get-tuple-element.14.keys, s32[8192]{0:T(1024)S(1)} %get-tuple-element.15.perm, f32[32,128]{1,0:T(8,128)S(1)} %share_data.1.data), custom_call_target="tpu_custom_call" | custom-call | tf_op jit(solution)/shard_map/scatter/pallas_call | solution.py:621
  128.2 0.0 copy-start
  128.2 2.0 copy-done
  130.3 73.7 %second_solve.1 = f32[8,256,256]{2,1,0:T(8,128)} custom-call(f32[8,256,256]{2,1,0:T(8,128)} %lc.3, f32[2,5,256,256]{3,2,1,0:T(8,128)} %get-tuple-element.11.halo, f32[8,256,256]{2,1,0:T(8,128)} %bitcast.13, f32[2,256,256]{2,1,0:T(8,128)} %get-tuple-element.12.uh, f32[8,128]{1,0:T(8,128)} %get-tuple-element.13.mean_in, f32[16,272,256]{2,1,0:T(8,128)} %copy-done), custom_call_target="tpu_custom_call" | custom-call | tf_op jit(solution)/shard_map/second_solve/pallas_call | solution.py:798
  203.9 3.0 %copy.8 = f32[8,256,256]{2,1,0:T(8,128)} copy(f32[8,256,256]{2,1,0:T(8,128)} %second_solve.1) | data formatting | bytes 4194304
  (2 shorter events, 0.0 us)
Async XLA Ops:
  95.3 1.6 copy-start.1
  128.2 2.0 copy-start

commit v2 on v0

v2 whole, which is shorter than its diff:
```python
import functools

import jax
import jax.numpy as jnp
from jax import lax
from jax.experimental import pallas as pl
from jax.experimental.pallas import tpu as pltpu
from jax.sharding import PartitionSpec as P

MESH = pl.DeviceIdType.MESH
F32 = jnp.float32
VMEM = pltpu.VMEM
SMEM = pltpu.SMEM
DMA = pltpu.SemaphoreType.DMA
PAD = 8
WIDE = 4
EARLY = 4
ROWS = 64
THETA = (6.0, 2.0, 10.0)


def lane_iota(shape):
    return lax.broadcasted_iota(jnp.int32, shape, len(shape) - 1)


def fold(value):
    rows, cols = value.shape
    return jnp.sum(value.reshape(rows // 8, 8, cols), axis=0)


def next_lane(value):
    return pltpu.roll(value, value.shape[1] - 1, 1)


def prev_lane(value):
    return pltpu.roll(value, 1, 1)


def chunks(count, start=0):
    out = []
    done = 0
    while done < count:
        rows = min(ROWS, count - done)
        out.append((start + done, rows))
        done += rows
    return out


def make_coefs(sig, dg, hx, hy, hz, start, stop, first, last, pieces, top=True):
    cols = sig.shape[-1]

    def body(q, carry):
        low_in = jnp.logical_and(q - 1 >= first, q <= last).astype(F32)
        for r, rows in pieces:
            here = sig[q + 1, pl.ds(PAD + r, rows), :]
            up = sig[q + 1, pl.ds(PAD + r + 1, rows), :]
            down = sig[q + 1, pl.ds(PAD + r - 1, rows), :]
            low = sig[q, pl.ds(PAD + r, rows), :]
            high = sig[q + 2, pl.ds(PAD + r, rows), :]
            lane = lane_iota(here.shape)
            right = jnp.where(lane == cols - 1, 0.0, next_lane(here))
            left = jnp.where(lane == 0, 0.0, prev_lane(here))
            hx[q, pl.ds(r, rows), :] = jnp.where(lane == cols - 1, 0.0, 0.5 * (here + right))
            hy[q, pl.ds(PAD + r, rows), :] = 0.5 * (here + up)
            hz[q, pl.ds(r, rows), :] = (0.5 * low_in) * (here + low)
            total = ((up + down) + (left + right)) + (low + high)
            dg[q, pl.ds(r, rows), :] = 3.0 * here + 0.5 * total
        return carry

    lax.fori_loop(start, stop, body, 0)
    if not top:
        return
    inside = jnp.logical_and(stop - 1 >= first, stop <= last).astype(F32)
    for r, rows in pieces:
        here = sig[stop + 1, pl.ds(PAD + r, rows), :]
        low = sig[stop, pl.ds(PAD + r, rows), :]
        hz[stop, pl.ds(r, rows), :] = (0.5 * inside) * (here + low)


def operator(v, p, dg, hx, hy, hz, q, r, rows):
    here = v[p, pl.ds(PAD + r, rows), :]
    wx = hx[q, pl.ds(r, rows), :]
    acc = dg[q, pl.ds(r, rows), :] * here
    acc = acc - wx * next_lane(here)
    acc = acc - prev_lane(wx * here)
    acc = acc - hy[q, pl.ds(PAD + r, rows), :] * v[p, pl.ds(PAD + r + 1, rows), :]
    acc = acc - hy[q, pl.ds(PAD + r - 1, rows), :] * v[p, pl.ds(PAD + r - 1, rows), :]
    acc = acc - hz[q, pl.ds(r, rows), :] * v[p - 1, pl.ds(PAD + r, rows), :]
    acc = acc - hz[q + 1, pl.ds(r, rows), :] * v[p + 1, pl.ds(PAD + r, rows), :]
    return here, acc


def zero_pads(ref, nx):
    zero = jnp.zeros((ref.shape[0], PAD, ref.shape[2]), F32)
    ref[:, pl.ds(0, PAD), :] = zero
    ref[:, pl.ds(PAD + nx, PAD), :] = zero


def splat(row, index):
    return jnp.sum(jnp.where(lane_iota(row.shape) == index, row, 0.0), axis=1, keepdims=True)


def solve_small(row, scale, thetas, n=0):
    gram = {}
    for i in range(4):
        for j in range(i + 1):
            gram[i, j] = gram[j, i] = splat(row, n)
            n += 1
    last = splat(row, n)
    mat = {}
    for i in range(4):
        for j in range(i + 1):
            if j == 3:
                mat[i, j] = last
            else:
                mat[i, j] = scale * gram[i, j + 1] + thetas[j] * gram[i, j]
    low, inv = {}, {}
    for j in range(4):
        pivot = mat[j, j]
        for k in range(j):
            pivot = pivot - low[j, k] * low[j, k] * mat["d", k]
        mat["d", j] = pivot
        good = pivot > 1e-7 * mat[j, j]
        inv[j] = jnp.where(good, 1.0 / jnp.where(good, pivot, 1.0), 0.0)
        for i in range(j + 1, 4):
            value = mat[i, j]
            for k in range(j):
                value = value - low[i, k] * low[j, k] * mat["d", k]
            low[i, j] = value * inv[j]
    y = []
    for i in range(4):
        value = gram[i, 0]
        for k in range(i):
            value = value - low[i, k] * y[k]
        y.append(value)
    c = [None] * 4
    for i in reversed(range(4)):
        value = y[i] * inv[i]
        for k in range(i + 1, 4):
            value = value - low[k, i] * c[k]
        c[i] = value
    return c


def pack_row(accs):
    lane = lane_iota((1, 128))
    row = jnp.zeros((1, 128), F32)
    for n, acc in enumerate(accs):
        total = jnp.sum(jnp.sum(acc, axis=0, keepdims=True), axis=1, keepdims=True)
        row = row + jnp.where(lane == n, total, 0.0)
    return row


def remote(src_ref, dst_ref, send_sem, recv_sem, target):
    return pltpu.make_async_remote_copy(
        src_ref=src_ref,
        dst_ref=dst_ref,
        send_sem=send_sem,
        recv_sem=recv_sem,
        device_id=target,
        device_id_type=MESH,
    )


def flip(src, bit):
    return src + bit - 2 * bit * (lax.rem(src // bit, 2))


def partners(me, slabs):
    near = 4
    fours = slabs // near
    place, four = lax.rem(me, near), me // near
    return (
        [four * near + lax.rem(place + d, near) for d in range(1, near)],
        [lax.rem(four + d, fours) * near + place for d in range(1, fours)],
    )


def pair_group(me):
    place = lax.rem(me, 4)
    return [me - place + lax.rem(place + d, 4) for d in range(4)]


def signal_all(src, me, slabs, others):
    barrier = pltpu.get_barrier_semaphore()
    targets = [(src, t) for group in partners(me, slabs) for t in group] + others
    for target in targets:
        pl.semaphore_signal(barrier, inc=1, device_id=target, device_id_type=MESH)
    return barrier, len(targets)


class Sum:
    def __init__(self, src, me, slabs, levels, across=None):
        groups = [[(src, t) for t in group] for group in partners(me, slabs)]
        if across is not None:
            groups[0] += [(across, t) for t in pair_group(me)]
        self.levels = [(level, group) for level, group in zip(levels, groups) if group]

    def send(self, n, value):
        (buf, send_sem, recv_sem), group = self.levels[n]
        buf[0] = value
        for d, target in enumerate(group):
            remote(buf.at[0], buf.at[d + 1], send_sem, recv_sem, target).start()

    def _wait(self, n, which):
        level, group = self.levels[n]
        rest = level[0].at[pl.ds(1, len(group))]
        pltpu.make_async_copy(rest, rest, level[which]).wait()

    def receive(self, n):
        self._wait(n, 2)
        return jnp.sum(self.levels[n][0][0][...], axis=0)

    def start(self, value):
        self.send(0, value)

    def middle(self):
        value = self.receive(0)
        if len(self.levels) > 1:
            self.send(1, value)
        return value

    def end(self, value):
        return self.receive(1) if len(self.levels) > 1 else value

    def whole(self, value):
        self.start(value)
        return self.end(self.middle())

    def close(self):
        for n in range(len(self.levels)):
            self._wait(n, 1)


def sum_scratch(slabs, shape, first=4):
    return [
        VMEM((first, *shape), F32), DMA(()), DMA(()),
        VMEM((max(slabs // 4, 2), *shape), F32), DMA(()), DMA(()),
    ]


def sum_levels(refs):
    return (refs[0:3], refs[3:6])


def first_kernel(
    slabs, lc_in, pt_in, u, tan, mean_out, lc_half, lc_near, u_mine, u_first, u_rest,
    lc, pt, lch, uh, sig, wgt, uw, dg, hx, hy, hz, v0, v1, v2, v3, pth, edge, relayed,
    s_load, s_take, s_first, r_first, s_c, r_c, s_x, r_x, s_core, r_core, s_v, r_v, s_e, r_e, s_out, r_in, *sums,
):
    src = lax.axis_index("src")
    me = lax.axis_index("slab")
    depth, nx, cols = lc.shape
    half = nx // 2
    has_low = me > 0
    has_high = me < slabs - 1
    core, side_x = lax.rem(src, 2), src // 2
    mate, across = flip(src, 1), flip(src, 2)
    inner_rows = pl.ds(PAD, nx)
    loads = [
        pltpu.make_async_copy(u, uw.at[pl.ds(1, depth), inner_rows], s_load.at[0]),
        pltpu.make_async_copy(lc_in, lc, s_load.at[1]),
        pltpu.make_async_copy(pt_in, pt, s_load.at[2]),
    ]
    for load in loads:
        load.start()
    ring = [(src, lax.rem(me + 1, slabs)), (src, lax.rem(me + slabs - 1, slabs))]
    barrier, count = signal_all(src, me, slabs, ring + [(mate, me)] + [(across, t) for t in (me, ring[0][1], ring[1][1])])
    pl.semaphore_wait(barrier, count)
    mean_sum = Sum(src, me, slabs, sum_levels(sums[0:6]))
    mom_sum = Sum(src, me, slabs, sum_levels(sums[6:12]))

    def arrives(side):
        return has_low if side == 0 else has_high

    def below(side):
        return me + 1 if side == 0 else me - 1

    def sends(side):
        return has_high if side == 0 else has_low

    def near(side):
        return depth - 1 if side == 0 else 0

    def part(n):
        return pl.ds(n * half, half)

    def copy_u(side, n, to, slot=None, onward=False):
        return routed(
            u.at[near(side), part(n)], uh.at[side, part(n)],
            s_first.at[side, n], r_first.at[side, n], to, side, slot, onward,
        )

    low_mid = slabs // 2 - 1
    by_relay = (
        jnp.logical_and(me == low_mid, side_x == 1),
        jnp.logical_and(me == low_mid + 1, side_x == 0),
    )

    def send(n, side, copy, slot):
        if n == 0:
            pl.when(sends(side))(lambda: copy(side, n, below(side)).start())
            return
        pl.when(jnp.logical_and(sends(side), jnp.logical_not(by_relay[side])))(
            lambda: copy(side, n, below(side)).start()
        )
        pl.when(by_relay[side])(lambda: copy(side, n, me, slot).start())

    def relay(copy, slot):
        for side in (0, 1):
            @pl.when(jnp.logical_and(me == low_mid, side_x == side))
            def _():
                remote(relayed.at[slot], relayed.at[slot], s_out.at[slot], r_in.at[slot], (across, me)).wait_recv()
                copy(side, 1, me, slot, True).start()

    def routed(ref, dst, send_sem, recv_sem, to, side, slot, onward):
        if slot is None:
            return remote(ref, dst, send_sem, recv_sem, (src, to))
        if onward:
            return remote(relayed.at[slot], dst, s_out.at[slot], recv_sem, (across, me + 1 - side))
        return remote(ref, relayed.at[slot], send_sem, r_in.at[slot], (across, me - side))

    my_rows = pl.ds(pl.multiple_of(half * side_x, PAD), half)
    their_rows = pl.ds(pl.multiple_of(half * (1 - side_x), PAD), half)

    def copy_c(ref, dst, side, to):
        return remote(
            ref.at[near(side), my_rows], dst.at[side, my_rows], s_c.at[side], r_c.at[side], (src, to)
        )

    def swap(ref, side, rows):
        return remote(ref.at[side, rows], ref.at[side, rows], s_x.at[side], r_x.at[side], (across, me))

    def forward(ref, side):
        return remote(ref.at[side], ref.at[side], s_core.at[side], r_core.at[side], (mate, me))

    def by_core(body):
        pl.when(core == 0)(lambda: body(lc_in, lch))
        pl.when(core == 1)(lambda: body(pt_in, pth))

    for side in (0, 1):
        @pl.when(sends(side))
        def _():
            by_core(lambda ref, dst: copy_c(ref, dst, side, below(side)).start())
    for n in (0, 1):
        for side in (0, 1):
            send(n, side, copy_u, 0)

    for ref in (sig, wgt, uw, hy, v0, v1, v2, v3):
        zero_pads(ref, nx)
    for load in loads:
        load.wait()

    def own(q, acc):
        for r, rows in chunks(nx):
            value = jnp.exp(lc[q, pl.ds(r, rows), :])
            sig[q + 1, pl.ds(PAD + r, rows), :] = value
            wgt[q + 1, pl.ds(PAD + r, rows), :] = value * pt[q, pl.ds(r, rows), :]
            acc = acc + fold(value)
        return acc

    acc = lax.fori_loop(0, depth, own, jnp.zeros((8, cols), F32))
    mean_sum.start(pack_row([acc]))

    fields = (v0, v1, v2, v3)
    for ref in fields:
        for side in (0, 1):
            def clear(ref=ref, side=side):
                ref[side * (depth + 1), pl.ds(PAD, nx), :] = jnp.zeros((nx, cols), F32)

            if ref is v3:
                clear()
            else:
                pl.when(jnp.logical_not(arrives(side)))(clear)
    mean_part = mean_sum.middle()

    for side in (0, 1):
        @pl.when(arrives(side))
        def _():
            def body(ref, dst):
                copy_c(ref, dst, side, me).wait_recv()
                swap(dst, side, my_rows).start()

            by_core(body)
    relay(copy_u, 0)
    for side in (0, 1):
        @pl.when(arrives(side))
        def _():
            def body(ref, dst):
                swap(dst, side, their_rows).wait_recv()
                forward(dst, side).start()

            by_core(body)

    def rhs_rows(q, pieces):
        for r, rows in pieces:
            c = wgt[q + 1, pl.ds(PAD + r, rows), :]
            f = uw[q + 1, pl.ds(PAD + r, rows), :]
            lane = lane_iota(c.shape)
            cr = jnp.where(lane == cols - 1, 0.0, next_lane(c))
            fr = jnp.where(lane == cols - 1, 0.0, next_lane(f))
            flow = (c + cr) * (f - fr)
            total = flow + jnp.where(lane == 0, c * f, -prev_lane(flow))
            for dq, dr in ((0, 1), (0, -1), (1, 0), (-1, 0)):
                cj = wgt[q + 1 + dq, pl.ds(PAD + r + dr, rows), :]
                fj = uw[q + 1 + dq, pl.ds(PAD + r + dr, rows), :]
                total = total + (c + cj) * (f - fj)
            v0[q + 1, pl.ds(PAD + r, rows), :] = -0.5 * total

    def copy_v(k, side, n, to, slot=None, onward=False):
        plane = depth if side == 0 else 1
        halo = 0 if side == 0 else depth + 1
        rows = pl.ds(PAD + n * half, half)
        ref = fields[k]
        return routed(
            ref.at[plane, rows], ref.at[halo, rows], s_v.at[k, side, n], r_v.at[k, side, n], to, side, slot, onward
        )

    def send_edge(k, side, n):
        send(n, 1 - side, functools.partial(copy_v, k), k + 1)

    for n in (0, 1):
        for side in (0, 1):
            plane = 0 if side == 0 else depth + 1

            @pl.when(arrives(side))
            def _():
                if n == 0:
                    pl.when(core == 0)(lambda: forward(pth, side).wait_recv())
                    pl.when(core == 1)(lambda: forward(lch, side).wait_recv())
                copy_u(side, n, me).wait_recv()
                for r, rows in chunks(half, n * half):
                    value = jnp.exp(lch[side, pl.ds(r, rows), :])
                    sig[plane, pl.ds(PAD + r, rows), :] = value
                    wgt[plane, pl.ds(PAD + r, rows), :] = value * pth[side, pl.ds(r, rows), :]
                    uw[plane, pl.ds(PAD + r, rows), :] = uh[side, pl.ds(r, rows), :]

            @pl.when(jnp.logical_not(arrives(side)))
            def _():
                for ref in (sig, wgt, uw):
                    ref[plane, pl.ds(PAD + n * half, half), :] = jnp.zeros((half, cols), F32)
                lch[side, part(n), :] = jnp.zeros((half, cols), F32)

            rhs_rows(0 if side == 0 else depth - 1, chunks(half, n * half))
            send_edge(0, side, n)

    frame_rows = half + PAD
    mine = half * side_x - PAD * side_x
    theirs = (half - PAD) - mine
    takes = []
    for n, (ref, dst, first, at) in enumerate((
        (lc, lc_half, 0, mine),
        (lch, lc_near, 0, mine),
        (uw, u_mine, 0, PAD + mine),
        (uw, u_first, 0, PAD + theirs),
        (uw, u_rest, EARLY, PAD + theirs),
    )):
        rows = pl.ds(pl.multiple_of(at, PAD), frame_rows)
        takes.append(pltpu.make_async_copy(ref.at[pl.ds(first, dst.shape[0]), rows], dst, s_take.at[n]))
    for take in takes:
        take.start()

    def inner(body, carry):
        return lax.fori_loop(1, depth - 1, body, carry)

    def rhs_plane(q, carry):
        rhs_rows(q, chunks(nx))
        return carry

    inner(rhs_plane, 0)
    first, last = -me * depth, (slabs - me) * depth - 1
    make_coefs(sig, dg, hx, hy, hz, 0, depth, first, last, chunks(nx))

    mean = splat(mean_sum.end(mean_part), 0) * (1.0 / (slabs * depth * nx * cols))
    mean_out[...] = jnp.broadcast_to(mean, (8, 128))
    scale = 6.0 * mean
    inv = 1.0 / scale

    zero = jnp.zeros((8, cols), F32)
    dots = []
    for k in range(3):
        shift = THETA[k] * mean * inv

        def step(q, accs, pieces=None, k=k, shift=shift):
            accs = list(accs)
            for r, rows in pieces or chunks(nx):
                here, image = operator(fields[k], q + 1, dg, hx, hy, hz, q, r, rows)
                new = inv * image - shift * here
                fields[k + 1][q + 1, pl.ds(PAD + r, rows), :] = new
                if k == 0:
                    accs[0] = accs[0] + fold(here * here)
                for i in range(k + 1):
                    other = here if i == k else fields[i][q + 1, pl.ds(PAD + r, rows), :]
                    accs[i + (k == 0)] = accs[i + (k == 0)] + fold(new * other)
                accs[-1] = accs[-1] + fold(new * new)
            return tuple(accs)

        accs = inner(step, (zero,) * (3 if k == 0 else k + 2))
        relay(functools.partial(copy_v, k), k + 1)
        for n in (0, 1):
            for side in (0, 1):
                pl.when(arrives(side))(lambda side=side, n=n, k=k: copy_v(k, side, n, me).wait_recv())
                accs = step(0 if side == 0 else depth - 1, accs, chunks(half, n * half))
                if k < 2:
                    send_edge(k + 1, side, n)
        dots.extend(accs)

    def copy_edge(side, to):
        plane = depth if side == 0 else 1
        return remote(
            v3.at[plane, pl.ds(PAD + side * half, half)], edge.at[side], s_e.at[side], r_e.at[side], (src, to)
        )

    for side in (0, 1):
        pl.when(sends(side))(lambda side=side: copy_edge(side, below(side)).start())
    def energy(q, acc):
        for r, rows in chunks(nx):
            here, image = operator(v3, q + 1, dg, hx, hy, hz, q, r, rows)
            acc = acc + fold(here * image)
        return acc

    acc = lax.fori_loop(0, depth, energy, zero)
    for side in (0, 1):
        got = arrives(side)
        pl.when(got)(lambda side=side: copy_edge(side, me).wait_recv())

        @pl.when(jnp.logical_not(got))
        def _():
            edge[side] = jnp.zeros((half, cols), F32)

        for r, rows in chunks(half):
            at = side * half + r
            face = hz[side * depth, pl.ds(at, rows), :] * v3[1 + side * (depth - 1), pl.ds(PAD + at, rows), :]
            acc = acc - 2.0 * fold(face * edge[side, pl.ds(r, rows), :])
    dots.append(acc)
    mom_sum.start(pack_row(dots))
    value = mom_sum.middle()

    row = mom_sum.end(value)
    c = solve_small(row, scale, [t * mean for t in THETA])

    def combine(q, carry):
        for r, rows in chunks(nx):
            value = c[0] * v0[q + 1, pl.ds(PAD + r, rows), :]
            for i in (1, 2, 3):
                value = value + c[i] * fields[i][q + 1, pl.ds(PAD + r, rows), :]
            tan[q, pl.ds(r, rows), :] = value
        return carry

    lax.fori_loop(0, depth, combine, 0)

    for take in takes:
        take.wait()
    for slot in range(4):
        pl.when(me == low_mid)(
            lambda slot=slot: remote(
                relayed.at[slot], relayed.at[slot], s_out.at[slot], r_in.at[slot], (across, me)
            ).wait_send()
        )
    for side in (0, 1):
        @pl.when(sends(side))
        def _():
            copy_c(lc_in, lch, side, me).wait_send()
            copy_edge(side, me).wait_send()
            for n in (0, 1):
                copy_u(side, n, me).wait_send()
                for k in range(3):
                    copy_v(k, side, n, me).wait_send()

        @pl.when(arrives(side))
        def _():
            swap(lch, side, my_rows).wait_send()
            forward(lch, side).wait_send()
    mean_sum.close()
    mom_sum.close()


def first_solve(slabs, lc, pt, u):
    depth, nx, cols = lc.shape
    plane = (nx + 2 * PAD, cols)
    half = nx // 2
    full = pl.BlockSpec(memory_space=VMEM)
    pair = (DMA((2,)), DMA((2,)))
    return pl.pallas_call(
        functools.partial(first_kernel, slabs),
        name="first_solve",
        out_shape=[
            jax.ShapeDtypeStruct((depth, nx, cols), F32),
            jax.ShapeDtypeStruct((8, 128), F32),
            *(
                jax.ShapeDtypeStruct((planes, half + PAD, cols), F32)
                for planes in (depth, 2, depth + 2, EARLY, depth + 2 - EARLY)
            ),
        ],
        in_specs=[pl.BlockSpec(memory_space=pltpu.HBM)] * 3,
        out_specs=[full] * 7,
        scratch_shapes=[VMEM((depth, nx, cols), F32)] * 2
        + [VMEM((2, nx, cols), F32)] * 2
        + [VMEM((depth + 2, *plane), F32)] * 3
        + [
            VMEM((depth, nx, cols), F32),
            VMEM((depth, nx, cols), F32),
            VMEM((depth, *plane), F32),
            VMEM((depth + 1, nx, cols), F32),
        ]
        + [VMEM((depth + 2, *plane), F32)] * 4
        + [VMEM((2, nx, cols), F32), VMEM((2, half, cols), F32), VMEM((4, half, cols), F32)]
        + [DMA((3,)), DMA((5,)), DMA((2, 2)), DMA((2, 2)), *pair, *pair, *pair]
        + [DMA((3, 2, 2)), DMA((3, 2, 2)), *pair, DMA((4,)), DMA((4,))]
        + sum_scratch(slabs, (1, 128)) * 2,
        compiler_params=pltpu.CompilerParams(
            collective_id=0, has_side_effects=True, vmem_limit_bytes=43 << 20
        ),
    )(lc, pt, u)


def search(keys, bound):
    size = keys.shape[0]

    def body(_, ends):
        low, high = ends
        mid = (low + high) // 2
        less = keys[jnp.minimum(mid, size - 1)] < bound
        open_ = low < high
        return (
            jnp.where(jnp.logical_and(open_, less), mid + 1, low),
            jnp.where(jnp.logical_and(open_, jnp.logical_not(less)), mid, high),
        )

    return lax.fori_loop(0, size.bit_length(), body, (jnp.int32(0), jnp.int32(size)))[0]


def bits(count):
    assert count & (count - 1) == 0
    return count.bit_length() - 1


def gather_kernel(group, depth, keys, plan, field, out):
    me = lax.axis_index("slab")
    out[...] = jnp.zeros_like(out)
    lines, cols = field.shape
    nx = lines // depth
    dipoles = plan.shape[1]
    entries = 2 * dipoles
    lane = lane_iota((1, cols))
    short = lane_iota((1, 128))
    start = search(keys, me * depth * entries)
    stop = search(keys, (me + 1) * depth * entries)
    base = me * lines

    def body(g, carry):
        parts = []
        for e in range(group):
            j = start + g * group + e
            key = keys[jnp.minimum(j, entries - 1)]
            o = key & (entries - 1)
            k = o & (dipoles - 1)
            cell = plan[o >> bits(dipoles), k]
            line = ((key >> bits(entries)) << bits(nx)) + (cell >> bits(cols)) - base
            inside = j < stop
            lane_at = jnp.where(inside, cell & (cols - 1), -1)
            picked = jnp.where(lane == lane_at, field[pl.ds(jnp.where(inside, line, 0), 1), :], 0.0)
            value = jnp.sum(picked, axis=1, keepdims=True)
            value = jnp.where(o < dipoles, value, -value)
            parts.append((k >> 7, jnp.where(short == (k & 127), value, 0.0)))
        for line, value in parts:
            out[pl.ds(line, 1), :] = out[pl.ds(line, 1), :] + value
        return carry

    lax.fori_loop(0, (stop - start + group - 1) // group, body, 0)


def gather(keys, plan, field, depth):
    smem = pl.BlockSpec(memory_space=SMEM)
    full = pl.BlockSpec(memory_space=VMEM)
    return pl.pallas_call(
        functools.partial(gather_kernel, 8, depth),
        name="gather",
        out_shape=jax.ShapeDtypeStruct((plan.shape[1] // 128, 128), F32),
        in_specs=[smem, smem, full],
        out_specs=full,
        compiler_params=pltpu.CompilerParams(vmem_limit_bytes=8 << 20),
    )(keys, plan, field)


def share_kernel(slabs, part, out, s_x, r_x, *sums):
    src = lax.axis_index("src")
    me = lax.axis_index("slab")
    side_x = src // 2
    across = flip(src, 2)
    barrier, count = signal_all(src, me, slabs, [(across, me)])
    pl.semaphore_wait(barrier, count)
    total = Sum(src, me, slabs, sum_levels(sums))
    value = total.whole(part[...])
    lines = value.shape[0]
    out[side_x, pl.ds(0, lines), :] = value
    out[side_x, pl.ds(lines, lines), :] = -value
    copy = remote(out.at[side_x], out.at[side_x], s_x, r_x, (across, me))
    copy.start()
    copy.wait()
    total.close()


def share(slabs, part):
    full = pl.BlockSpec(memory_space=VMEM)
    lines = part.shape[0]
    return pl.pallas_call(
        functools.partial(share_kernel, slabs),
        name="share_data",
        out_shape=jax.ShapeDtypeStruct((2, 2 * lines, 128), F32),
        in_specs=[full],
        out_specs=full,
        scratch_shapes=[DMA(()), DMA(())] + sum_scratch(slabs, part.shape),
        compiler_params=pltpu.CompilerParams(
            collective_id=1, has_side_effects=True, vmem_limit_bytes=8 << 20
        ),
    )(part)


def scatter_kernel(group, depth, nx, lines, keys, plan, data, *outs):
    me = lax.axis_index("slab")
    side_x = lax.axis_index("src") // 2
    total, cols = outs[0].shape
    planes = total // lines
    dipoles = plan.shape[1]
    entries = 2 * dipoles
    lane = lane_iota((1, cols))
    low = me * depth - WIDE
    start = search(keys, low * entries)
    stop = search(keys, (low + planes) * entries)
    row_base = (nx // 2) * side_x - 2 * PAD

    def clear(q, carry):
        for out in outs:
            out[pl.ds(pl.multiple_of(q * lines, 8), lines), :] = jnp.zeros((lines, cols), F32)
        return carry

    lax.fori_loop(0, planes, clear, 0)

    def body(g, carry):
        parts = []
        for e in range(group):
            j = start + g * group + e
            key = keys[jnp.minimum(j, entries - 1)]
            o = key & (entries - 1)
            cell = plan[o >> bits(dipoles), o & (dipoles - 1)]
            line = (cell >> bits(cols)) - row_base
            inside = jnp.logical_and(j < stop, jnp.logical_and(line >= PAD, line < lines - PAD))
            hit = lane == jnp.where(inside, cell & (cols - 1), -1)
            at = jnp.where(inside, ((key >> bits(entries)) - low) * lines + line, 0)
            parts.append((at, [jnp.where(hit, data[n, o >> 7, o & 127], 0.0) for n in (0, 1)]))
        for at, values in parts:
            for out, value in zip(outs, values):
                out[pl.ds(at, 1), :] = out[pl.ds(at, 1), :] + value
        return carry

    lax.fori_loop(0, (stop - start + group - 1) // group, body, 0)


def scatter(keys, plan, data, depth, nx, cols):
    smem = pl.BlockSpec(memory_space=SMEM)
    full = pl.BlockSpec(memory_space=VMEM)
    lines = nx // 2 + 4 * PAD
    planes = depth + 2 * WIDE
    back = pl.pallas_call(
        functools.partial(scatter_kernel, 8, depth, nx, lines),
        name="scatter",
        out_shape=[jax.ShapeDtypeStruct((planes * lines, cols), F32)] * 2,
        in_specs=[smem, smem, smem],
        out_specs=[full, full],
        compiler_params=pltpu.CompilerParams(vmem_limit_bytes=8 << 20),
    )(keys, plan, data)
    return [ref.reshape(planes, lines, cols) for ref in back]


def second_kernel(
    slabs, nx, lc_half, lc_near, u_mine, u_first, u_rest, mean_in, v00, v01, out,
    sig, dg, hx, hy, hz, v1, v2, v3, u2, adj, give, take, pair, far,
    s_load, s_u, r_u, s_far, r_far, s_c2, r_c2, s_give, r_give, s_x, r_x, s_own, r_own, s_fwd, r_fwd,
    *sums,
):
    src = lax.axis_index("src")
    me = lax.axis_index("slab")
    depth, _, cols = out.shape
    half = nx // 2
    frame = half + 2 * PAD
    frame_rows = half + PAD
    quarter = depth // 2
    core, side_x = lax.rem(src, 2), src // 2
    mate, across = flip(src, 1), flip(src, 2)
    wide = depth + 2 * WIDE
    ring = [(src, lax.rem(me + 1, slabs)), (src, lax.rem(me + slabs - 1, slabs))]
    barrier, count = signal_all(src, me, slabs, ring + [(mate, me)] + [(across, t) for t in pair_group(me)])
    total = Sum(src, me, slabs, sum_levels(sums), across)
    owned = chunks(half, PAD)
    rims = [(0, PAD), (PAD + half, PAD)]
    every = rims[:1] + owned + rims[1:]

    zero_pads(sig, frame)
    zero_pads(hy, frame)
    for ref in (v1, v2, v3):
        for j in (0, 1):
            zero_pads(ref.at[j], frame)

    outside = pl.ds(pl.multiple_of(PAD + (half + PAD) * side_x, PAD), PAD)
    u2[:, :, pl.ds(pl.multiple_of((half + PAD) * side_x, PAD), PAD), :] = jnp.zeros((2, depth + 2, PAD, cols), F32)
    frame_mine = pl.ds(pl.multiple_of(PAD * (1 - side_x), PAD), frame_rows)
    frame_theirs = pl.ds(pl.multiple_of(PAD * side_x, PAD), frame_rows)
    early = pl.ds(0, EARLY)
    late = pl.ds(EARLY, depth + 2 - EARLY)
    loads = [
        pltpu.make_async_copy(u_mine, u2.at[side_x, :, frame_mine], s_load.at[0]),
        pltpu.make_async_copy(u_first, u2.at[1 - side_x, early, frame_mine], s_load.at[1]),
    ]
    for load in loads:
        load.start()
    low_in, high_in = (me > 0).astype(F32), (me < slabs - 1).astype(F32)

    def conductivity(ref, count, first, factor=None):
        def body(n, carry):
            for r, rows in chunks(frame_rows):
                to = pl.multiple_of(PAD + PAD * (1 - side_x) + r, PAD)
                value = jnp.exp(ref[n, pl.ds(r, rows), :])
                sig[first + 1 + n, pl.ds(to, rows), :] = value if factor is None else factor * value
            sig[first + 1 + n, outside, :] = jnp.zeros((PAD, cols), F32)
            return carry

        lax.fori_loop(0, count, body, 0)

    conductivity(lc_half, depth, WIDE)
    conductivity(lc_near, 1, WIDE - 1, low_in)
    conductivity(lc_near.at[pl.ds(1, 1)], 1, WIDE + depth, high_in)

    arrives = (me > 0, me < slabs - 1)
    sends = (me < slabs - 1, me > 0)
    to_slab = (me + 1, me - 1)
    mine = (pl.ds(2 - 2 * core, 2), pl.ds(2 * core, 2))
    other = (pl.ds(2 * core, 2), pl.ds(2 - 2 * core, 2))

    def copy_far(side, to):
        planes = pl.ds(depth - 3 - 2 * core, 2) if side == 0 else pl.ds(1 + 2 * core, 2)
        return remote(lc_half.at[planes], far.at[side, mine[side]], s_far.at[side], r_far.at[side], (src, to))

    def share_far(side, planes):
        ref = far.at[side, planes]
        return remote(ref, ref, s_c2.at[side], r_c2.at[side], (mate, me))

    copy_rest = remote(u_rest, u2.at[side_x, late, frame_theirs], s_u, r_u, (across, me))
    pl.semaphore_wait(barrier, count)
    for side in (0, 1):
        pl.when(sends[side])(lambda side=side: copy_far(side, to_slab[side]).start())
    copy_rest.start()

    first, last = WIDE - me * depth, WIDE + (slabs - me) * depth - 1
    low_open, high_open = side_x.astype(F32), 1.0 - side_x.astype(F32)

    def coefs(start, stop, top=True):
        make_coefs(sig, dg, hx, hy, hz, start, stop, first, last, every, top)

        def close(q, carry):
            for line, factor in ((2 * PAD - 1, low_open), (2 * PAD + half - 1, high_open)):
                hy[q, pl.ds(line, 1), :] = hy[q, pl.ds(line, 1), :] * factor
            return carry

        lax.fori_loop(start, stop, close, 0)

    mean = mean_in[0:1, 0:1]
    scale = 6.0 * mean
    inv = 1.0 / scale
    zero = jnp.zeros((8, cols), F32)
    fields = [(v0, v1.at[j], v2.at[j], v3.at[j]) for j, v0 in enumerate((v00, v01))]
    sums_of = {}

    def run(k, start, stop, dotted):
        shift = THETA[k] * mean * inv
        for j in (0, 1):
            def step(q, accs, j=j):
                accs = list(accs)
                for r, rows in every:
                    here, image = operator(fields[j][k], q - k, dg, hx, hy, hz, q, r, rows)
                    new = inv * image - shift * here
                    fields[j][k + 1][q - k - 1, pl.ds(PAD + r, rows), :] = new
                    if not dotted or (r, rows) not in owned:
                        continue
                    if k == 0:
                        accs[0] = accs[0] + fold(here * here)
                    for i in range(k + 1):
                        other = here if i == k else fields[j][i][q - i, pl.ds(PAD + r, rows), :]
                        accs[i + (k == 0)] = accs[i + (k == 0)] + fold(new * other)
                    accs[-1] = accs[-1] + fold(new * new)
                return tuple(accs)

            accs = sums_of.get((j, k), (zero,) * (3 if k == 0 else k + 2)) if dotted else ()
            accs = lax.fori_loop(start, stop, step, accs)
            if dotted:
                sums_of[j, k] = accs

    top = WIDE + depth
    coefs(WIDE, top)
    run(0, WIDE, top, True)
    for side in (0, 1):
        @pl.when(arrives[side])
        def _():
            copy_far(side, me).wait_recv()
            share_far(side, mine[side]).start()

        @pl.when(jnp.logical_not(arrives[side]))
        def _():
            far[side] = jnp.zeros(far.shape[1:], F32)

    for k in (1, 2):
        run(k, WIDE + k, top - k, True)
    for side in (0, 1):
        pl.when(arrives[side])(lambda side=side: share_far(side, other[side]).wait_recv())
    conductivity(far.at[0], WIDE, -1, low_in)
    conductivity(far.at[1], WIDE, top + 1, high_in)
    coefs(0, WIDE, False)
    coefs(top, wide)
    for k in range(3):
        run(k, k + 1, WIDE, False)
        if k:
            run(k, WIDE, WIDE + k, True)
            run(k, top - k, top, True)
        run(k, top, wide - k - 1, False)
    dots = [[acc for k in range(3) for acc in sums_of[j, k]] for j in (0, 1)]

    for j in (0, 1):
        def energy(q, acc, j=j):
            for r, rows in owned:
                here, image = operator(v3.at[j], q + 1, dg, hx, hy, hz, q + WIDE, r, rows)
                acc = acc + fold(here * image)
            return acc

        dots[j].append(lax.fori_loop(0, depth, energy, zero))

    row = total.whole(pack_row(dots[0] + dots[1]))
    thetas = [t * mean for t in THETA]
    coef = [solve_small(row, scale, thetas, n) for n in (0, len(dots[0]))]

    def combine(q, carry):
        for j in (0, 1):
            c = coef[j]
            for r, rows in every:
                value = c[3] * v3[j, q, pl.ds(PAD + r, rows), :]
                for i, ref in enumerate(fields[j][:3]):
                    value = value + c[i] * ref[q + 3 - i, pl.ds(PAD + r, rows), :]
                adj[j, q, pl.ds(r, rows), :] = value
        return carry

    lax.fori_loop(0, depth + 2, combine, 0)
    for load in loads:
        load.wait()
    copy_rest.wait()
    for side in (0, 1):
        pl.when(sends[side])(lambda side=side: copy_far(side, me).wait_send())
        pl.when(arrives[side])(lambda side=side: share_far(side, mine[side]).wait_send())

    def partial(q, dst, slot):
        for r, rows in owned:
            total = jnp.zeros((rows, cols), F32)
            for j in (0, 1):
                f = u2[j, q + 1, pl.ds(r, rows), :]
                a = adj[j, q + 1, pl.ds(r, rows), :]
                lane = lane_iota(f.shape)
                fr = jnp.where(lane == cols - 1, 0.0, next_lane(f))
                ar = jnp.where(lane == cols - 1, 0.0, next_lane(a))
                flow = (f - fr) * (a - ar)
                total = total + (flow + jnp.where(lane == 0, f * a, prev_lane(flow)))
                for dq, dr in ((0, 1), (0, -1), (1, 0), (-1, 0)):
                    fj = u2[j, q + 1 + dq, pl.ds(r + dr, rows), :]
                    aj = adj[j, q + 1 + dq, pl.ds(r + dr, rows), :]
                    total = total + (f - fj) * (a - aj)
            scaled = -0.5 * sig[q + WIDE + 1, pl.ds(PAD + r, rows), :] * total
            dst[slot, pl.ds(r - PAD, rows), :] = scaled

    def copy_give(n):
        return remote(give.at[n], take.at[n], s_give.at[n], r_give.at[n], (mate, me))

    rows_mine = pl.ds(pl.multiple_of(half * side_x, PAD), half)
    rows_theirs = pl.ds(pl.multiple_of(half * (1 - side_x), PAD), half)

    def copy_x(n):
        ref = out.at[core * quarter + n, rows_mine]
        return remote(ref, ref, s_x.at[n], r_x.at[n], (across, me))

    def copy_own(n):
        ref = out.at[core * quarter + n, rows_mine]
        return remote(ref, ref, s_own.at[n], r_own.at[n], (mate, me))

    def copy_fwd(n):
        ref = out.at[core * quarter + n, rows_theirs]
        return remote(ref, ref, s_fwd.at[n], r_fwd.at[n], (mate, me))

    def giving(n, carry):
        partial((1 - core) * quarter + n, give, n)
        copy_give(n).start()
        return carry

    def keeping(n, carry):
        partial(core * quarter + n, pair, n)
        copy_give(n).wait_recv()
        for r, rows in chunks(half):
            at = pl.multiple_of(half * side_x + r, PAD)
            out[core * quarter + n, pl.ds(at, rows), :] = pair[n, pl.ds(r, rows), :] + take[n, pl.ds(r, rows), :]
        copy_x(n).start()
        copy_own(n).start()
        return carry

    def passing(n, carry):
        copy_x(n).wait_recv()
        copy_fwd(n).start()
        return carry

    def ending(n, carry):
        copy_own(n).wait_recv()
        copy_fwd(n).wait_recv()
        for copy in (copy_give, copy_x, copy_own, copy_fwd):
            copy(n).wait_send()
        return carry

    for body in (giving, keeping, passing, ending):
        lax.fori_loop(0, quarter, body, 0)
    total.close()


def second_solve(slabs, nx, lc_half, lc_near, u_mine, u_first, u_rest, mean, back):
    depth, _, cols = lc_half.shape
    half = nx // 2
    frame = half + 2 * PAD
    plane = (frame + 2 * PAD, cols)
    wide = depth + 2 * WIDE
    quarter = depth // 2
    full = pl.BlockSpec(memory_space=VMEM)
    anywhere = pl.BlockSpec(memory_space=pl.ANY)
    pair = [DMA((2,)), DMA((2,))]
    return pl.pallas_call(
        functools.partial(second_kernel, slabs, nx),
        name="second_solve",
        out_shape=jax.ShapeDtypeStruct((depth, nx, cols), F32),
        in_specs=[full, full, anywhere, anywhere, anywhere, full, full, full],
        out_specs=full,
        scratch_shapes=[
            VMEM((wide + 2, *plane), F32),
            VMEM((wide, frame, cols), F32),
            VMEM((wide, frame, cols), F32),
            VMEM((wide, *plane), F32),
            VMEM((wide + 1, frame, cols), F32),
            VMEM((2, wide - 2, *plane), F32),
            VMEM((2, wide - 4, *plane), F32),
            VMEM((2, wide - 6, *plane), F32),
            VMEM((2, depth + 2, frame, cols), F32),
            VMEM((2, depth + 2, frame, cols), F32),
        ]
        + [VMEM((quarter, half, cols), F32)] * 3
        + [VMEM((2, WIDE, half + PAD, cols), F32)]
        + [DMA((2,)), DMA(()), DMA(())]
        + pair * 2
        + [DMA((quarter,))] * 8
        + sum_scratch(slabs, (1, 128), 8),
        compiler_params=pltpu.CompilerParams(
            collective_id=2, has_side_effects=True, vmem_limit_bytes=42 << 20
        ),
    )(lc_half, lc_near, u_mine, u_first, u_rest, mean, *back)


def shards(slabs, log_cond, perturb, potentials, rec_depth, rec_plan):
    depth, nx, cols = log_cond.shape
    dipoles = rec_depth.shape[1]
    order = lax.broadcasted_iota(jnp.int32, rec_depth.shape, 0) * dipoles
    order = order + lax.broadcasted_iota(jnp.int32, rec_depth.shape, 1)
    keys = lax.sort((rec_depth * (2 * dipoles) + order).reshape(-1), is_stable=False)
    arguments = (pltpu.with_memory_space_constraint(a, pltpu.HBM) for a in (log_cond, perturb, potentials[0]))
    tangent, mean, lc_half, lc_near, u_mine, u_first, u_rest = first_solve(slabs, *arguments)
    part = gather(keys, rec_plan, tangent.reshape(depth * nx, cols), depth)
    data = share(slabs, part)
    u_first, data = lax.optimization_barrier((u_first, data))
    u_first = lax.ppermute(u_first, "src", [(i, (i + 2) % 4) for i in range(4)])
    back = scatter(keys, rec_plan, data, depth, nx, cols)
    return second_solve(slabs, nx, lc_half, lc_near, u_mine, u_first, u_rest, mean, back)


def solution(mesh):
    in_specs = (
        P("slab", None, None),
        P("slab", None, None),
        P("src", "slab", None, None),
        P(),
        P(),
    )
    return jax.shard_map(
        functools.partial(shards, mesh.shape["slab"]),
        mesh=mesh,
        in_specs=in_specs,
        out_specs=P("slab", None, None),
        check_vma=False,
    )
```

time: 2010 us -> 180 us (0.09)
  blocking collectives: 1260 us -> 0 us
  waiting for transfers between devices: 396 us -> 0.01 us
  Pallas kernels: 0 us -> 171 us
  other arithmetic: 159 us -> 6.43 us
  local copies, waits for them, and re-layouts: 96.7 us -> 1.33 us
  starting transfers between devices: 51.4 us -> 0.66 us
  between operations: 33.6 us -> 0.05 us
    psum x15 -> x0, blocking collectives: 1260 us -> none  [the longest x8 625 us: squares(): return lax.psum(inner(resid, resid), 'slab')]
    psum x1 -> x0, waiting for transfers between devices: 337 us -> none  [shards(): return lax.psum(partial_sum, 'src')]
    pallas_call x0 -> x5, Pallas kernels: none -> 171 us  [the longest x1 70.7 us: first_solve(): pl.pallas_call(functools.partial(first_kernel, slabs), name='first_solve'...]
    reduce_sum x15 -> x0, other arithmetic: 65.9 us -> none  [inner(): return jnp.sum(first * second, axis=(1, 2, 3))]
    ppermute x22 -> x1, waiting for transfers between devices: 59.2 us -> 0.01 us  [shards(): u_first = lax.ppermute(u_first, 'src', [(i, (i + 2) % 4) for i in range(4)])]
    ppermute x22 -> x1, starting transfers between devices: 51.4 us -> 0.66 us  [shards(): u_first = lax.ppermute(u_first, 'src', [(i, (i + 2) % 4) for i in range(4)])]
    gather x1 -> x0, local copies, waits for them, and re-layouts: 45.5 us -> none  [shards(): picked = flat[:, index].reshape(sources, 2, -1) * owned[None]]
    scatter-add x1 -> x0, other arithmetic: 44.6 us -> none  [shards(): back = jnp.zeros((sources, extent * plane), jnp.float32).at[:, wide_index...]
  transfers between devices with their start and end apart: 23 -> 1, of which waited for: 16 -> 0; matrix products, arithmetic and copies ran while one was open for 2% -> 0% of each run, Pallas kernels for 0% -> 5%
where the time goes in v2:
time: 180 us; the launch traced here: 179 us
  Pallas kernels  171 us (95%)
  other arithmetic  6.43 us (4%)
    pallas_call x1, Pallas kernels, first_solve(): pl.pallas_call(functools.partial(first_kernel, slabs), name='first_solve'...  70.7 us
    pallas_call x1, Pallas kernels, second_solve(): pl.pallas_call(functools.partial(second_kernel, slabs, nx), name='second_...  67.8 us
    pallas_call x1, Pallas kernels, share(): pl.pallas_call(functools.partial(share_kernel, slabs), name='share_data',...  15.8 us
    pallas_call x1, Pallas kernels, scatter(): pl.pallas_call(functools.partial(scatter_kernel, 8, depth, nx, lines), na...  9.87 us
    pallas_call x1, Pallas kernels, gather(): pl.pallas_call(functools.partial(gather_kernel, 8, depth), name='gather',...  6.74 us
    sort x1, other arithmetic, shards(): lax.sort((rec_depth * (2 * dipoles) + order).reshape(-1), is_stable=False)  5.59 us
  transfers between devices with their start and end apart: 1, of which 0 were waited for; matrix products, arithmetic and copies ran while one was open for 0% of the time, Pallas kernels for 5%

profile of v2, /device:TPU:1, one launch (start us, length us, event | category | flops | bytes accessed | tf_op | source)
XLA Modules:
  0.0 179.5 jit_solution(2366666511516427502)
XLA Ops:
  0.0 0.8 add_bitcast_fusion
  0.9 5.6 %sort.7.keys = s32[8192]{0:T(1024)S(1)} sort(s32[8192]{0:T(1024)S(1)} %bitcast.11), dimensions={0}, to_apply=%region_0.0 | sort | flops 106496 | bytes 65536 | tf_op jit(solution)/shard_map/sort | solution.py:1071
  6.5 0.0 copy-start
  6.5 70.7 %first_solve.1 = (f32[8,256,256]{2,1,0:T(8,128)S(1)}, f32[8,128]{1,0:T(8,128)S(1)}, f32[8,136,256]{2,1,0:T(8,128)S(1)}, f32[2,136,256]{2,1,0:T(8,128)S(1)}, f32[...) custom-call(f32[8,256,256]{2,1,0:T(8,128)} %lc_in.1, f32[8,256,256]{2,1,0:T(8,128)} %pt_in.1, ...), custom_call_target="tpu_custom_call" | custom-call | tf_op jit(solution)/shard_map/first_solve/pallas_call | solution.py:584
  77.2 0.0 copy-done
  77.2 6.7 %gather.1.part = f32[32,128]{1,0:T(8,128)S(1)} custom-call(s32[8192]{0:T(1024)S(1)} %sort.7.keys, s32[2,4096]{1,0:T(2,128)S(1)} %copy-done, f32[2048,256]{1,0:T(8,128)S(1)} %bitcast.9), custom_call_target="tpu_custom_call" | custom-call | tf_op jit(solution)/shard_map/gather/pallas_call | solution.py:676
  84.0 15.8 %share_data.1.data = f32[2,64,128]{2,1,0:T(8,128)S(1)} custom-call(f32[32,128]{1,0:T(8,128)S(1)} %gather.1.part), custom_call_target="tpu_custom_call" | custom-call | tf_op jit(solution)/shard_map/share_data/pallas_call | solution.py:707
  99.8 0.7 collective-permute-start
  100.5 9.9 %scatter.1 = (f32[2560,256]{1,0:T(8,128)S(1)}, f32[2560,256]{1,0:T(8,128)S(1)}) custom-call(s32[8192]{0:T(1024)S(1)} %sort.7.keys, s32[2,4096]{1,0:T(2,128)S(1)} %copy-done, f32[2,64,128]{2,1,0:T(8,128)S(1)} %share_data.1.data), custom_call_target="tpu_custom_call" | custom-call | tf_op jit(solution)/shard_map/scatter/pallas_call | solution.py:765
  110.3 0.0 collective-permute-done.u_first
  110.4 67.8 %second_solve.1 = f32[8,256,256]{2,1,0:T(8,128)S(1)} custom-call(f32[8,136,256]{2,1,0:T(8,128)S(1)} %get-tuple-element.16.lc_half, f32[2,136,256]{2,1,0:T(8,128)S(1)} %get-tuple-element.17.lc_near, f32[10,136,256]{2,1,0:T(8,128)S(1)} %get-tuple-element.18.u_mine, f32[4,136,256]{2,1,0:T(8,128)S(1)} %collective-permute-done.u_first, ...), custom_call_target="tpu_custom_call" | custom-call | tf_op jit(solution)/shard_map/second_solve/pallas_call | solution.py:1036
  178.2 1.3 copy.8
  (2 shorter events, 0.0 us)
Async XLA Ops:
  6.5 70.8 %copy-start = (s32[2,4096]{1,0:T(2,128)S(1)}, s32[2,4096]{1,0:T(2,128)}, u32[]{:S(2)}) copy-start(s32[2,4096]{1,0:T(2,128)} %plan.3) | copy-start | bytes 98308
  99.8 10.5 %collective-permute-start = (f32[4,136,256]{2,1,0:T(8,128)S(1)}, f32[4,136,256]{2,1,0:T(8,128)S(1)}, u32[]{:S(2)}, u32[]{:S(2)}) collective-permute-start(f32[4,136,256]{2,1,0:T(8,128)S(1)} %get-tuple-element.21), channel_id=1, source_target_pairs={{0,64},{32,96},{64,0},{96,32},{1,65},{33,97},{65,1},{97,33},{2,66}... | collective-permute-start | bytes 1671176 | tf_op jit(solution)/shard_map/ppermute | solution.py:1077

commit v3 on v2

--- a/solution.py
+++ b/solution.py
@@ -288,37 +288,42 @@
     def copy_u(side, n, to, slot=None, onward=False):
         return routed(
             u.at[near(side), part(n)], uh.at[side, part(n)],
-            s_first.at[side, n], r_first.at[side, n], to, side, slot, onward,
+            s_first.at[side, n], r_first.at[side, n], to, slot, onward,
         )
 
     low_mid = slabs // 2 - 1
-    by_relay = (
-        jnp.logical_and(me == low_mid, side_x == 1),
-        jnp.logical_and(me == low_mid + 1, side_x == 0),
-    )
+
+    def by_relay(side):
+        return jnp.logical_and(me == low_mid + side, side_x == 1 - side)
+
+    def is_relay(side):
+        return jnp.logical_and(me == low_mid + side, side_x == side)
 
     def send(n, side, copy, slot):
-        if n == 0:
+        if n == 1:
             pl.when(sends(side))(lambda: copy(side, n, below(side)).start())
             return
-        pl.when(jnp.logical_and(sends(side), jnp.logical_not(by_relay[side])))(
+        pl.when(jnp.logical_and(sends(side), jnp.logical_not(by_relay(side))))(
             lambda: copy(side, n, below(side)).start()
         )
-        pl.when(by_relay[side])(lambda: copy(side, n, me, slot).start())
+        pl.when(by_relay(side))(lambda: copy(side, n, me, slot).start())
+
+    def arrived(slot):
+        return remote(relayed.at[slot], relayed.at[slot], s_out.at[slot], r_in.at[slot], (across, me))
 
     def relay(copy, slot):
         for side in (0, 1):
-            @pl.when(jnp.logical_and(me == low_mid, side_x == side))
+            @pl.when(is_relay(side))
             def _():
-                remote(relayed.at[slot], relayed.at[slot], s_out.at[slot], r_in.at[slot], (across, me)).wait_recv()
-                copy(side, 1, me, slot, True).start()
-
-    def routed(ref, dst, send_sem, recv_sem, to, side, slot, onward):
+                arrived(slot).wait_recv()
+                copy(side, 0, below(side), slot, True).start()
+
+    def routed(ref, dst, send_sem, recv_sem, to, slot, onward):
         if slot is None:
             return remote(ref, dst, send_sem, recv_sem, (src, to))
         if onward:
-            return remote(relayed.at[slot], dst, s_out.at[slot], recv_sem, (across, me + 1 - side))
-        return remote(ref, relayed.at[slot], send_sem, r_in.at[slot], (across, me - side))
+            return remote(relayed.at[slot], dst, s_out.at[slot], recv_sem, (across, to))
+        return remote(ref, relayed.at[slot], send_sem, r_in.at[slot], (across, me))
 
     my_rows = pl.ds(pl.multiple_of(half * side_x, PAD), half)
     their_rows = pl.ds(pl.multiple_of(half * (1 - side_x), PAD), half)
@@ -342,14 +347,20 @@
         @pl.when(sends(side))
         def _():
             by_core(lambda ref, dst: copy_c(ref, dst, side, below(side)).start())
-    for n in (0, 1):
-        for side in (0, 1):
-            send(n, side, copy_u, 0)
 
     for ref in (sig, wgt, uw, hy, v0, v1, v2, v3):
         zero_pads(ref, nx)
     for load in loads:
         load.wait()
+
+    for side in (0, 1):
+        @pl.when(sends(side))
+        def _():
+            copy_c(lc_in, lch, side, me).wait_send()
+
+    for n in (0, 1):
+        for side in (0, 1):
+            send(n, side, copy_u, 0)
 
     def own(q, acc):
         for r, rows in chunks(nx):
@@ -413,7 +424,7 @@
         rows = pl.ds(PAD + n * half, half)
         ref = fields[k]
         return routed(
-            ref.at[plane, rows], ref.at[halo, rows], s_v.at[k, side, n], r_v.at[k, side, n], to, side, slot, onward
+            ref.at[plane, rows], ref.at[halo, rows], s_v.at[k, side, n], r_v.at[k, side, n], to, slot, onward
         )
 
     def send_edge(k, side, n):
@@ -551,16 +562,15 @@
 
     for take in takes:
         take.wait()
-    for slot in range(4):
-        pl.when(me == low_mid)(
-            lambda slot=slot: remote(
-                relayed.at[slot], relayed.at[slot], s_out.at[slot], r_in.at[slot], (across, me)
-            ).wait_send()
-        )
+    for side in (0, 1):
+        @pl.when(is_relay(side))
+        def _():
+            for slot in range(4):
+                arrived(slot).wait_send()
+
     for side in (0, 1):
         @pl.when(sends(side))
         def _():
-            copy_c(lc_in, lch, side, me).wait_send()
             copy_edge(side, me).wait_send()
             for n in (0, 1):
                 copy_u(side, n, me).wait_send()
@@ -635,12 +645,11 @@
     return count.bit_length() - 1
 
 
-def gather_kernel(group, depth, keys, plan, field, out):
+def gather_kernel(group, depth, dipoles, keys, cells, field, out):
     me = lax.axis_index("slab")
     out[...] = jnp.zeros_like(out)
     lines, cols = field.shape
     nx = lines // depth
-    dipoles = plan.shape[1]
     entries = 2 * dipoles
     lane = lane_iota((1, cols))
     short = lane_iota((1, 128))
@@ -650,14 +659,14 @@
 
     def body(g, carry):
         parts = []
+        least = start + g * group
+        j = jnp.minimum(least, entries - group)
         for e in range(group):
-            j = start + g * group + e
-            key = keys[jnp.minimum(j, entries - 1)]
+            key, cell = keys[j + e], cells[j + e]
             o = key & (entries - 1)
             k = o & (dipoles - 1)
-            cell = plan[o >> bits(dipoles), k]
             line = ((key >> bits(entries)) << bits(nx)) + (cell >> bits(cols)) - base
-            inside = j < stop
+            inside = jnp.logical_and(j + e >= least, j + e < stop)
             lane_at = jnp.where(inside, cell & (cols - 1), -1)
             picked = jnp.where(lane == lane_at, field[pl.ds(jnp.where(inside, line, 0), 1), :], 0.0)
             value = jnp.sum(picked, axis=1, keepdims=True)
@@ -670,17 +679,18 @@
     lax.fori_loop(0, (stop - start + group - 1) // group, body, 0)
 
 
-def gather(keys, plan, field, depth):
+def gather(keys, cells, field, depth):
     smem = pl.BlockSpec(memory_space=SMEM)
     full = pl.BlockSpec(memory_space=VMEM)
+    dipoles = keys.shape[0] // 2
     return pl.pallas_call(
-        functools.partial(gather_kernel, 8, depth),
+        functools.partial(gather_kernel, 8, depth, dipoles),
         name="gather",
-        out_shape=jax.ShapeDtypeStruct((plan.shape[1] // 128, 128), F32),
+        out_shape=jax.ShapeDtypeStruct((dipoles // 128, 128), F32),
         in_specs=[smem, smem, full],
         out_specs=full,
         compiler_params=pltpu.CompilerParams(vmem_limit_bytes=8 << 20),
-    )(keys, plan, field)
+    )(keys, cells, field)
 
 
 def share_kernel(slabs, part, out, s_x, r_x, *sums):
@@ -717,18 +727,18 @@
     )(part)
 
 
-def scatter_kernel(group, depth, nx, lines, keys, plan, data, *outs):
+def scatter_kernel(group, depth, nx, lines, keys, cells, data, *outs):
     me = lax.axis_index("slab")
     side_x = lax.axis_index("src") // 2
     total, cols = outs[0].shape
     planes = total // lines
-    dipoles = plan.shape[1]
-    entries = 2 * dipoles
+    entries = keys.shape[0]
     lane = lane_iota((1, cols))
     low = me * depth - WIDE
     start = search(keys, low * entries)
     stop = search(keys, (low + planes) * entries)
     row_base = (nx // 2) * side_x - 2 * PAD
+    plane_base = low * lines + row_base
 
     def clear(q, carry):
         for out in outs:
@@ -739,16 +749,17 @@
 
     def body(g, carry):
         parts = []
+        least = start + g * group
+        j = jnp.minimum(least, entries - group)
         for e in range(group):
-            j = start + g * group + e
-            key = keys[jnp.minimum(j, entries - 1)]
+            key, cell = keys[j + e], cells[j + e]
             o = key & (entries - 1)
-            cell = plan[o >> bits(dipoles), o & (dipoles - 1)]
-            line = (cell >> bits(cols)) - row_base
-            inside = jnp.logical_and(j < stop, jnp.logical_and(line >= PAD, line < lines - PAD))
+            row = cell >> bits(cols)
+            inside = jnp.logical_and(j + e >= least, j + e < stop)
+            inside = jnp.logical_and(inside, jnp.logical_and(row >= row_base + PAD, row < row_base + lines - PAD))
             hit = lane == jnp.where(inside, cell & (cols - 1), -1)
-            at = jnp.where(inside, ((key >> bits(entries)) - low) * lines + line, 0)
-            parts.append((at, [jnp.where(hit, data[n, o >> 7, o & 127], 0.0) for n in (0, 1)]))
+            at = jnp.where(inside, (key >> bits(entries)) * lines + row - plane_base, 0)
+            parts.append((at, [jnp.where(hit, data[o + n * entries], 0.0) for n in (0, 1)]))
         for at, values in parts:
             for out, value in zip(outs, values):
                 out[pl.ds(at, 1), :] = out[pl.ds(at, 1), :] + value
@@ -757,7 +768,7 @@
     lax.fori_loop(0, (stop - start + group - 1) // group, body, 0)
 
 
-def scatter(keys, plan, data, depth, nx, cols):
+def scatter(keys, cells, data, depth, nx, cols):
     smem = pl.BlockSpec(memory_space=SMEM)
     full = pl.BlockSpec(memory_space=VMEM)
     lines = nx // 2 + 4 * PAD
@@ -769,7 +780,7 @@
         in_specs=[smem, smem, smem],
         out_specs=[full, full],
         compiler_params=pltpu.CompilerParams(vmem_limit_bytes=8 << 20),
-    )(keys, plan, data)
+    )(keys, cells, data.reshape(-1))
     return [ref.reshape(planes, lines, cols) for ref in back]
 
 
@@ -834,22 +845,23 @@
     arrives = (me > 0, me < slabs - 1)
     sends = (me < slabs - 1, me > 0)
     to_slab = (me + 1, me - 1)
-    mine = (pl.ds(2 - 2 * core, 2), pl.ds(2 * core, 2))
-    other = (pl.ds(2 * core, 2), pl.ds(2 - 2 * core, 2))
+    part = -(-frame_rows // (2 * PAD)) * PAD
+    fetched = pl.ds(pl.multiple_of((frame_rows - part) * core, PAD), part)
+    given = pl.ds(pl.multiple_of(part * core, PAD), frame_rows - part)
+    taken = pl.ds(pl.multiple_of(part * (1 - core), PAD), frame_rows - part)
 
     def copy_far(side, to):
-        planes = pl.ds(depth - 3 - 2 * core, 2) if side == 0 else pl.ds(1 + 2 * core, 2)
-        return remote(lc_half.at[planes], far.at[side, mine[side]], s_far.at[side], r_far.at[side], (src, to))
-
-    def share_far(side, planes):
-        ref = far.at[side, planes]
+        planes = pl.ds(depth - WIDE if side == 0 else 1, WIDE - 1)
+        return remote(lc_half.at[planes, fetched], far.at[side, :, fetched], s_far.at[side], r_far.at[side], (src, to))
+
+    def share_far(side, rows):
+        ref = far.at[side, :, rows]
         return remote(ref, ref, s_c2.at[side], r_c2.at[side], (mate, me))
 
     copy_rest = remote(u_rest, u2.at[side_x, late, frame_theirs], s_u, r_u, (across, me))
     pl.semaphore_wait(barrier, count)
     for side in (0, 1):
         pl.when(sends[side])(lambda side=side: copy_far(side, to_slab[side]).start())
-    copy_rest.start()
 
     first, last = WIDE - me * depth, WIDE + (slabs - me) * depth - 1
     low_open, high_open = side_x.astype(F32), 1.0 - side_x.astype(F32)
@@ -902,20 +914,21 @@
         @pl.when(arrives[side])
         def _():
             copy_far(side, me).wait_recv()
-            share_far(side, mine[side]).start()
+            share_far(side, given).start()
 
         @pl.when(jnp.logical_not(arrives[side]))
         def _():
             far[side] = jnp.zeros(far.shape[1:], F32)
 
+    copy_rest.start()
     for k in (1, 2):
         run(k, WIDE + k, top - k, True)
     for side in (0, 1):
-        pl.when(arrives[side])(lambda side=side: share_far(side, other[side]).wait_recv())
-    conductivity(far.at[0], WIDE, -1, low_in)
-    conductivity(far.at[1], WIDE, top + 1, high_in)
-    coefs(0, WIDE, False)
-    coefs(top, wide)
+        pl.when(arrives[side])(lambda side=side: share_far(side, taken).wait_recv())
+    conductivity(far.at[0], WIDE - 1, 0, low_in)
+    conductivity(far.at[1], WIDE - 1, top + 1, high_in)
+    coefs(1, WIDE, False)
+    coefs(top, wide - 1)
     for k in range(3):
         run(k, k + 1, WIDE, False)
         if k:
@@ -953,7 +966,7 @@
     copy_rest.wait()
     for side in (0, 1):
         pl.when(sends[side])(lambda side=side: copy_far(side, me).wait_send())
-        pl.when(arrives[side])(lambda side=side: share_far(side, mine[side]).wait_send())
+        pl.when(arrives[side])(lambda side=side: share_far(side, given).wait_send())
 
     def partial(q, dst, slot):
         for r, rows in owned:
@@ -1052,7 +1065,7 @@
             VMEM((2, depth + 2, frame, cols), F32),
         ]
         + [VMEM((quarter, half, cols), F32)] * 3
-        + [VMEM((2, WIDE, half + PAD, cols), F32)]
+        + [VMEM((2, WIDE - 1, half + PAD, cols), F32)]
         + [DMA((2,)), DMA(()), DMA(())]
         + pair * 2
         + [DMA((quarter,))] * 8
@@ -1068,14 +1081,15 @@
     dipoles = rec_depth.shape[1]
     order = lax.broadcasted_iota(jnp.int32, rec_depth.shape, 0) * dipoles
     order = order + lax.broadcasted_iota(jnp.int32, rec_depth.shape, 1)
-    keys = lax.sort((rec_depth * (2 * dipoles) + order).reshape(-1), is_stable=False)
+    keys = (rec_depth * (2 * dipoles) + order).reshape(-1)
+    keys, cells = lax.sort((keys, rec_plan.reshape(-1)), num_keys=1, is_stable=False)
     arguments = (pltpu.with_memory_space_constraint(a, pltpu.HBM) for a in (log_cond, perturb, potentials[0]))
     tangent, mean, lc_half, lc_near, u_mine, u_first, u_rest = first_solve(slabs, *arguments)
-    part = gather(keys, rec_plan, tangent.reshape(depth * nx, cols), depth)
+    part = gather(keys, cells, tangent.reshape(depth * nx, cols), depth)
     data = share(slabs, part)
     u_first, data = lax.optimization_barrier((u_first, data))
     u_first = lax.ppermute(u_first, "src", [(i, (i + 2) % 4) for i in range(4)])
-    back = scatter(keys, rec_plan, data, depth, nx, cols)
+    back = scatter(keys, cells, data, depth, nx, cols)
     return second_solve(slabs, nx, lc_half, lc_near, u_mine, u_first, u_rest, mean, back)
 
 

time: 180 us -> 172 us (0.956)
  Pallas kernels: 171 us -> 161 us
    pallas_call x1, Pallas kernels: 67.8 us -> 58.4 us  [second_solve(): pl.pallas_call(functools.partial(second_kernel, slabs, nx), name='second_...]
    pallas_call x1, Pallas kernels: 70.7 us -> 75.5 us  [first_solve(): pl.pallas_call(functools.partial(first_kernel, slabs), name='first_solve'...]
    pallas_call x1, Pallas kernels: 15.8 us -> 13.4 us  [share(): pl.pallas_call(functools.partial(share_kernel, slabs), name='share_data',...]
    pallas_call x1, Pallas kernels: 9.87 us -> 7.71 us  [scatter(): pl.pallas_call(functools.partial(scatter_kernel, 8, depth, nx, lines), na...]
  transfers between devices with their start and end apart: 1 -> 1, of which waited for: 0 -> 0; matrix products, arithmetic and copies ran while one was open for 0% -> 0% of each run, Pallas kernels for 5% -> 4%
where the time goes in v3:
time: 172 us
  Pallas kernels  161 us (94%)
  other arithmetic  6.52 us (4%)
  local copies, waits for them, and re-layouts  2.09 us (1%)
  starting transfers between devices  2 us (1%)
    pallas_call x1, Pallas kernels, first_solve(): pl.pallas_call(functools.partial(first_kernel, slabs), name='first_solve'...  75.5 us
    pallas_call x1, Pallas kernels, second_solve(): pl.pallas_call(functools.partial(second_kernel, slabs, nx), name='second_...  58.4 us
    pallas_call x1, Pallas kernels, share(): pl.pallas_call(functools.partial(share_kernel, slabs), name='share_data',...  13.4 us
    pallas_call x1, Pallas kernels, scatter(): pl.pallas_call(functools.partial(scatter_kernel, 8, depth, nx, lines), na...  7.71 us
    pallas_call x1, Pallas kernels, gather(): pl.pallas_call(functools.partial(gather_kernel, 8, depth, dipoles), name=...  6.28 us
    sort x1, other arithmetic, shards(): lax.sort((keys, rec_plan.reshape(-1)), num_keys=1, is_stable=False)  5.68 us
  transfers between devices with their start and end apart: 1, of which 0 were waited for; matrix products, arithmetic and copies ran while one was open for 0% of the time, Pallas kernels for 4%

profile of v3, /device:TPU:1, one launch (start us, length us, event | category | flops | bytes accessed | tf_op | source)
XLA Modules:
  0.0 172.0 jit_solution(17875911070695638257)
XLA Ops:
  0.0 0.8 add_bitcast_fusion
  0.9 0.8 copy.7
  1.6 5.7 %sort.15 = (s32[8192]{0:T(1024)S(1)}, s32[8192]{0:T(1024)S(1)}) sort(s32[8192]{0:T(1024)S(1)} %bitcast.15, s32[8192]{0:T(1024)S(1)} %bitcast.16), dimensions={0}, to_apply=%region_0.0 | sort | flops 106496 | bytes 131072 | tf_op jit(solution)/shard_map/sort | solution.py:1085
  7.3 75.5 %first_solve.1 = (f32[8,256,256]{2,1,0:T(8,128)S(1)}, f32[8,128]{1,0:T(8,128)S(1)}, f32[8,136,256]{2,1,0:T(8,128)S(1)}, f32[2,136,256]{2,1,0:T(8,128)S(1)}, f32[...) custom-call(f32[8,256,256]{2,1,0:T(8,128)} %lc_in.1, f32[8,256,256]{2,1,0:T(8,128)} %pt_in.1, ...), custom_call_target="tpu_custom_call" | custom-call | tf_op jit(solution)/shard_map/first_solve/pallas_call | solution.py:594
  82.8 6.3 %gather.1.part = f32[32,128]{1,0:T(8,128)S(1)} custom-call(s32[8192]{0:T(1024)S(1)} %get-tuple-element.22.keys, s32[8192]{0:T(1024)S(1)} %get-tuple-element.23.cells, f32[2048,256]{1,0:T(8,128)S(1)} %bitcast.12), custom_call_target="tpu_custom_call" | custom-call | tf_op jit(solution)/shard_map/gather/pallas_call | solution.py:686
  89.1 13.4 %share_data.1 = f32[2,64,128]{2,1,0:T(8,128)S(1)} custom-call(f32[32,128]{1,0:T(8,128)S(1)} %gather.1.part), custom_call_target="tpu_custom_call" | custom-call | tf_op jit(solution)/shard_map/share_data/pallas_call | solution.py:717
  102.5 2.0 %collective-permute-start = (f32[4,136,256]{2,1,0:T(8,128)S(1)}, f32[4,136,256]{2,1,0:T(8,128)S(1)}, u32[]{:S(2)}, u32[]{:S(2)}) collective-permute-start(f32[4,136,256]{2,1,0:T(8,128)S(1)} %get-tuple-element.25), channel_id=1, source_target_pairs={{0,64},{32,96},{64,0},{96,32},{1,65},{33,97},{65,1},{97,33},{2,66}... | collective-permute-start | bytes 1671176 | tf_op jit(solution)/shard_map/ppermute | solution.py:1091
  104.5 7.7 %scatter.1 = (f32[2560,256]{1,0:T(8,128)S(1)}, f32[2560,256]{1,0:T(8,128)S(1)}) custom-call(s32[8192]{0:T(1024)S(1)} %get-tuple-element.22.keys, s32[8192]{0:T(1024)S(1)} %get-tuple-element.23.cells, f32[16384]{0:T(1024)S(1)} %bitcast.13), custom_call_target="tpu_custom_call" | custom-call | tf_op jit(solution)/shard_map/scatter/pallas_call | solution.py:776
  112.2 0.0 collective-permute-done.u_first
  112.2 58.4 %second_solve.1 = f32[8,256,256]{2,1,0:T(8,128)S(1)} custom-call(f32[8,136,256]{2,1,0:T(8,128)S(1)} %get-tuple-element.18.lc_half, f32[2,136,256]{2,1,0:T(8,128)S(1)} %get-tuple-element.19.lc_near, f32[10,136,256]{2,1,0:T(8,128)S(1)} %get-tuple-element.20.u_mine, f32[4,136,256]{2,1,0:T(8,128)S(1)} %collective-permute-done.u_first, ...), custom_call_target="tpu_custom_call" | custom-call | tf_op jit(solution)/shard_map/second_solve/pallas_call | solution.py:1049
  170.7 1.3 copy.9
  (2 shorter events, 0.0 us)
Async XLA Ops:
  102.5 9.8 %collective-permute-start = (f32[4,136,256]{2,1,0:T(8,128)S(1)}, f32[4,136,256]{2,1,0:T(8,128)S(1)}, u32[]{:S(2)}, u32[]{:S(2)}) collective-permute-start(f32[4,136,256]{2,1,0:T(8,128)S(1)} %get-tuple-element.25), channel_id=1, source_target_pairs={{0,64},{32,96},{64,0},{96,32},{1,65},{33,97},{65,1},{97,33},{2,66}... | collective-permute-start | bytes 1671176 | tf_op jit(solution)/shard_map/ppermute | solution.py:1091

commit v4 on v3

--- a/solution.py
+++ b/solution.py
@@ -29,11 +29,36 @@
 
 
 def next_lane(value):
-    return pltpu.roll(value, value.shape[1] - 1, 1)
+    half = value.shape[1] // 2
+    even, odd = value[:, :half], value[:, half:]
+    return jnp.concatenate([odd, pltpu.roll(even, half - 1, 1)], axis=1)
 
 
 def prev_lane(value):
-    return pltpu.roll(value, 1, 1)
+    half = value.shape[1] // 2
+    even, odd = value[:, :half], value[:, half:]
+    return jnp.concatenate([pltpu.roll(odd, 1, 1), even], axis=1)
+
+
+def lane_of(column, cols):
+    return (column >> 1) + (column & 1) * (cols // 2)
+
+
+def order_matrix(cols, back):
+    row = lax.broadcasted_iota(jnp.int32, (cols, cols), 0)
+    col = lax.broadcasted_iota(jnp.int32, (cols, cols), 1)
+    hit = row == lane_of(col, cols) if back else col == lane_of(row, cols)
+    return jnp.where(hit, 1.0, 0.0).astype(jnp.bfloat16)
+
+
+def reorder(value, matrix):
+    total = None
+    for _ in range(3):
+        piece = value.astype(jnp.bfloat16)
+        value = value - piece.astype(F32)
+        moved = jnp.dot(piece, matrix, preferred_element_type=F32)
+        total = moved if total is None else total + moved
+    return total
 
 
 def chunks(count, start=0):
@@ -245,8 +270,8 @@
 
 def first_kernel(
     slabs, lc_in, pt_in, u, tan, mean_out, lc_half, lc_near, u_mine, u_first, u_rest,
-    lc, pt, lch, uh, sig, wgt, uw, dg, hx, hy, hz, v0, v1, v2, v3, pth, edge, relayed,
-    s_load, s_take, s_first, r_first, s_c, r_c, s_x, r_x, s_core, r_core, s_v, r_v, s_e, r_e, s_out, r_in, *sums,
+    lc, pt, lch, uh, sig, wgt, uw, dg, hx, hy, hz, v0, v1, v2, v3, pth, edge, order,
+    s_load, s_take, s_first, r_first, s_c, r_c, s_x, r_x, s_core, r_core, s_v, r_v, s_e, r_e, *sums,
 ):
     src = lax.axis_index("src")
     me = lax.axis_index("slab")
@@ -265,7 +290,19 @@
     for load in loads:
         load.start()
     ring = [(src, lax.rem(me + 1, slabs)), (src, lax.rem(me + slabs - 1, slabs))]
-    barrier, count = signal_all(src, me, slabs, ring + [(mate, me)] + [(across, t) for t in (me, ring[0][1], ring[1][1])])
+    barrier, count = signal_all(src, me, slabs, ring + [(mate, me), (across, me)])
+    order[...] = order_matrix(cols, False)
+
+    def shuffle(q, carry):
+        for n in (0, 1):
+            for ref, plane, first in ((lc, q, 0), (pt, q, 0), (uw, q + 1, PAD)):
+                rows = pl.ds(first + n * half, half)
+                ref[plane, rows, :] = reorder(ref[plane, rows, :], order[...])
+        return carry
+
+    for load in loads:
+        load.wait()
+    lax.fori_loop(0, 2, lambda i, c: shuffle(i * (depth - 1), c), 0)
     pl.semaphore_wait(barrier, count)
     mean_sum = Sum(src, me, slabs, sum_levels(sums[0:6]))
     mom_sum = Sum(src, me, slabs, sum_levels(sums[6:12]))
@@ -285,45 +322,11 @@
     def part(n):
         return pl.ds(n * half, half)
 
-    def copy_u(side, n, to, slot=None, onward=False):
-        return routed(
-            u.at[near(side), part(n)], uh.at[side, part(n)],
-            s_first.at[side, n], r_first.at[side, n], to, slot, onward,
+    def copy_u(side, n, to):
+        return remote(
+            uw.at[1 + near(side), pl.ds(PAD + n * half, half)], uh.at[side, part(n)],
+            s_first.at[side, n], r_first.at[side, n], (src, to),
         )
-
-    low_mid = slabs // 2 - 1
-
-    def by_relay(side):
-        return jnp.logical_and(me == low_mid + side, side_x == 1 - side)
-
-    def is_relay(side):
-        return jnp.logical_and(me == low_mid + side, side_x == side)
-
-    def send(n, side, copy, slot):
-        if n == 1:
-            pl.when(sends(side))(lambda: copy(side, n, below(side)).start())
-            return
-        pl.when(jnp.logical_and(sends(side), jnp.logical_not(by_relay(side))))(
-            lambda: copy(side, n, below(side)).start()
-        )
-        pl.when(by_relay(side))(lambda: copy(side, n, me, slot).start())
-
-    def arrived(slot):
-        return remote(relayed.at[slot], relayed.at[slot], s_out.at[slot], r_in.at[slot], (across, me))
-
-    def relay(copy, slot):
-        for side in (0, 1):
-            @pl.when(is_relay(side))
-            def _():
-                arrived(slot).wait_recv()
-                copy(side, 0, below(side), slot, True).start()
-
-    def routed(ref, dst, send_sem, recv_sem, to, slot, onward):
-        if slot is None:
-            return remote(ref, dst, send_sem, recv_sem, (src, to))
-        if onward:
-            return remote(relayed.at[slot], dst, s_out.at[slot], recv_sem, (across, to))
-        return remote(ref, relayed.at[slot], send_sem, r_in.at[slot], (across, me))
 
     my_rows = pl.ds(pl.multiple_of(half * side_x, PAD), half)
     their_rows = pl.ds(pl.multiple_of(half * (1 - side_x), PAD), half)
@@ -340,8 +343,8 @@
         return remote(ref.at[side], ref.at[side], s_core.at[side], r_core.at[side], (mate, me))
 
     def by_core(body):
-        pl.when(core == 0)(lambda: body(lc_in, lch))
-        pl.when(core == 1)(lambda: body(pt_in, pth))
+        pl.when(core == 0)(lambda: body(lc, lch))
+        pl.when(core == 1)(lambda: body(pt, pth))
 
     for side in (0, 1):
         @pl.when(sends(side))
@@ -350,17 +353,14 @@
 
     for ref in (sig, wgt, uw, hy, v0, v1, v2, v3):
         zero_pads(ref, nx)
-    for load in loads:
-        load.wait()
-
     for side in (0, 1):
         @pl.when(sends(side))
         def _():
-            copy_c(lc_in, lch, side, me).wait_send()
+            copy_c(lc, lch, side, me).wait_send()
 
     for n in (0, 1):
         for side in (0, 1):
-            send(n, side, copy_u, 0)
+            pl.when(sends(side))(lambda side=side, n=n: copy_u(side, n, below(side)).start())
 
     def own(q, acc):
         for r, rows in chunks(nx):
@@ -370,6 +370,7 @@
             acc = acc + fold(value)
         return acc
 
+    lax.fori_loop(1, depth - 1, shuffle, 0)
     acc = lax.fori_loop(0, depth, own, jnp.zeros((8, cols), F32))
     mean_sum.start(pack_row([acc]))
 
@@ -393,7 +394,6 @@
                 swap(dst, side, my_rows).start()
 
             by_core(body)
-    relay(copy_u, 0)
     for side in (0, 1):
         @pl.when(arrives(side))
         def _():
@@ -418,17 +418,21 @@
                 total = total + (c + cj) * (f - fj)
             v0[q + 1, pl.ds(PAD + r, rows), :] = -0.5 * total
 
-    def copy_v(k, side, n, to, slot=None, onward=False):
+    def copy_v(k, side, n, to):
         plane = depth if side == 0 else 1
         halo = 0 if side == 0 else depth + 1
         rows = pl.ds(PAD + n * half, half)
         ref = fields[k]
-        return routed(
-            ref.at[plane, rows], ref.at[halo, rows], s_v.at[k, side, n], r_v.at[k, side, n], to, slot, onward
+        return remote(
+            ref.at[plane, rows], ref.at[halo, rows], s_v.at[k, side, n], r_v.at[k, side, n], (src, to)
         )
 
     def send_edge(k, side, n):
-        send(n, 1 - side, functools.partial(copy_v, k), k + 1)
+        out = 1 - side
+
+        @pl.when(sends(out))
+        def _():
+            copy_v(k, out, n, below(out)).start()
 
     for n in (0, 1):
         for side in (0, 1):
@@ -507,7 +511,6 @@
             return tuple(accs)
 
         accs = inner(step, (zero,) * (3 if k == 0 else k + 2))
-        relay(functools.partial(copy_v, k), k + 1)
         for n in (0, 1):
             for side in (0, 1):
                 pl.when(arrives(side))(lambda side=side, n=n, k=k: copy_v(k, side, n, me).wait_recv())
@@ -562,12 +565,6 @@
 
     for take in takes:
         take.wait()
-    for side in (0, 1):
-        @pl.when(is_relay(side))
-        def _():
-            for slot in range(4):
-                arrived(slot).wait_send()
-
     for side in (0, 1):
         @pl.when(sends(side))
         def _():
@@ -614,9 +611,9 @@
             VMEM((depth + 1, nx, cols), F32),
         ]
         + [VMEM((depth + 2, *plane), F32)] * 4
-        + [VMEM((2, nx, cols), F32), VMEM((2, half, cols), F32), VMEM((4, half, cols), F32)]
+        + [VMEM((2, nx, cols), F32), VMEM((2, half, cols), F32), VMEM((cols, cols), jnp.bfloat16)]
         + [DMA((3,)), DMA((5,)), DMA((2, 2)), DMA((2, 2)), *pair, *pair, *pair]
-        + [DMA((3, 2, 2)), DMA((3, 2, 2)), *pair, DMA((4,)), DMA((4,))]
+        + [DMA((3, 2, 2)), DMA((3, 2, 2)), *pair]
         + sum_scratch(slabs, (1, 128)) * 2,
         compiler_params=pltpu.CompilerParams(
             collective_id=0, has_side_effects=True, vmem_limit_bytes=43 << 20
@@ -667,7 +664,7 @@
             k = o & (dipoles - 1)
             line = ((key >> bits(entries)) << bits(nx)) + (cell >> bits(cols)) - base
             inside = jnp.logical_and(j + e >= least, j + e < stop)
-            lane_at = jnp.where(inside, cell & (cols - 1), -1)
+            lane_at = jnp.where(inside, lane_of(cell & (cols - 1), cols), -1)
             picked = jnp.where(lane == lane_at, field[pl.ds(jnp.where(inside, line, 0), 1), :], 0.0)
             value = jnp.sum(picked, axis=1, keepdims=True)
             value = jnp.where(o < dipoles, value, -value)
@@ -757,7 +754,7 @@
             row = cell >> bits(cols)
             inside = jnp.logical_and(j + e >= least, j + e < stop)
             inside = jnp.logical_and(inside, jnp.logical_and(row >= row_base + PAD, row < row_base + lines - PAD))
-            hit = lane == jnp.where(inside, cell & (cols - 1), -1)
+            hit = lane == jnp.where(inside, lane_of(cell & (cols - 1), cols), -1)
             at = jnp.where(inside, (key >> bits(entries)) * lines + row - plane_base, 0)
             parts.append((at, [jnp.where(hit, data[o + n * entries], 0.0) for n in (0, 1)]))
         for at, values in parts:
@@ -786,7 +783,7 @@
 
 def second_kernel(
     slabs, nx, lc_half, lc_near, u_mine, u_first, u_rest, mean_in, v00, v01, out,
-    sig, dg, hx, hy, hz, v1, v2, v3, u2, adj, give, take, pair, far,
+    sig, dg, hx, hy, hz, v1, v2, v3, u2, adj, give, take, pair, far, order,
     s_load, s_u, r_u, s_far, r_far, s_c2, r_c2, s_give, r_give, s_x, r_x, s_own, r_own, s_fwd, r_fwd,
     *sums,
 ):
@@ -803,6 +800,7 @@
     ring = [(src, lax.rem(me + 1, slabs)), (src, lax.rem(me + slabs - 1, slabs))]
     barrier, count = signal_all(src, me, slabs, ring + [(mate, me)] + [(across, t) for t in pair_group(me)])
     total = Sum(src, me, slabs, sum_levels(sums), across)
+    order[...] = order_matrix(cols, True)
     owned = chunks(half, PAD)
     rims = [(0, PAD), (PAD + half, PAD)]
     every = rims[:1] + owned + rims[1:]
@@ -1012,9 +1010,10 @@
     def keeping(n, carry):
         partial(core * quarter + n, pair, n)
         copy_give(n).wait_recv()
-        for r, rows in chunks(half):
+        for r, rows in ((0, half),):
             at = pl.multiple_of(half * side_x + r, PAD)
-            out[core * quarter + n, pl.ds(at, rows), :] = pair[n, pl.ds(r, rows), :] + take[n, pl.ds(r, rows), :]
+            value = pair[n, pl.ds(r, rows), :] + take[n, pl.ds(r, rows), :]
+            out[core * quarter + n, pl.ds(at, rows), :] = reorder(value, order[...])
         copy_x(n).start()
         copy_own(n).start()
         return carry
@@ -1065,7 +1064,7 @@
             VMEM((2, depth + 2, frame, cols), F32),
         ]
         + [VMEM((quarter, half, cols), F32)] * 3
-        + [VMEM((2, WIDE - 1, half + PAD, cols), F32)]
+        + [VMEM((2, WIDE - 1, half + PAD, cols), F32), VMEM((cols, cols), jnp.bfloat16)]
         + [DMA((2,)), DMA(()), DMA(())]
         + pair * 2
         + [DMA((quarter,))] * 8

time: 172 us -> 159 us (0.924)
  Pallas kernels: 161 us -> 149 us
  starting transfers between devices: 2 us -> 0.09 us
    pallas_call x1, Pallas kernels: 75.5 us -> 64.7 us  [first_solve(): pl.pallas_call(functools.partial(first_kernel, slabs), name='first_solve'...]
    ppermute x1, starting transfers between devices: 2 us -> 0.09 us  [shards(): u_first = lax.ppermute(u_first, 'src', [(i, (i + 2) % 4) for i in range(4)])]
  transfers between devices with their start and end apart: 1 -> 1, of which waited for: 0 -> 1; matrix products, arithmetic and copies ran while one was open for 0% -> 0% of each run, Pallas kernels for 4% -> 5%
where the time goes in v4:
time: 159 us
  Pallas kernels  149 us (94%)
  other arithmetic  6.52 us (4%)
  local copies, waits for them, and re-layouts  2.09 us (1%)
    pallas_call x1, Pallas kernels, first_solve(): pl.pallas_call(functools.partial(first_kernel, slabs), name='first_solve'...  64.7 us
    pallas_call x1, Pallas kernels, second_solve(): pl.pallas_call(functools.partial(second_kernel, slabs, nx), name='second_...  57.1 us
    pallas_call x1, Pallas kernels, share(): pl.pallas_call(functools.partial(share_kernel, slabs), name='share_data',...  12.8 us
    pallas_call x1, Pallas kernels, scatter(): pl.pallas_call(functools.partial(scatter_kernel, 8, depth, nx, lines), na...  8.26 us
    pallas_call x1, Pallas kernels, gather(): pl.pallas_call(functools.partial(gather_kernel, 8, depth, dipoles), name=...  6.33 us
    sort x1, other arithmetic, shards(): lax.sort((keys, rec_plan.reshape(-1)), num_keys=1, is_stable=False)  5.68 us
  transfers between devices with their start and end apart: 1, of which 1 were waited for; matrix products, arithmetic and copies ran while one was open for 0% of the time, Pallas kernels for 5%

profile of v4, /device:TPU:1, one launch (start us, length us, event | category | flops | bytes accessed | tf_op | source)
XLA Modules:
  0.0 158.8 jit_solution(15468724139427706996)
XLA Ops:
  0.0 0.8 add_bitcast_fusion
  0.9 0.8 copy.7
  1.6 5.7 %sort.15 = (s32[8192]{0:T(1024)S(1)}, s32[8192]{0:T(1024)S(1)}) sort(s32[8192]{0:T(1024)S(1)} %bitcast.15, s32[8192]{0:T(1024)S(1)} %bitcast.16), dimensions={0}, to_apply=%region_0.0 | sort | flops 106496 | bytes 131072 | tf_op jit(solution)/shard_map/sort | solution.py:1084
  7.3 64.7 %first_solve.1 = (f32[8,256,256]{2,1,0:T(8,128)S(1)}, f32[8,128]{1,0:T(8,128)S(1)}, f32[8,136,256]{2,1,0:T(8,128)S(1)}, f32[2,136,256]{2,1,0:T(8,128)S(1)}, f32[...) custom-call(f32[8,256,256]{2,1,0:T(8,128)} %lc_in.1, f32[8,256,256]{2,1,0:T(8,128)} %pt_in.1, ...), custom_call_target="tpu_custom_call" | custom-call | tf_op jit(solution)/shard_map/first_solve/pallas_call | solution.py:591
  72.0 6.3 %gather.1.part = f32[32,128]{1,0:T(8,128)S(1)} custom-call(s32[8192]{0:T(1024)S(1)} %get-tuple-element.22.keys, s32[8192]{0:T(1024)S(1)} %get-tuple-element.23.cells, f32[2048,256]{1,0:T(8,128)S(1)} %bitcast.12), custom_call_target="tpu_custom_call" | custom-call | tf_op jit(solution)/shard_map/gather/pallas_call | solution.py:683
  78.4 12.8 %share_data.1 = f32[2,64,128]{2,1,0:T(8,128)S(1)} custom-call(f32[32,128]{1,0:T(8,128)S(1)} %gather.1.part), custom_call_target="tpu_custom_call" | custom-call | tf_op jit(solution)/shard_map/share_data/pallas_call | solution.py:714
  91.2 0.1 collective-permute-start
  91.3 8.3 %scatter.1 = (f32[2560,256]{1,0:T(8,128)S(1)}, f32[2560,256]{1,0:T(8,128)S(1)}) custom-call(s32[8192]{0:T(1024)S(1)} %get-tuple-element.22.keys, s32[8192]{0:T(1024)S(1)} %get-tuple-element.23.cells, f32[16384]{0:T(1024)S(1)} %bitcast.13), custom_call_target="tpu_custom_call" | custom-call | tf_op jit(solution)/shard_map/scatter/pallas_call | solution.py:773
  99.6 0.9 collective-permute-done.u_first
  100.4 57.1 %second_solve.1 = f32[8,256,256]{2,1,0:T(8,128)S(1)} custom-call(f32[8,136,256]{2,1,0:T(8,128)S(1)} %get-tuple-element.18.lc_half, f32[2,136,256]{2,1,0:T(8,128)S(1)} %get-tuple-element.19.lc_near, f32[10,136,256]{2,1,0:T(8,128)S(1)} %get-tuple-element.20.u_mine, f32[4,136,256]{2,1,0:T(8,128)S(1)} %collective-permute-done.u_first, ...), custom_call_target="tpu_custom_call" | custom-call | tf_op jit(solution)/shard_map/second_solve/pallas_call | solution.py:1048
  157.5 1.3 copy.9
  (2 shorter events, 0.0 us)
Async XLA Ops:
  91.2 9.2 %collective-permute-start = (f32[4,136,256]{2,1,0:T(8,128)S(1)}, f32[4,136,256]{2,1,0:T(8,128)S(1)}, u32[]{:S(2)}, u32[]{:S(2)}) collective-permute-start(f32[4,136,256]{2,1,0:T(8,128)S(1)} %get-tuple-element.25), channel_id=1, source_target_pairs={{0,64},{32,96},{64,0},{96,32},{1,65},{33,97},{65,1},{97,33},{2,66}... | collective-permute-start | bytes 1671176 | tf_op jit(solution)/shard_map/ppermute | solution.py:1090

commit v5 on v4

--- a/solution.py
+++ b/solution.py
@@ -621,20 +621,37 @@
     )(lc, pt, u)
 
 
-def search(keys, bound):
-    size = keys.shape[0]
-
-    def body(_, ends):
-        low, high = ends
-        mid = (low + high) // 2
-        less = keys[jnp.minimum(mid, size - 1)] < bound
-        open_ = low < high
-        return (
-            jnp.where(jnp.logical_and(open_, less), mid + 1, low),
-            jnp.where(jnp.logical_and(open_, jnp.logical_not(less)), mid, high),
-        )
-
-    return lax.fori_loop(0, size.bit_length(), body, (jnp.int32(0), jnp.int32(size)))[0]
+def over_window(group, ordered, first_key, last_key, keys, cells, keys_s, cells_s, sems, body):
+    start, stop = (
+        jnp.sum(jnp.where(ordered[...] < bound, 1.0, 0.0)).astype(jnp.int32) for bound in (first_key, last_key)
+    )
+    size = keys_s.shape[0]
+
+    def piece(w, carry):
+        base = pl.multiple_of(w * size, size)
+        copies = [
+            pltpu.make_async_copy(ref.at[pl.ds(base, size)], dst, sems.at[n])
+            for n, (ref, dst) in enumerate(((keys, keys_s), (cells, cells_s)))
+        ]
+        for copy in copies:
+            copy.start()
+        for copy in copies:
+            copy.wait()
+        low = jnp.maximum(start - base, 0)
+        high = jnp.minimum(stop - base, size)
+
+        def step(g, carry):
+            body(low + g * group, high)
+            return carry
+
+        return lax.fori_loop(0, (high - low + group - 1) // group, step, carry)
+
+    lax.fori_loop(start // size, (stop + size - 1) // size, piece, 0)
+
+
+def window_scratch(entries):
+    size = min(1024, entries)
+    return [SMEM((size,), jnp.int32), SMEM((size,), jnp.int32), DMA((2,))]
 
 
 def bits(count):
@@ -642,7 +659,7 @@
     return count.bit_length() - 1
 
 
-def gather_kernel(group, depth, dipoles, keys, cells, field, out):
+def gather_kernel(group, depth, dipoles, ordered, keys, cells, field, out, keys_s, cells_s, sems):
     me = lax.axis_index("slab")
     out[...] = jnp.zeros_like(out)
     lines, cols = field.shape
@@ -650,16 +667,13 @@
     entries = 2 * dipoles
     lane = lane_iota((1, cols))
     short = lane_iota((1, 128))
-    start = search(keys, me * depth * entries)
-    stop = search(keys, (me + 1) * depth * entries)
     base = me * lines
 
-    def body(g, carry):
+    def body(least, stop):
         parts = []
-        least = start + g * group
-        j = jnp.minimum(least, entries - group)
+        j = jnp.minimum(least, keys_s.shape[0] - group)
         for e in range(group):
-            key, cell = keys[j + e], cells[j + e]
+            key, cell = keys_s[j + e], cells_s[j + e]
             o = key & (entries - 1)
             k = o & (dipoles - 1)
             line = ((key >> bits(entries)) << bits(nx)) + (cell >> bits(cols)) - base
@@ -671,23 +685,24 @@
             parts.append((k >> 7, jnp.where(short == (k & 127), value, 0.0)))
         for line, value in parts:
             out[pl.ds(line, 1), :] = out[pl.ds(line, 1), :] + value
-        return carry
-
-    lax.fori_loop(0, (stop - start + group - 1) // group, body, 0)
+
+    first = me * depth * entries
+    over_window(group, ordered, first, first + depth * entries, keys, cells, keys_s, cells_s, sems, body)
 
 
 def gather(keys, cells, field, depth):
-    smem = pl.BlockSpec(memory_space=SMEM)
+    anywhere = pl.BlockSpec(memory_space=pl.ANY)
     full = pl.BlockSpec(memory_space=VMEM)
-    dipoles = keys.shape[0] // 2
+    entries = keys.shape[0]
     return pl.pallas_call(
-        functools.partial(gather_kernel, 8, depth, dipoles),
+        functools.partial(gather_kernel, 16, depth, entries // 2),
         name="gather",
-        out_shape=jax.ShapeDtypeStruct((dipoles // 128, 128), F32),
-        in_specs=[smem, smem, full],
+        out_shape=jax.ShapeDtypeStruct((entries // 256, 128), F32),
+        in_specs=[full, anywhere, anywhere, full],
         out_specs=full,
+        scratch_shapes=window_scratch(entries),
         compiler_params=pltpu.CompilerParams(vmem_limit_bytes=8 << 20),
-    )(keys, cells, field)
+    )(keys.reshape(-1, 128), keys, cells, field)
 
 
 def share_kernel(slabs, part, out, s_x, r_x, *sums):
@@ -698,10 +713,7 @@
     barrier, count = signal_all(src, me, slabs, [(across, me)])
     pl.semaphore_wait(barrier, count)
     total = Sum(src, me, slabs, sum_levels(sums))
-    value = total.whole(part[...])
-    lines = value.shape[0]
-    out[side_x, pl.ds(0, lines), :] = value
-    out[side_x, pl.ds(lines, lines), :] = -value
+    out[side_x] = total.whole(part[...])
     copy = remote(out.at[side_x], out.at[side_x], s_x, r_x, (across, me))
     copy.start()
     copy.wait()
@@ -710,11 +722,10 @@
 
 def share(slabs, part):
     full = pl.BlockSpec(memory_space=VMEM)
-    lines = part.shape[0]
     return pl.pallas_call(
         functools.partial(share_kernel, slabs),
         name="share_data",
-        out_shape=jax.ShapeDtypeStruct((2, 2 * lines, 128), F32),
+        out_shape=jax.ShapeDtypeStruct((2, *part.shape), F32),
         in_specs=[full],
         out_specs=full,
         scratch_shapes=[DMA(()), DMA(())] + sum_scratch(slabs, part.shape),
@@ -724,16 +735,16 @@
     )(part)
 
 
-def scatter_kernel(group, depth, nx, lines, keys, cells, data, *outs):
+def scatter_kernel(group, depth, nx, lines, ordered, keys, cells, data, out0, out1, keys_s, cells_s, sems):
     me = lax.axis_index("slab")
     side_x = lax.axis_index("src") // 2
-    total, cols = outs[0].shape
+    outs = (out0, out1)
+    total, cols = out0.shape
     planes = total // lines
     entries = keys.shape[0]
+    dipoles = entries // 2
     lane = lane_iota((1, cols))
     low = me * depth - WIDE
-    start = search(keys, low * entries)
-    stop = search(keys, (low + planes) * entries)
     row_base = (nx // 2) * side_x - 2 * PAD
     plane_base = low * lines + row_base
 
@@ -744,29 +755,32 @@
 
     lax.fori_loop(0, planes, clear, 0)
 
-    def body(g, carry):
+    def body(least, stop):
         parts = []
-        least = start + g * group
-        j = jnp.minimum(least, entries - group)
+        j = jnp.minimum(least, keys_s.shape[0] - group)
         for e in range(group):
-            key, cell = keys[j + e], cells[j + e]
+            key, cell = keys_s[j + e], cells_s[j + e]
             o = key & (entries - 1)
+            k = o & (dipoles - 1)
             row = cell >> bits(cols)
             inside = jnp.logical_and(j + e >= least, j + e < stop)
             inside = jnp.logical_and(inside, jnp.logical_and(row >= row_base + PAD, row < row_base + lines - PAD))
             hit = lane == jnp.where(inside, lane_of(cell & (cols - 1), cols), -1)
             at = jnp.where(inside, (key >> bits(entries)) * lines + row - plane_base, 0)
-            parts.append((at, [jnp.where(hit, data[o + n * entries], 0.0) for n in (0, 1)]))
+            sign = jnp.where(o < dipoles, 1.0, -1.0)
+            parts.append((at, [jnp.where(hit, data[k + n * dipoles] * sign, 0.0) for n in (0, 1)]))
         for at, values in parts:
             for out, value in zip(outs, values):
                 out[pl.ds(at, 1), :] = out[pl.ds(at, 1), :] + value
-        return carry
-
-    lax.fori_loop(0, (stop - start + group - 1) // group, body, 0)
+
+    over_window(
+        group, ordered, low * entries, (low + planes) * entries, keys, cells, keys_s, cells_s, sems, body
+    )
 
 
 def scatter(keys, cells, data, depth, nx, cols):
     smem = pl.BlockSpec(memory_space=SMEM)
+    anywhere = pl.BlockSpec(memory_space=pl.ANY)
     full = pl.BlockSpec(memory_space=VMEM)
     lines = nx // 2 + 4 * PAD
     planes = depth + 2 * WIDE
@@ -774,10 +788,11 @@
         functools.partial(scatter_kernel, 8, depth, nx, lines),
         name="scatter",
         out_shape=[jax.ShapeDtypeStruct((planes * lines, cols), F32)] * 2,
-        in_specs=[smem, smem, smem],
+        in_specs=[full, anywhere, anywhere, smem],
         out_specs=[full, full],
+        scratch_shapes=window_scratch(keys.shape[0]),
         compiler_params=pltpu.CompilerParams(vmem_limit_bytes=8 << 20),
-    )(keys, cells, data.reshape(-1))
+    )(keys.reshape(-1, 128), keys, cells, data.reshape(-1))
     return [ref.reshape(planes, lines, cols) for ref in back]
 
 
@@ -860,6 +875,7 @@
     pl.semaphore_wait(barrier, count)
     for side in (0, 1):
         pl.when(sends[side])(lambda side=side: copy_far(side, to_slab[side]).start())
+    copy_rest.start()
 
     first, last = WIDE - me * depth, WIDE + (slabs - me) * depth - 1
     low_open, high_open = side_x.astype(F32), 1.0 - side_x.astype(F32)
@@ -908,6 +924,7 @@
     top = WIDE + depth
     coefs(WIDE, top)
     run(0, WIDE, top, True)
+    run(1, WIDE + 1, top - 1, True)
     for side in (0, 1):
         @pl.when(arrives[side])
         def _():
@@ -918,9 +935,7 @@
         def _():
             far[side] = jnp.zeros(far.shape[1:], F32)
 
-    copy_rest.start()
-    for k in (1, 2):
-        run(k, WIDE + k, top - k, True)
+    run(2, WIDE + 2, top - 2, True)
     for side in (0, 1):
         pl.when(arrives[side])(lambda side=side: share_far(side, taken).wait_recv())
     conductivity(far.at[0], WIDE - 1, 0, low_in)
@@ -1030,7 +1045,14 @@
             copy(n).wait_send()
         return carry
 
-    for body in (giving, keeping, passing, ending):
+    def in_turn(n, carry):
+        giving(n + 1, carry)
+        return keeping(n, carry)
+
+    giving(0, 0)
+    lax.fori_loop(0, quarter - 1, in_turn, 0)
+    keeping(quarter - 1, 0)
+    for body in (passing, ending):
         lax.fori_loop(0, quarter, body, 0)
     total.close()
 

time: 159 us -> 157 us (0.987)
  Pallas kernels: 149 us -> 146 us
    pallas_call x1, Pallas kernels: 6.33 us -> 3.7 us  [gather(): pl.pallas_call(functools.partial(gather_kernel, 16, depth, entries // 2),...]
where the time goes in v5:
time: 157 us; the launch traced here: 156 us
  Pallas kernels  146 us (93%)
  other arithmetic  6.52 us (4%)
  local copies, waits for them, and re-layouts  2.09 us (1%)
    pallas_call x1, Pallas kernels, first_solve(): pl.pallas_call(functools.partial(first_kernel, slabs), name='first_solve'...  64.7 us
    pallas_call x1, Pallas kernels, second_solve(): pl.pallas_call(functools.partial(second_kernel, slabs, nx), name='second_...  57.3 us
    pallas_call x1, Pallas kernels, share(): pl.pallas_call(functools.partial(share_kernel, slabs), name='share_data',...  12.9 us
    pallas_call x1, Pallas kernels, scatter(): pl.pallas_call(functools.partial(scatter_kernel, 8, depth, nx, lines), na...  7.82 us
    sort x1, other arithmetic, shards(): lax.sort((keys, rec_plan.reshape(-1)), num_keys=1, is_stable=False)  5.68 us
    pallas_call x1, Pallas kernels, gather(): pl.pallas_call(functools.partial(gather_kernel, 16, depth, entries // 2),...  3.7 us
  transfers between devices with their start and end apart: 1, of which 1 were waited for; matrix products, arithmetic and copies ran while one was open for 0% of the time, Pallas kernels for 5%

profile of v5, /device:TPU:1, one launch (start us, length us, event | category | flops | bytes accessed | tf_op | source)
XLA Modules:
  0.0 156.3 jit_solution(5286229226514750545)
XLA Ops:
  0.0 0.8 add_bitcast_fusion
  0.9 0.8 copy.7
  1.6 5.7 %sort.15 = (s32[8192]{0:T(1024)S(1)}, s32[8192]{0:T(1024)S(1)}) sort(s32[8192]{0:T(1024)S(1)} %bitcast.18, s32[8192]{0:T(1024)S(1)} %bitcast.19), dimensions={0}, to_apply=%region_0.0 | sort | flops 106496 | bytes 131072 | tf_op jit(solution)/shard_map/sort | solution.py:1106
  7.3 64.7 %first_solve.1 = (f32[8,256,256]{2,1,0:T(8,128)S(1)}, f32[8,128]{1,0:T(8,128)S(1)}, f32[8,136,256]{2,1,0:T(8,128)S(1)}, f32[2,136,256]{2,1,0:T(8,128)S(1)}, f32[...) custom-call(f32[8,256,256]{2,1,0:T(8,128)} %lc_in.1, f32[8,256,256]{2,1,0:T(8,128)} %pt_in.1, ...), custom_call_target="tpu_custom_call" | custom-call | tf_op jit(solution)/shard_map/first_solve/pallas_call | solution.py:591
  72.0 3.7 %gather.1.part = f32[32,128]{1,0:T(8,128)S(1)} custom-call(s32[64,128]{1,0:T(8,128)S(1)} %bitcast.14, s32[8192]{0:T(1024)S(1)} %get-tuple-element.22.keys, s32[8192]{0:T(1024)S(1)} %get-tuple-element.23.cells, f32[2048,256]{1,0:T(8,128)S(1)} %bitcast.13), custom_call_target="tpu_custom_call" | custom-call | tf_op jit(solution)/shard_map/gather/pallas_call | solution.py:697
  75.7 12.9 %share_data.1 = f32[2,32,128]{2,1,0:T(8,128)S(1)} custom-call(f32[32,128]{1,0:T(8,128)S(1)} %gather.1.part), custom_call_target="tpu_custom_call" | custom-call | tf_op jit(solution)/shard_map/share_data/pallas_call | solution.py:725
  88.6 0.1 collective-permute-start
  88.7 7.8 %scatter.1 = (f32[2560,256]{1,0:T(8,128)S(1)}, f32[2560,256]{1,0:T(8,128)S(1)}) custom-call(s32[64,128]{1,0:T(8,128)S(1)} %bitcast.15, s32[8192]{0:T(1024)S(1)} %get-tuple-element.22.keys, s32[8192]{0:T(1024)S(1)} %get-tuple-element.23.cells, f32[8192]{0:T(1024)S(1)} %bitcast.16), custom_call_target="tpu_custom_call" | custom-call | tf_op jit(solution)/shard_map/scatter/pallas_call | solution.py:787
  96.6 1.1 collective-permute-done.u_first
  97.7 57.3 %second_solve.1 = f32[8,256,256]{2,1,0:T(8,128)S(1)} custom-call(f32[8,136,256]{2,1,0:T(8,128)S(1)} %get-tuple-element.18.lc_half, f32[2,136,256]{2,1,0:T(8,128)S(1)} %get-tuple-element.19.lc_near, f32[10,136,256]{2,1,0:T(8,128)S(1)} %get-tuple-element.20.u_mine, f32[4,136,256]{2,1,0:T(8,128)S(1)} %collective-permute-done.u_first, ...), custom_call_target="tpu_custom_call" | custom-call | tf_op jit(solution)/shard_map/second_solve/pallas_call | solution.py:1070
  155.0 1.3 copy.9
  (2 shorter events, 0.0 us)
Async XLA Ops:
  88.6 9.0 %collective-permute-start = (f32[4,136,256]{2,1,0:T(8,128)S(1)}, f32[4,136,256]{2,1,0:T(8,128)S(1)}, u32[]{:S(2)}, u32[]{:S(2)}) collective-permute-start(f32[4,136,256]{2,1,0:T(8,128)S(1)} %get-tuple-element.25), channel_id=1, source_target_pairs={{0,64},{32,96},{64,0},{96,32},{1,65},{33,97},{65,1},{97,33},{2,66}... | collective-permute-start | bytes 1671176 | tf_op jit(solution)/shard_map/ppermute | solution.py:1112

commit v6 on v5

--- a/solution.py
+++ b/solution.py
@@ -269,9 +269,9 @@
 
 
 def first_kernel(
-    slabs, lc_in, pt_in, u, tan, mean_out, lc_half, lc_near, u_mine, u_first, u_rest,
+    slabs, lc_in, pt_in, u, u_low, u_high, tan, mean_out, lc_half, lc_near, u_mine, u_first, u_rest,
     lc, pt, lch, uh, sig, wgt, uw, dg, hx, hy, hz, v0, v1, v2, v3, pth, edge, order,
-    s_load, s_take, s_first, r_first, s_c, r_c, s_x, r_x, s_core, r_core, s_v, r_v, s_e, r_e, *sums,
+    s_load, s_take, s_c, r_c, s_x, r_x, s_core, r_core, s_v, r_v, s_e, r_e, *sums,
 ):
     src = lax.axis_index("src")
     me = lax.axis_index("slab")
@@ -303,6 +303,10 @@
     for load in loads:
         load.wait()
     lax.fori_loop(0, 2, lambda i, c: shuffle(i * (depth - 1), c), 0)
+    for side, ref in ((0, u_low), (1, u_high)):
+        for n in (0, 1):
+            rows = pl.ds(n * half, half)
+            uh[side, rows, :] = reorder(ref[0, rows, :], order[...])
     pl.semaphore_wait(barrier, count)
     mean_sum = Sum(src, me, slabs, sum_levels(sums[0:6]))
     mom_sum = Sum(src, me, slabs, sum_levels(sums[6:12]))
@@ -321,12 +325,6 @@
 
     def part(n):
         return pl.ds(n * half, half)
-
-    def copy_u(side, n, to):
-        return remote(
-            uw.at[1 + near(side), pl.ds(PAD + n * half, half)], uh.at[side, part(n)],
-            s_first.at[side, n], r_first.at[side, n], (src, to),
-        )
 
     my_rows = pl.ds(pl.multiple_of(half * side_x, PAD), half)
     their_rows = pl.ds(pl.multiple_of(half * (1 - side_x), PAD), half)
@@ -353,15 +351,6 @@
 
     for ref in (sig, wgt, uw, hy, v0, v1, v2, v3):
         zero_pads(ref, nx)
-    for side in (0, 1):
-        @pl.when(sends(side))
-        def _():
-            copy_c(lc, lch, side, me).wait_send()
-
-    for n in (0, 1):
-        for side in (0, 1):
-            pl.when(sends(side))(lambda side=side, n=n: copy_u(side, n, below(side)).start())
-
     def own(q, acc):
         for r, rows in chunks(nx):
             value = jnp.exp(lc[q, pl.ds(r, rows), :])
@@ -443,7 +432,6 @@
                 if n == 0:
                     pl.when(core == 0)(lambda: forward(pth, side).wait_recv())
                     pl.when(core == 1)(lambda: forward(lch, side).wait_recv())
-                copy_u(side, n, me).wait_recv()
                 for r, rows in chunks(half, n * half):
                     value = jnp.exp(lch[side, pl.ds(r, rows), :])
                     sig[plane, pl.ds(PAD + r, rows), :] = value
@@ -568,9 +556,9 @@
     for side in (0, 1):
         @pl.when(sends(side))
         def _():
+            copy_c(lc, lch, side, me).wait_send()
             copy_edge(side, me).wait_send()
             for n in (0, 1):
-                copy_u(side, n, me).wait_send()
                 for k in range(3):
                     copy_v(k, side, n, me).wait_send()
 
@@ -582,7 +570,7 @@
     mom_sum.close()
 
 
-def first_solve(slabs, lc, pt, u):
+def first_solve(slabs, lc, pt, u, u_low, u_high):
     depth, nx, cols = lc.shape
     plane = (nx + 2 * PAD, cols)
     half = nx // 2
@@ -599,7 +587,7 @@
                 for planes in (depth, 2, depth + 2, EARLY, depth + 2 - EARLY)
             ),
         ],
-        in_specs=[pl.BlockSpec(memory_space=pltpu.HBM)] * 3,
+        in_specs=[pl.BlockSpec(memory_space=pltpu.HBM)] * 3 + [full] * 2,
         out_specs=[full] * 7,
         scratch_shapes=[VMEM((depth, nx, cols), F32)] * 2
         + [VMEM((2, nx, cols), F32)] * 2
@@ -612,13 +600,13 @@
         ]
         + [VMEM((depth + 2, *plane), F32)] * 4
         + [VMEM((2, nx, cols), F32), VMEM((2, half, cols), F32), VMEM((cols, cols), jnp.bfloat16)]
-        + [DMA((3,)), DMA((5,)), DMA((2, 2)), DMA((2, 2)), *pair, *pair, *pair]
+        + [DMA((3,)), DMA((5,)), *pair, *pair, *pair]
         + [DMA((3, 2, 2)), DMA((3, 2, 2)), *pair]
         + sum_scratch(slabs, (1, 128)) * 2,
         compiler_params=pltpu.CompilerParams(
             collective_id=0, has_side_effects=True, vmem_limit_bytes=43 << 20
         ),
-    )(lc, pt, u)
+    )(lc, pt, u, u_low, u_high)
 
 
 def over_window(group, ordered, first_key, last_key, keys, cells, keys_s, cells_s, sems, body):
@@ -1104,8 +1092,13 @@
     order = order + lax.broadcasted_iota(jnp.int32, rec_depth.shape, 1)
     keys = (rec_depth * (2 * dipoles) + order).reshape(-1)
     keys, cells = lax.sort((keys, rec_plan.reshape(-1)), num_keys=1, is_stable=False)
+    up = [(i, i + 1) for i in range(slabs - 1)]
+    u_low = lax.ppermute(potentials[0, depth - 1 :], "slab", up)
+    u_high = lax.ppermute(potentials[0, :1], "slab", [(j, i) for i, j in up])
     arguments = (pltpu.with_memory_space_constraint(a, pltpu.HBM) for a in (log_cond, perturb, potentials[0]))
-    tangent, mean, lc_half, lc_near, u_mine, u_first, u_rest = first_solve(slabs, *arguments)
+    tangent, mean, lc_half, lc_near, u_mine, u_first, u_rest = first_solve(
+        slabs, *arguments, u_low, u_high
+    )
     part = gather(keys, cells, tangent.reshape(depth * nx, cols), depth)
     data = share(slabs, part)
     u_first, data = lax.optimization_barrier((u_first, data))

time: 157 us -> 167 us (1.064)
  starting transfers between devices: 0.09 us -> 8.06 us
  Pallas kernels: 146 us -> 149 us
    ppermute x0 -> x2, starting transfers between devices: none -> 5.97 us  [the longest x1 4.67 us: shards(): u_low = lax.ppermute(potentials[0, depth - 1:], 'slab', up)]
    pallas_call x1, Pallas kernels: 64.7 us -> 67.8 us  [first_solve(): pl.pallas_call(functools.partial(first_kernel, slabs), name='first_solve'...]
    ppermute x1, starting transfers between devices: 0.09 us -> 2.09 us  [shards(): u_first = lax.ppermute(u_first, 'src', [(i, (i + 2) % 4) for i in range(4)])]
    pallas_call x1, Pallas kernels: 12.9 us -> 10.9 us  [share(): pl.pallas_call(functools.partial(share_kernel, slabs), name='share_data',...]
  transfers between devices with their start and end apart: 1 -> 3, of which waited for: 1 -> 0; matrix products, arithmetic and copies ran while one was open for 0% -> 4% of each run, Pallas kernels for 5% -> 5%
where the time goes in v6:
time: 167 us; the launch traced here: 166 us
  Pallas kernels  149 us (89%)
  starting transfers between devices  8.06 us (5%)
  other arithmetic  6.52 us (4%)
  local copies, waits for them, and re-layouts  3.15 us (2%)
    pallas_call x1, Pallas kernels, first_solve(): pl.pallas_call(functools.partial(first_kernel, slabs), name='first_solve'...  67.8 us
    pallas_call x1, Pallas kernels, second_solve(): pl.pallas_call(functools.partial(second_kernel, slabs, nx), name='second_...  58 us
    pallas_call x1, Pallas kernels, share(): pl.pallas_call(functools.partial(share_kernel, slabs), name='share_data',...  10.9 us
    pallas_call x1, Pallas kernels, scatter(): pl.pallas_call(functools.partial(scatter_kernel, 8, depth, nx, lines), na...  7.92 us
    sort x1, other arithmetic, shards(): lax.sort((keys, rec_plan.reshape(-1)), num_keys=1, is_stable=False)  5.68 us
    ppermute x1, starting transfers between devices, shards(): u_low = lax.ppermute(potentials[0, depth - 1:], 'slab', up)  4.67 us
    pallas_call x1, Pallas kernels, gather(): pl.pallas_call(functools.partial(gather_kernel, 16, depth, entries // 2),...  3.88 us
  transfers between devices with their start and end apart: 3, of which 0 were waited for; matrix products, arithmetic and copies ran while one was open for 4% of the time, Pallas kernels for 5%

profile of v6, /device:TPU:1, one launch (start us, length us, event | category | flops | bytes accessed | tf_op | source)
XLA Modules:
  0.0 166.4 jit_solution(13931087795670974497)
XLA Ops:
  0.0 1.1 slice_bitcast_fusion
  1.1 1.3 collective-permute-start.1
  2.4 4.7 %collective-permute-start = (f32[1,256,256]{2,1,0:T(8,128)S(1)}, f32[1,256,256]{2,1,0:T(8,128)S(1)}, u32[]{:S(2)}, u32[]{:S(2)}) collective-permute-start(f32[1,256,256]{2,1,0:T(8,128)S(1)} %get-tuple-element.32), channel_id=1, source_target_pairs={{0,1},{1,2},{2,3},{3,4},{4,5},{5,6},{6,7},{7,8},{8,9},{9,10},{10,1... | collective-permute-start | bytes 786440 | tf_op jit(solution)/shard_map/ppermute | solution.py:1096
  7.1 0.8 add_bitcast_fusion
  7.9 0.8 copy.7
  8.7 5.7 %sort.15 = (s32[8192]{0:T(1024)S(1)}, s32[8192]{0:T(1024)S(1)}) sort(s32[8192]{0:T(1024)S(1)} %bitcast.22, s32[8192]{0:T(1024)S(1)} %bitcast.23), dimensions={0}, to_apply=%region_0.0 | sort | flops 106496 | bytes 131072 | tf_op jit(solution)/shard_map/sort | solution.py:1094
  14.4 0.0 collective-permute-done.1.u_high
  14.4 0.0 collective-permute-done.u_low
  14.4 67.8 %first_solve.1 = (f32[8,256,256]{2,1,0:T(8,128)S(1)}, f32[8,128]{1,0:T(8,128)S(1)}, f32[8,136,256]{2,1,0:T(8,128)S(1)}, f32[2,136,256]{2,1,0:T(8,128)S(1)}, f32[...) custom-call(f32[8,256,256]{2,1,0:T(8,128)} %lc_in.1, f32[8,256,256]{2,1,0:T(8,128)} %pt_in.1, ...), custom_call_target="tpu_custom_call" | custom-call | tf_op jit(solution)/shard_map/first_solve/pallas_call | solution.py:579
  82.2 3.9 %gather.1.part = f32[32,128]{1,0:T(8,128)S(1)} custom-call(s32[64,128]{1,0:T(8,128)S(1)} %bitcast.18, s32[8192]{0:T(1024)S(1)} %get-tuple-element.22.keys, s32[8192]{0:T(1024)S(1)} %get-tuple-element.23.cells, f32[2048,256]{1,0:T(8,128)S(1)} %bitcast.17), custom_call_target="tpu_custom_call" | custom-call | tf_op jit(solution)/shard_map/gather/pallas_call | solution.py:685
  86.1 10.9 %share_data.1 = f32[2,32,128]{2,1,0:T(8,128)S(1)} custom-call(f32[32,128]{1,0:T(8,128)S(1)} %gather.1.part), custom_call_target="tpu_custom_call" | custom-call | tf_op jit(solution)/shard_map/share_data/pallas_call | solution.py:713
  97.0 2.1 %collective-permute-start.2 = (f32[4,136,256]{2,1,0:T(8,128)S(1)}, f32[4,136,256]{2,1,0:T(8,128)S(1)}, u32[]{:S(2)}, u32[]{:S(2)}) collective-permute-start(f32[4,136,256]{2,1,0:T(8,128)S(1)} %get-tuple-element.25), channel_id=1, source_target_pairs={{0,64},{32,96},{64,0},{96,32},{1,65},{33,97},{65,1},{97,33},{2,66}... | collective-permute-start | bytes 1671176 | tf_op jit(solution)/shard_map/ppermute | solution.py:1105
  99.1 7.9 %scatter.1 = (f32[2560,256]{1,0:T(8,128)S(1)}, f32[2560,256]{1,0:T(8,128)S(1)}) custom-call(s32[64,128]{1,0:T(8,128)S(1)} %bitcast.19, s32[8192]{0:T(1024)S(1)} %get-tuple-element.22.keys, s32[8192]{0:T(1024)S(1)} %get-tuple-element.23.cells, f32[8192]{0:T(1024)S(1)} %bitcast.20), custom_call_target="tpu_custom_call" | custom-call | tf_op jit(solution)/shard_map/scatter/pallas_call | solution.py:775
  107.1 0.0 collective-permute-done.2.u_first
  107.1 58.0 %second_solve.1 = f32[8,256,256]{2,1,0:T(8,128)S(1)} custom-call(f32[8,136,256]{2,1,0:T(8,128)S(1)} %get-tuple-element.18.lc_half, f32[2,136,256]{2,1,0:T(8,128)S(1)} %get-tuple-element.19.lc_near, f32[10,136,256]{2,1,0:T(8,128)S(1)} %get-tuple-element.20.u_mine, f32[4,136,256]{2,1,0:T(8,128)S(1)} %collective-permute-done.2.u_first, ...), custom_call_target="tpu_custom_call" | custom-call | tf_op jit(solution)/shard_map/second_solve/pallas_call | solution.py:1058
  165.1 1.3 copy.9
  (2 shorter events, 0.0 us)
Async XLA Ops:
  1.1 13.3 %collective-permute-start.1 = (f32[1,256,256]{2,1,0:T(8,128)S(1)}, f32[1,256,256]{2,1,0:T(8,128)S(1)}, u32[]{:S(2)}, u32[]{:S(2)}) collective-permute-start(f32[1,256,256]{2,1,0:T(8,128)S(1)} %get-tuple-element.31), channel_id=1, source_target_pairs={{1,0},{2,1},{3,2},{4,3},{5,4},{6,5},{7,6},{8,7},{9,8},{10,9},{11,1... | collective-permute-start | bytes 786440 | tf_op jit(solution)/shard_map/ppermute | solution.py:1097
  2.4 12.0 %collective-permute-start = (f32[1,256,256]{2,1,0:T(8,128)S(1)}, f32[1,256,256]{2,1,0:T(8,128)S(1)}, u32[]{:S(2)}, u32[]{:S(2)}) collective-permute-start(f32[1,256,256]{2,1,0:T(8,128)S(1)} %get-tuple-element.32), channel_id=1, source_target_pairs={{0,1},{1,2},{2,3},{3,4},{4,5},{5,6},{6,7},{7,8},{8,9},{9,10},{10,1... | collective-permute-start | bytes 786440 | tf_op jit(solution)/shard_map/ppermute | solution.py:1096
  97.0 10.0 %collective-permute-start.2 = (f32[4,136,256]{2,1,0:T(8,128)S(1)}, f32[4,136,256]{2,1,0:T(8,128)S(1)}, u32[]{:S(2)}, u32[]{:S(2)}) collective-permute-start(f32[4,136,256]{2,1,0:T(8,128)S(1)} %get-tuple-element.25), channel_id=1, source_target_pairs={{0,64},{32,96},{64,0},{96,32},{1,65},{33,97},{65,1},{97,33},{2,66}... | collective-permute-start | bytes 1671176 | tf_op jit(solution)/shard_map/ppermute | solution.py:1105

commit v7 on v5

--- a/solution.py
+++ b/solution.py
@@ -350,18 +350,12 @@
         @pl.when(sends(side))
         def _():
             by_core(lambda ref, dst: copy_c(ref, dst, side, below(side)).start())
-
-    for ref in (sig, wgt, uw, hy, v0, v1, v2, v3):
-        zero_pads(ref, nx)
-    for side in (0, 1):
-        @pl.when(sends(side))
-        def _():
-            copy_c(lc, lch, side, me).wait_send()
-
     for n in (0, 1):
         for side in (0, 1):
             pl.when(sends(side))(lambda side=side, n=n: copy_u(side, n, below(side)).start())
 
+    for ref in (sig, wgt, uw, hy, v0, v1, v2, v3):
+        zero_pads(ref, nx)
     def own(q, acc):
         for r, rows in chunks(nx):
             value = jnp.exp(lc[q, pl.ds(r, rows), :])
@@ -568,6 +562,7 @@
     for side in (0, 1):
         @pl.when(sends(side))
         def _():
+            copy_c(lc, lch, side, me).wait_send()
             copy_edge(side, me).wait_send()
             for n in (0, 1):
                 copy_u(side, n, me).wait_send()

time: 157 us -> 157 us (level)
  no operation moved by 1% of the time
where the time goes in v7:
time: 157 us
  Pallas kernels  147 us (94%)
  other arithmetic  6.52 us (4%)
  local copies, waits for them, and re-layouts  2.09 us (1%)
    pallas_call x1, Pallas kernels, first_solve(): pl.pallas_call(functools.partial(first_kernel, slabs), name='first_solve'...  65.6 us
    pallas_call x1, Pallas kernels, second_solve(): pl.pallas_call(functools.partial(second_kernel, slabs, nx), name='second_...  57.5 us
    pallas_call x1, Pallas kernels, share(): pl.pallas_call(functools.partial(share_kernel, slabs), name='share_data',...  12.2 us
    pallas_call x1, Pallas kernels, scatter(): pl.pallas_call(functools.partial(scatter_kernel, 8, depth, nx, lines), na...  8.04 us
    sort x1, other arithmetic, shards(): lax.sort((keys, rec_plan.reshape(-1)), num_keys=1, is_stable=False)  5.68 us
    pallas_call x1, Pallas kernels, gather(): pl.pallas_call(functools.partial(gather_kernel, 16, depth, entries // 2),...  3.87 us
  transfers between devices with their start and end apart: 1, of which 1 were waited for; matrix products, arithmetic and copies ran while one was open for 0% of the time, Pallas kernels for 5%

profile of v7, /device:TPU:1, one launch (start us, length us, event | category | flops | bytes accessed | tf_op | source)
XLA Modules:
  0.0 156.5 jit_solution(5018115959395893562)
XLA Ops:
  0.0 0.8 add_bitcast_fusion
  0.9 0.8 copy.7
  1.6 5.7 %sort.15 = (s32[8192]{0:T(1024)S(1)}, s32[8192]{0:T(1024)S(1)}) sort(s32[8192]{0:T(1024)S(1)} %bitcast.18, s32[8192]{0:T(1024)S(1)} %bitcast.19), dimensions={0}, to_apply=%region_0.0 | sort | flops 106496 | bytes 131072 | tf_op jit(solution)/shard_map/sort | solution.py:1101
  7.3 65.6 %first_solve.1 = (f32[8,256,256]{2,1,0:T(8,128)S(1)}, f32[8,128]{1,0:T(8,128)S(1)}, f32[8,136,256]{2,1,0:T(8,128)S(1)}, f32[2,136,256]{2,1,0:T(8,128)S(1)}, f32[...) custom-call(f32[8,256,256]{2,1,0:T(8,128)} %lc_in.1, f32[8,256,256]{2,1,0:T(8,128)} %pt_in.1, ...), custom_call_target="tpu_custom_call" | custom-call | tf_op jit(solution)/shard_map/first_solve/pallas_call | solution.py:586
  72.9 3.9 %gather.1.part = f32[32,128]{1,0:T(8,128)S(1)} custom-call(s32[64,128]{1,0:T(8,128)S(1)} %bitcast.14, s32[8192]{0:T(1024)S(1)} %get-tuple-element.22.keys, s32[8192]{0:T(1024)S(1)} %get-tuple-element.23.cells, f32[2048,256]{1,0:T(8,128)S(1)} %bitcast.13), custom_call_target="tpu_custom_call" | custom-call | tf_op jit(solution)/shard_map/gather/pallas_call | solution.py:692
  76.8 12.2 %share_data.1 = f32[2,32,128]{2,1,0:T(8,128)S(1)} custom-call(f32[32,128]{1,0:T(8,128)S(1)} %gather.1.part), custom_call_target="tpu_custom_call" | custom-call | tf_op jit(solution)/shard_map/share_data/pallas_call | solution.py:720
  89.0 0.1 collective-permute-start
  89.1 8.0 %scatter.1 = (f32[2560,256]{1,0:T(8,128)S(1)}, f32[2560,256]{1,0:T(8,128)S(1)}) custom-call(s32[64,128]{1,0:T(8,128)S(1)} %bitcast.15, s32[8192]{0:T(1024)S(1)} %get-tuple-element.22.keys, s32[8192]{0:T(1024)S(1)} %get-tuple-element.23.cells, f32[8192]{0:T(1024)S(1)} %bitcast.16), custom_call_target="tpu_custom_call" | custom-call | tf_op jit(solution)/shard_map/scatter/pallas_call | solution.py:782
  97.1 0.5 collective-permute-done.u_first
  97.6 57.5 %second_solve.1 = f32[8,256,256]{2,1,0:T(8,128)S(1)} custom-call(f32[8,136,256]{2,1,0:T(8,128)S(1)} %get-tuple-element.18.lc_half, f32[2,136,256]{2,1,0:T(8,128)S(1)} %get-tuple-element.19.lc_near, f32[10,136,256]{2,1,0:T(8,128)S(1)} %get-tuple-element.20.u_mine, f32[4,136,256]{2,1,0:T(8,128)S(1)} %collective-permute-done.u_first, ...), custom_call_target="tpu_custom_call" | custom-call | tf_op jit(solution)/shard_map/second_solve/pallas_call | solution.py:1065
  155.2 1.3 copy.9
  (2 shorter events, 0.0 us)
Async XLA Ops:
  89.0 8.6 %collective-permute-start = (f32[4,136,256]{2,1,0:T(8,128)S(1)}, f32[4,136,256]{2,1,0:T(8,128)S(1)}, u32[]{:S(2)}, u32[]{:S(2)}) collective-permute-start(f32[4,136,256]{2,1,0:T(8,128)S(1)} %get-tuple-element.25), channel_id=1, source_target_pairs={{0,64},{32,96},{64,0},{96,32},{1,65},{33,97},{65,1},{97,33},{2,66}... | collective-permute-start | bytes 1671176 | tf_op jit(solution)/shard_map/ppermute | solution.py:1107

commit v8 on v5

--- a/solution.py
+++ b/solution.py
@@ -735,11 +735,10 @@
     )(part)
 
 
-def scatter_kernel(group, depth, nx, lines, ordered, keys, cells, data, out0, out1, keys_s, cells_s, sems):
+def scatter_kernel(group, depth, nx, lines, ordered, keys, cells, data, out, keys_s, cells_s, sems):
     me = lax.axis_index("slab")
     side_x = lax.axis_index("src") // 2
-    outs = (out0, out1)
-    total, cols = out0.shape
+    total, cols = out.shape[0], out.shape[1] // 2
     planes = total // lines
     entries = keys.shape[0]
     dipoles = entries // 2
@@ -749,8 +748,7 @@
     plane_base = low * lines + row_base
 
     def clear(q, carry):
-        for out in outs:
-            out[pl.ds(pl.multiple_of(q * lines, 8), lines), :] = jnp.zeros((lines, cols), F32)
+        out[pl.ds(pl.multiple_of(q * lines, 8), lines), :] = jnp.zeros((lines, 2 * cols), F32)
         return carry
 
     lax.fori_loop(0, planes, clear, 0)
@@ -767,11 +765,11 @@
             inside = jnp.logical_and(inside, jnp.logical_and(row >= row_base + PAD, row < row_base + lines - PAD))
             hit = lane == jnp.where(inside, lane_of(cell & (cols - 1), cols), -1)
             at = jnp.where(inside, (key >> bits(entries)) * lines + row - plane_base, 0)
-            sign = jnp.where(o < dipoles, 1.0, -1.0)
-            parts.append((at, [jnp.where(hit, data[k + n * dipoles] * sign, 0.0) for n in (0, 1)]))
-        for at, values in parts:
-            for out, value in zip(outs, values):
-                out[pl.ds(at, 1), :] = out[pl.ds(at, 1), :] + value
+            signed = jnp.where(hit, jnp.where(o < dipoles, 1.0, -1.0), 0.0)
+            values = [signed * data[k + n * dipoles] for n in (0, 1)]
+            parts.append((at, jnp.concatenate(values, axis=1)))
+        for at, value in parts:
+            out[pl.ds(at, 1), :] = out[pl.ds(at, 1), :] + value
 
     over_window(
         group, ordered, low * entries, (low + planes) * entries, keys, cells, keys_s, cells_s, sems, body
@@ -787,17 +785,17 @@
     back = pl.pallas_call(
         functools.partial(scatter_kernel, 8, depth, nx, lines),
         name="scatter",
-        out_shape=[jax.ShapeDtypeStruct((planes * lines, cols), F32)] * 2,
+        out_shape=jax.ShapeDtypeStruct((planes * lines, 2 * cols), F32),
         in_specs=[full, anywhere, anywhere, smem],
-        out_specs=[full, full],
+        out_specs=full,
         scratch_shapes=window_scratch(keys.shape[0]),
         compiler_params=pltpu.CompilerParams(vmem_limit_bytes=8 << 20),
     )(keys.reshape(-1, 128), keys, cells, data.reshape(-1))
-    return [ref.reshape(planes, lines, cols) for ref in back]
+    return back.reshape(planes, lines, 2 * cols)
 
 
 def second_kernel(
-    slabs, nx, lc_half, lc_near, u_mine, u_first, u_rest, mean_in, v00, v01, out,
+    slabs, nx, lc_half, lc_near, u_mine, u_first, u_rest, mean_in, v0, out,
     sig, dg, hx, hy, hz, v1, v2, v3, u2, adj, give, take, pair, far, order,
     s_load, s_u, r_u, s_far, r_far, s_c2, r_c2, s_give, r_give, s_x, r_x, s_own, r_own, s_fwd, r_fwd,
     *sums,
@@ -894,7 +892,7 @@
     scale = 6.0 * mean
     inv = 1.0 / scale
     zero = jnp.zeros((8, cols), F32)
-    fields = [(v0, v1.at[j], v2.at[j], v3.at[j]) for j, v0 in enumerate((v00, v01))]
+    fields = [(v0.at[:, :, pl.ds(j * cols, cols)], v1.at[j], v2.at[j], v3.at[j]) for j in (0, 1)]
     sums_of = {}
 
     def run(k, start, stop, dotted):
@@ -973,7 +971,8 @@
                 adj[j, q, pl.ds(r, rows), :] = value
         return carry
 
-    lax.fori_loop(0, depth + 2, combine, 0)
+    give_first, keep_first = (1 - core) * quarter, core * quarter
+    lax.fori_loop(give_first, give_first + 3, combine, 0)
     for load in loads:
         load.wait()
     copy_rest.wait()
@@ -1046,10 +1045,13 @@
         return carry
 
     def in_turn(n, carry):
+        combine(give_first + n + 3, carry)
         giving(n + 1, carry)
-        return keeping(n, carry)
+        keeping(n, carry)
+        return combine(keep_first + n + 3, carry)
 
     giving(0, 0)
+    lax.fori_loop(keep_first, keep_first + 3, combine, 0)
     lax.fori_loop(0, quarter - 1, in_turn, 0)
     keeping(quarter - 1, 0)
     for body in (passing, ending):
@@ -1071,7 +1073,7 @@
         functools.partial(second_kernel, slabs, nx),
         name="second_solve",
         out_shape=jax.ShapeDtypeStruct((depth, nx, cols), F32),
-        in_specs=[full, full, anywhere, anywhere, anywhere, full, full, full],
+        in_specs=[full, full, anywhere, anywhere, anywhere, full, full],
         out_specs=full,
         scratch_shapes=[
             VMEM((wide + 2, *plane), F32),
@@ -1094,7 +1096,7 @@
         compiler_params=pltpu.CompilerParams(
             collective_id=2, has_side_effects=True, vmem_limit_bytes=42 << 20
         ),
-    )(lc_half, lc_near, u_mine, u_first, u_rest, mean, *back)
+    )(lc_half, lc_near, u_mine, u_first, u_rest, mean, back)
 
 
 def shards(slabs, log_cond, perturb, potentials, rec_depth, rec_plan):

time: 157 us -> 155 us (0.987)
    pallas_call x1, Pallas kernels: 57.3 us -> 55.7 us  [second_solve(): pl.pallas_call(functools.partial(second_kernel, slabs, nx), name='second_...]
where the time goes in v8:
time: 155 us
  Pallas kernels  145 us (94%)
  other arithmetic  6.52 us (4%)
  local copies, waits for them, and re-layouts  2.09 us (1%)
  waiting for transfers between devices  1.78 us (1%)
    pallas_call x1, Pallas kernels, first_solve(): pl.pallas_call(functools.partial(first_kernel, slabs), name='first_solve'...  64.7 us
    pallas_call x1, Pallas kernels, second_solve(): pl.pallas_call(functools.partial(second_kernel, slabs, nx), name='second_...  55.7 us
    pallas_call x1, Pallas kernels, share(): pl.pallas_call(functools.partial(share_kernel, slabs), name='share_data',...  13.2 us
    pallas_call x1, Pallas kernels, scatter(): pl.pallas_call(functools.partial(scatter_kernel, 8, depth, nx, lines), na...  7.25 us
    sort x1, other arithmetic, shards(): lax.sort((keys, rec_plan.reshape(-1)), num_keys=1, is_stable=False)  5.68 us
    pallas_call x1, Pallas kernels, gather(): pl.pallas_call(functools.partial(gather_kernel, 16, depth, entries // 2),...  3.69 us
  transfers between devices with their start and end apart: 1, of which 1 were waited for; matrix products, arithmetic and copies ran while one was open for 0% of the time, Pallas kernels for 5%

profile of v8, /device:TPU:1, one launch (start us, length us, event | category | flops | bytes accessed | tf_op | source)
XLA Modules:
  0.0 155.1 jit_solution(6002716686857205497)
XLA Ops:
  0.0 0.8 add_bitcast_fusion
  0.9 0.8 copy.7
  1.6 5.7 %sort.15 = (s32[8192]{0:T(1024)S(1)}, s32[8192]{0:T(1024)S(1)}) sort(s32[8192]{0:T(1024)S(1)} %bitcast.16, s32[8192]{0:T(1024)S(1)} %bitcast.17), dimensions={0}, to_apply=%region_0.0 | sort | flops 106496 | bytes 131072 | tf_op jit(solution)/shard_map/sort | solution.py:1108
  7.3 64.7 %first_solve.1 = (f32[8,256,256]{2,1,0:T(8,128)S(1)}, f32[8,128]{1,0:T(8,128)S(1)}, f32[8,136,256]{2,1,0:T(8,128)S(1)}, f32[2,136,256]{2,1,0:T(8,128)S(1)}, f32[...) custom-call(f32[8,256,256]{2,1,0:T(8,128)} %lc_in.1, f32[8,256,256]{2,1,0:T(8,128)} %pt_in.1, ...), custom_call_target="tpu_custom_call" | custom-call | tf_op jit(solution)/shard_map/first_solve/pallas_call | solution.py:591
  72.0 3.7 %gather.1.part = f32[32,128]{1,0:T(8,128)S(1)} custom-call(s32[64,128]{1,0:T(8,128)S(1)} %bitcast.12, s32[8192]{0:T(1024)S(1)} %get-tuple-element.20.keys, s32[8192]{0:T(1024)S(1)} %get-tuple-element.21.cells, f32[2048,256]{1,0:T(8,128)S(1)} %bitcast.11), custom_call_target="tpu_custom_call" | custom-call | tf_op jit(solution)/shard_map/gather/pallas_call | solution.py:697
  75.7 13.2 %share_data.1 = f32[2,32,128]{2,1,0:T(8,128)S(1)} custom-call(f32[32,128]{1,0:T(8,128)S(1)} %gather.1.part), custom_call_target="tpu_custom_call" | custom-call | tf_op jit(solution)/shard_map/share_data/pallas_call | solution.py:725
  88.9 0.1 collective-permute-start
  89.0 7.3 %scatter.1 = f32[2560,512]{1,0:T(8,128)S(1)} custom-call(s32[64,128]{1,0:T(8,128)S(1)} %bitcast.13, s32[8192]{0:T(1024)S(1)} %get-tuple-element.20.keys, s32[8192]{0:T(1024)S(1)} %get-tuple-element.21.cells, f32[8192]{0:T(1024)S(1)} %bitcast.14), custom_call_target="tpu_custom_call" | custom-call | tf_op jit(solution)/shard_map/scatter/pallas_call | solution.py:785
  96.3 1.8 %collective-permute-done.u_first = f32[4,136,256]{2,1,0:T(8,128)S(1)} collective-permute-done((f32[4,136,256]{2,1,0:T(8,128)S(1)}, f32[4,136,256]{2,1,0:T(8,128)S(1)}, u32[]{:S(2)}, u32[]{:S(2)}) %collective-permute-start) | collective-permute-done | bytes 557088 | tf_op jit(solution)/shard_map/ppermute | solution.py:1114
  98.1 55.7 %second_solve.1 = f32[8,256,256]{2,1,0:T(8,128)S(1)} custom-call(f32[8,136,256]{2,1,0:T(8,128)S(1)} %get-tuple-element.16.lc_half, f32[2,136,256]{2,1,0:T(8,128)S(1)} %get-tuple-element.17.lc_near, f32[10,136,256]{2,1,0:T(8,128)S(1)} %get-tuple-element.18.u_mine, f32[4,136,256]{2,1,0:T(8,128)S(1)} %collective-permute-done.u_first, ...), custom_call_target="tpu_custom_call" | custom-call | tf_op jit(solution)/shard_map/second_solve/pallas_call | solution.py:1072
  153.8 1.3 copy.9
  (2 shorter events, 0.0 us)
Async XLA Ops:
  88.9 9.1 %collective-permute-start = (f32[4,136,256]{2,1,0:T(8,128)S(1)}, f32[4,136,256]{2,1,0:T(8,128)S(1)}, u32[]{:S(2)}, u32[]{:S(2)}) collective-permute-start(f32[4,136,256]{2,1,0:T(8,128)S(1)} %get-tuple-element.23), channel_id=1, source_target_pairs={{0,64},{32,96},{64,0},{96,32},{1,65},{33,97},{65,1},{97,33},{2,66}... | collective-permute-start | bytes 1671176 | tf_op jit(solution)/shard_map/ppermute | solution.py:1114

commit v9 on v8

--- a/solution.py
+++ b/solution.py
@@ -14,7 +14,7 @@
 DMA = pltpu.SemaphoreType.DMA
 PAD = 8
 WIDE = 4
-EARLY = 4
+EARLY = 3
 ROWS = 64
 THETA = (6.0, 2.0, 10.0)
 

time: 155 us -> 156 us (level)
  Pallas kernels: 145 us -> 147 us
  waiting for transfers between devices: 1.78 us -> 0.01 us
    pallas_call x1, Pallas kernels: 55.7 us -> 58.6 us  [second_solve(): pl.pallas_call(functools.partial(second_kernel, slabs, nx), name='second_...]
    ppermute x1, waiting for transfers between devices: 1.78 us -> 0.01 us  [shards(): u_first = lax.ppermute(u_first, 'src', [(i, (i + 2) % 4) for i in range(4)])]
  transfers between devices with their start and end apart: 1 -> 1, of which waited for: 1 -> 0; matrix products, arithmetic and copies ran while one was open for 0% -> 0% of each run, Pallas kernels for 5% -> 5%
where the time goes in v9:
time: 156 us
  Pallas kernels  147 us (94%)
  other arithmetic  6.52 us (4%)
  local copies, waits for them, and re-layouts  2.09 us (1%)
    pallas_call x1, Pallas kernels, first_solve(): pl.pallas_call(functools.partial(first_kernel, slabs), name='first_solve'...  64.7 us
    pallas_call x1, Pallas kernels, second_solve(): pl.pallas_call(functools.partial(second_kernel, slabs, nx), name='second_...  58.6 us
    pallas_call x1, Pallas kernels, share(): pl.pallas_call(functools.partial(share_kernel, slabs), name='share_data',...  13 us
    pallas_call x1, Pallas kernels, scatter(): pl.pallas_call(functools.partial(scatter_kernel, 8, depth, nx, lines), na...  7.15 us
    sort x1, other arithmetic, shards(): lax.sort((keys, rec_plan.reshape(-1)), num_keys=1, is_stable=False)  5.68 us
    pallas_call x1, Pallas kernels, gather(): pl.pallas_call(functools.partial(gather_kernel, 16, depth, entries // 2),...  3.7 us
  transfers between devices with their start and end apart: 1, of which 0 were waited for; matrix products, arithmetic and copies ran while one was open for 0% of the time, Pallas kernels for 5%

profile of v9, /device:TPU:1, one launch (start us, length us, event | category | flops | bytes accessed | tf_op | source)
XLA Modules:
  0.0 155.9 jit_solution(11941934752810621097)
XLA Ops:
  0.0 0.8 add_bitcast_fusion
  0.9 0.8 copy.7
  1.6 5.7 %sort.15 = (s32[8192]{0:T(1024)S(1)}, s32[8192]{0:T(1024)S(1)}) sort(s32[8192]{0:T(1024)S(1)} %bitcast.16, s32[8192]{0:T(1024)S(1)} %bitcast.17), dimensions={0}, to_apply=%region_0.0 | sort | flops 106496 | bytes 131072 | tf_op jit(solution)/shard_map/sort | solution.py:1108
  7.3 64.7 %first_solve.1 = (f32[8,256,256]{2,1,0:T(8,128)S(1)}, f32[8,128]{1,0:T(8,128)S(1)}, f32[8,136,256]{2,1,0:T(8,128)S(1)}, f32[2,136,256]{2,1,0:T(8,128)S(1)}, f32[...) custom-call(f32[8,256,256]{2,1,0:T(8,128)} %lc_in.1, f32[8,256,256]{2,1,0:T(8,128)} %pt_in.1, ...), custom_call_target="tpu_custom_call" | custom-call | tf_op jit(solution)/shard_map/first_solve/pallas_call | solution.py:591
  72.0 3.7 %gather.1.part = f32[32,128]{1,0:T(8,128)S(1)} custom-call(s32[64,128]{1,0:T(8,128)S(1)} %bitcast.12, s32[8192]{0:T(1024)S(1)} %get-tuple-element.20.keys, s32[8192]{0:T(1024)S(1)} %get-tuple-element.21.cells, f32[2048,256]{1,0:T(8,128)S(1)} %bitcast.11), custom_call_target="tpu_custom_call" | custom-call | tf_op jit(solution)/shard_map/gather/pallas_call | solution.py:697
  75.7 13.0 %share_data.1 = f32[2,32,128]{2,1,0:T(8,128)S(1)} custom-call(f32[32,128]{1,0:T(8,128)S(1)} %gather.1.part), custom_call_target="tpu_custom_call" | custom-call | tf_op jit(solution)/shard_map/share_data/pallas_call | solution.py:725
  88.7 0.1 collective-permute-start
  88.8 7.2 %scatter.1 = f32[2560,512]{1,0:T(8,128)S(1)} custom-call(s32[64,128]{1,0:T(8,128)S(1)} %bitcast.13, s32[8192]{0:T(1024)S(1)} %get-tuple-element.20.keys, s32[8192]{0:T(1024)S(1)} %get-tuple-element.21.cells, f32[8192]{0:T(1024)S(1)} %bitcast.14), custom_call_target="tpu_custom_call" | custom-call | tf_op jit(solution)/shard_map/scatter/pallas_call | solution.py:785
  96.0 0.0 collective-permute-done.u_first
  96.0 58.6 %second_solve.1 = f32[8,256,256]{2,1,0:T(8,128)S(1)} custom-call(f32[8,136,256]{2,1,0:T(8,128)S(1)} %get-tuple-element.16.lc_half, f32[2,136,256]{2,1,0:T(8,128)S(1)} %get-tuple-element.17.lc_near, f32[10,136,256]{2,1,0:T(8,128)S(1)} %get-tuple-element.18.u_mine, f32[3,136,256]{2,1,0:T(8,128)S(1)} %collective-permute-done.u_first, ...), custom_call_target="tpu_custom_call" | custom-call | tf_op jit(solution)/shard_map/second_solve/pallas_call | solution.py:1072
  154.5 1.3 copy.9
  (2 shorter events, 0.0 us)
Async XLA Ops:
  88.7 7.3 %collective-permute-start = (f32[3,136,256]{2,1,0:T(8,128)S(1)}, f32[3,136,256]{2,1,0:T(8,128)S(1)}, u32[]{:S(2)}, u32[]{:S(2)}) collective-permute-start(f32[3,136,256]{2,1,0:T(8,128)S(1)} %get-tuple-element.23), channel_id=1, source_target_pairs={{0,64},{32,96},{64,0},{96,32},{1,65},{33,97},{65,1},{97,33},{2,66}... | collective-permute-start | bytes 1253384 | tf_op jit(solution)/shard_map/ppermute | solution.py:1114
